TPU v7x, 128 devices: a whole 4x4x4 slice. The times are simulated.
128 devices in a mesh: replica: 8 (over x, core), shard: 16 (over z, y).
Axes of the slice: x: 4, y: 4, z: 4, core: 2. Of those that a mesh axis runs over, the one named last changes fastest.
Arguments:
- tokens: bfloat16 [16384, 768], P(('replica', 'shard')), may hold values from -6 to 6
- cotangent: bfloat16 [16384, 768], P(('replica', 'shard')), may hold values from -6 to 6
- lengths: int32 [8, 3], P('replica'), may hold values from 1 to 1536, 2048 in all within a row
- positions: int32 [8, 2048], P('replica'), may hold values from 0 to 2047, each once within a row
- w_rows: float32 [768, 6144], P('shard'), may hold values from -0.8660254 to 0.8660254
- w_down: float32 [3072, 768], P('shard'), may hold values from -0.109375 to 0.109375
- vectors: float32 [12, 768], P(None, 'shard'), may hold values from -1.8 to 1.8
- moment_rows: float32 [768, 6144], P('shard'), may hold values from -40 to 40
- second_rows: float32 [768, 6144], P('shard'), may hold values from 212.992 to 868.352
- moment_down: float32 [3072, 768], P('shard'), may hold values from -40 to 40
- second_down: float32 [3072, 768], P('shard'), may hold values from 212.992 to 868.352
- moment_vectors: float32 [12, 768], P(None, 'shard'), may hold values from -40 to 40
- second_vectors: float32 [12, 768], P(None, 'shard'), may hold values from 212.992 to 868.352
Outputs:
- outputs: bfloat16 [16384, 768], P(('replica', 'shard'))
- grad_input: bfloat16 [16384, 768], P(('replica', 'shard'))
- new_rows: float32 [768, 6144], P('shard')
- new_moment_rows: float32 [768, 6144], P('shard')
- new_second_rows: float32 [768, 6144], P('shard')
- new_down: float32 [3072, 768], P('shard')
- new_moment_down: float32 [3072, 768], P('shard')
- new_second_down: float32 [3072, 768], P('shard')
- new_vectors: float32 [12, 768], P(None, 'shard')
- new_moment_vectors: float32 [12, 768], P(None, 'shard')
- new_second_vectors: float32 [12, 768], P(None, 'shard')
Inputs may be any that keep to these rules, and one draw needn't show every extreme that they name: Each row of lengths sums to 2048; its largest entry is three quarters of 2048. Each row of positions is a permutation of 0 to 2047.
All inputs are finite; a program needn't handle non-finite values.
Results may differ from a plain program's by a relative error of at most 0.012.
The roundings to bfloat16 on the way count: a program that leaves them out, or rounds other values in their place, can miss the bound.
Values may be sent and summed in bfloat16 or wider, within the bound.
A program may use at most 192 MiB of HBM per device.

v0:
```python
import jax
import jax.numpy as jnp
from jax import lax
from jax.sharding import PartitionSpec as P

H = 12
HD = 64
STEP = 10


EPS_NORM = 1e-05
BETA_ONE = 0.9
BETA_TWO = 0.95
EPS_ADAM = 1e-08
LR_MATRIX = 0.02
LR_VECTOR = 0.3
DECAY = 0.1
HUGE_NEG = -1e30


def sent_together(arrays, axis, dim, along):
    both = jnp.concatenate(arrays, axis=along)
    whole, at, done = (lax.all_gather(both, axis, axis=dim, tiled=True), 0, [])
    for a in arrays:
        done.append(lax.slice_in_dim(whole, at, at + a.shape[along], axis=along))
        at += a.shape[along]
    return tuple(done)


def packed_total(arrays, axis):
    ravelled, at, done = (jnp.concatenate([a.reshape(-1) for a in arrays]), 0, [])
    total = lax.psum(ravelled, axis)
    for a in arrays:
        done.append(total[at : at + a.size].reshape(a.shape))
        at += a.size
    return tuple(done)


def layer_norm(inputs, gain, shift):
    average = jnp.mean(inputs, -1, keepdims=True)
    centred = inputs - average
    spread = jnp.mean(centred * centred, -1, keepdims=True)
    return centred * lax.rsqrt(spread + EPS_NORM) * gain + shift


def gelu_tanh(inputs):
    return jax.nn.gelu(inputs, approximate=True)


def adamw(weight, moment, second, grad, rate, decay):
    moment_new = BETA_ONE * moment + (1.0 - BETA_ONE) * grad
    second_new = BETA_TWO * second + (1.0 - BETA_TWO) * grad * grad
    moment_hat = moment_new / (1.0 - BETA_ONE**STEP)
    second_hat = second_new / (1.0 - BETA_TWO**STEP)
    weight_new = weight - rate * (moment_hat / (jnp.sqrt(second_hat) + EPS_ADAM) + decay * weight)
    return (weight_new, moment_new, second_new)


def to_heads(matrix):
    return matrix.reshape(matrix.shape[0], H, HD).transpose(1, 0, 2)


def from_heads(stacked):
    return stacked.transpose(1, 0, 2).reshape(stacked.shape[1], H * HD)


def per_device(
    tokens,
    cotangent,
    lengths,
    positions,
    w_rows,
    w_down,
    vectors,
    moment_rows,
    second_rows,
    moment_down,
    second_down,
    moment_vectors,
    second_vectors,
):
    tok_rows, model_dim = tokens.shape
    scale = HD ** (-0.5)
    shard_index = lax.axis_index("shard")
    low_weights = (
        w_rows.astype(jnp.bfloat16),
        w_down.astype(jnp.bfloat16),
        vectors.astype(jnp.bfloat16),
    )
    full_rows, full_down, full_vecs = (
        lax.all_gather(low_weights[0], "shard", axis=0, tiled=True),
        lax.all_gather(low_weights[1], "shard", axis=0, tiled=True),
        lax.all_gather(low_weights[2], "shard", axis=1, tiled=True),
    )
    vec_vals = full_vecs.astype(jnp.float32)
    gain_one, shift_one, bias_query, bias_value = (
        vec_vals[0],
        vec_vals[1],
        vec_vals[2],
        vec_vals[3],
    )
    bias_out, gain_two, shift_two, bias_down = (vec_vals[4], vec_vals[5], vec_vals[6], vec_vals[7])
    bias_first = vec_vals[8:].reshape(-1)
    place_all = positions[0]
    place_own = lax.dynamic_slice_in_dim(place_all, shard_index * tok_rows, tok_rows)
    seq_ends = jnp.cumsum(lengths[0])
    seg_all = jnp.sum((place_all[:, None] >= seq_ends[None, :]).astype(jnp.int32), axis=1)
    seg_own = jnp.sum((place_own[:, None] >= seq_ends[None, :]).astype(jnp.int32), axis=1)
    allowed = (seg_own[:, None] == seg_all[None, :]) & (place_all[None, :] <= place_own[:, None])
    inputs = tokens.astype(jnp.float32)
    normed = layer_norm(inputs, gain_one, shift_one).astype(jnp.bfloat16)
    projected = jnp.dot(normed, full_rows[:, : 3 * model_dim], preferred_element_type=jnp.float32)
    queries = (projected[:, :model_dim] + bias_query).astype(jnp.bfloat16)
    key_rows = projected[:, model_dim : 2 * model_dim].astype(jnp.bfloat16)
    value_rows = (projected[:, 2 * model_dim :] + bias_value).astype(jnp.bfloat16)
    key_all, value_all = sent_together((key_rows, value_rows), "shard", 0, 1)
    query_heads = to_heads(queries)
    key_heads = to_heads(key_all)
    value_heads = to_heads(value_all)

    def attend(packed):
        query_one, key_one, value_one = packed
        scores = (
            jnp.einsum("qd,kd->qk", query_one, key_one, preferred_element_type=jnp.float32) * scale
        )
        scores = jnp.where(allowed, scores, HUGE_NEG)
        top = jnp.max(scores, -1, keepdims=True)
        raised = jnp.exp(scores - top)
        total = jnp.sum(raised, -1, keepdims=True)
        probs = (raised / total).astype(jnp.bfloat16)
        result = jnp.einsum("qk,kd->qd", probs, value_one, preferred_element_type=jnp.float32)
        return (result, top[:, 0] + jnp.log(total[:, 0]))

    head_out, log_total = lax.map(attend, (query_heads, key_heads, value_heads))
    attended = from_heads(head_out).astype(jnp.bfloat16)
    middle = (
        inputs
        + jnp.dot(
            attended,
            full_rows[:, 3 * model_dim : 4 * model_dim],
            preferred_element_type=jnp.float32,
        )
        + bias_out
    )
    normed_two = layer_norm(middle, gain_two, shift_two).astype(jnp.bfloat16)
    pre_act = (
        jnp.dot(normed_two, full_rows[:, 4 * model_dim :], preferred_element_type=jnp.float32)
        + bias_first
    )
    hidden = gelu_tanh(pre_act).astype(jnp.bfloat16)
    outputs = (
        middle + jnp.dot(hidden, full_down, preferred_element_type=jnp.float32) + bias_down
    ).astype(jnp.bfloat16)
    w_query_kv = full_rows[:, : 3 * model_dim]
    w_out = full_rows[:, 3 * model_dim : 4 * model_dim]
    w_first = full_rows[:, 4 * model_dim :]
    grad_out = cotangent.astype(jnp.float32)
    grad_down = jnp.einsum("ti,to->io", hidden, cotangent, preferred_element_type=jnp.float32)
    grad_bias_down = jnp.sum(grad_out, 0)
    grad_hidden = jnp.einsum("to,io->ti", cotangent, full_down, preferred_element_type=jnp.float32)
    gelu_back = jax.vjp(gelu_tanh, pre_act)[1]
    grad_pre = gelu_back(grad_hidden)[0].astype(jnp.bfloat16)
    grad_first = jnp.einsum("td,ti->di", normed_two, grad_pre, preferred_element_type=jnp.float32)
    grad_bias_first = jnp.sum(grad_pre.astype(jnp.float32), 0)
    grad_normed_two = jnp.einsum("ti,di->td", grad_pre, w_first, preferred_element_type=jnp.float32)
    norm_two_back = jax.vjp(layer_norm, middle, gain_two, shift_two)[1]
    grad_mid_norm, grad_gain_two, grad_shift_two = norm_two_back(grad_normed_two)
    grad_middle = grad_out + grad_mid_norm
    grad_branch = grad_middle.astype(jnp.bfloat16)
    grad_out_proj = jnp.einsum(
        "td,to->do", attended, grad_branch, preferred_element_type=jnp.float32
    )
    grad_bias_out = jnp.sum(grad_branch.astype(jnp.float32), 0)
    grad_attended = jnp.einsum(
        "to,do->td", grad_branch, w_out, preferred_element_type=jnp.float32
    ).astype(jnp.bfloat16)
    grad_heads = to_heads(grad_attended)

    def attend_query(packed):
        query_one, key_one, value_one, grad_one, total_one = packed
        scores = (
            jnp.einsum("qd,kd->qk", query_one, key_one, preferred_element_type=jnp.float32) * scale
        )
        scores = jnp.where(allowed, scores, HUGE_NEG)
        probs = jnp.exp(scores - total_one[:, None])
        grad_probs = jnp.einsum(
            "qd,kd->qk", grad_one, value_one, preferred_element_type=jnp.float32
        )
        inner = jnp.sum(grad_probs * probs, -1, keepdims=True)
        grad_scores = (probs * (grad_probs - inner)).astype(jnp.bfloat16)
        grad_query = (
            jnp.einsum("qk,kd->qd", grad_scores, key_one, preferred_element_type=jnp.float32)
            * scale
        )
        return (grad_query, inner[:, 0])

    grad_q_heads, inner_rows = lax.map(
        attend_query, (query_heads, key_heads, value_heads, grad_heads, log_total)
    )
    grad_queries = from_heads(grad_q_heads).astype(jnp.bfloat16)
    query_pack, grad_pack = sent_together((queries, grad_attended), "shard", 0, 1)
    total_pack, inner_pack = sent_together((log_total, inner_rows), "shard", 1, 0)
    allowed_keys = (seg_all[:, None] == seg_own[None, :]) & (
        place_own[None, :] <= place_all[:, None]
    )

    def attend_key(packed):
        query_one, grad_one, total_one, inner_one, key_one, value_one = packed
        scores = (
            jnp.einsum("qd,kd->qk", query_one, key_one, preferred_element_type=jnp.float32) * scale
        )
        scores = jnp.where(allowed_keys, scores, HUGE_NEG)
        probs = jnp.exp(scores - total_one[:, None])
        grad_probs = jnp.einsum(
            "qd,kd->qk", grad_one, value_one, preferred_element_type=jnp.float32
        )
        grad_scores = (probs * (grad_probs - inner_one[:, None])).astype(jnp.bfloat16)
        grad_key = (
            jnp.einsum("qk,qd->kd", grad_scores, query_one, preferred_element_type=jnp.float32)
            * scale
        )
        grad_value = jnp.einsum(
            "qk,qd->kd", probs.astype(jnp.bfloat16), grad_one, preferred_element_type=jnp.float32
        )
        return (grad_key, grad_value)

    grad_k_heads, grad_v_heads = lax.map(
        attend_key,
        (
            to_heads(query_pack),
            to_heads(grad_pack),
            total_pack,
            inner_pack,
            to_heads(key_rows),
            to_heads(value_rows),
        ),
    )
    grad_keys = from_heads(grad_k_heads).astype(jnp.bfloat16)
    grad_values = from_heads(grad_v_heads).astype(jnp.bfloat16)
    grad_projected = jnp.concatenate([grad_queries, grad_keys, grad_values], 1)
    grad_query_kv = jnp.einsum(
        "td,tj->dj", normed, grad_projected, preferred_element_type=jnp.float32
    )
    grad_bias_query = jnp.sum(grad_queries.astype(jnp.float32), 0)
    grad_bias_value = jnp.sum(grad_values.astype(jnp.float32), 0)
    grad_normed = jnp.einsum(
        "tj,dj->td", grad_projected, w_query_kv, preferred_element_type=jnp.float32
    )
    norm_one_back = jax.vjp(layer_norm, inputs, gain_one, shift_one)[1]
    grad_in_norm, grad_gain_one, grad_shift_one = norm_one_back(grad_normed)
    grad_input = (grad_middle + grad_in_norm).astype(jnp.bfloat16)
    grad_rows_local = jnp.concatenate([grad_query_kv, grad_out_proj, grad_first], 1)
    grad_vec_local = jnp.concatenate(
        [
            jnp.stack(
                [
                    grad_gain_one,
                    grad_shift_one,
                    grad_bias_query,
                    grad_bias_value,
                    grad_bias_out,
                    grad_gain_two,
                    grad_shift_two,
                    grad_bias_down,
                ]
            ),
            grad_bias_first.reshape(-1, model_dim),
        ],
        0,
    )
    owned = (
        lax.psum_scatter(grad_rows_local, "shard", scatter_dimension=0, tiled=True),
        lax.psum_scatter(grad_down, "shard", scatter_dimension=0, tiled=True),
        lax.psum_scatter(grad_vec_local, "shard", scatter_dimension=1, tiled=True),
    )
    grad_rows, grad_down_sum, grad_vecs = packed_total((owned[0], owned[1], owned[2]), "replica")
    rows_new = adamw(w_rows, moment_rows, second_rows, grad_rows, LR_MATRIX, DECAY)
    down_new = adamw(w_down, moment_down, second_down, grad_down_sum, LR_MATRIX, DECAY)
    vec_new = adamw(vectors, moment_vectors, second_vectors, grad_vecs, LR_VECTOR, 0.0)
    return (
        outputs,
        grad_input,
        rows_new[0],
        rows_new[1],
        rows_new[2],
        down_new[0],
        down_new[1],
        down_new[2],
        vec_new[0],
        vec_new[1],
        vec_new[2],
    )


def solution(mesh):
    return jax.shard_map(
        per_device,
        mesh=mesh,
        in_specs=(
            P(("replica", "shard"), None),
            P(("replica", "shard"), None),
            P("replica", None),
            P("replica", None),
            P("shard", None),
            P("shard", None),
            P(None, "shard"),
            P("shard", None),
            P("shard", None),
            P("shard", None),
            P("shard", None),
            P(None, "shard"),
            P(None, "shard"),
        ),
        out_specs=(
            P(("replica", "shard"), None),
            P(("replica", "shard"), None),
            P("shard", None),
            P("shard", None),
            P("shard", None),
            P("shard", None),
            P("shard", None),
            P("shard", None),
            P(None, "shard"),
            P(None, "shard"),
            P(None, "shard"),
        ),
        check_vma=False,
    )
```

profile of v0, /device:TPU:1, one launch (start us, length us, event | category | flops | bytes accessed | tf_op | source)
XLA Modules:
  0.0 704.5 jit_solution(6550378009148591967)
XLA Ops:
  7.3 2.2 convert_element_type.127
  10.4 21.4 %all-gather = bf16[16,48,12]{1,2,0:T(8,128)(2,1)S(1)} all-gather(bf16[1,48,12]{1,2,0:T(8,128)(2,1)S(1)} %convert_bitcast_fusion), channel_id=1, replica_groups=mesh['replica'=8,'shard'=16] {'shard'}, dimensions={0}, use_global_device_ids=true | all-gather | bytes 19584 | tf_op jit(solution)/shard_map/all_gather | solution.py:93
  32.9 57.2 %all-gather.6.cloned.1.call-done = bf16[768,6144]{1,0:T(8,128)(2,1)} async-done(((bf16[48,6144]{1,0:T(8,128)(2,1)}), bf16[768,6144]{1,0:T(8,128)(2,1)}) %all-gather.6.cloned.1.call-update) | async-done | bytes 9437200 | tf_op jit(solution)/shard_map/all_gather | solution.py:91
  90.1 2.7 fusion.79
  96.6 49.9 %all-gather.10.cloned.1.call-done = bf16[3072,768]{1,0:T(8,128)(2,1)} async-done(((bf16[192,768]{1,0:T(8,128)(2,1)}), bf16[3072,768]{1,0:T(8,128)(2,1)}) %all-gather.10.cloned.1.call-update) | async-done | bytes 4718608 | tf_op jit(solution)/shard_map/all_gather | solution.py:92
  146.5 5.1 fusion.132
  152.7 57.5 %all-gather.8.cloned.1.call-done = bf16[2048,1536]{1,0:T(8,128)(2,1)} async-done(((bf16[128,1536]{1,0:T(8,128)(2,1)}), bf16[2048,1536]{1,0:T(8,128)(2,1)}) %all-gather.8.cloned.1.call-update) | async-done | bytes 6291472 | tf_op jit(solution)/shard_map/all_gather | solution.py:23
  210.3 5.0 fusion.129
  215.2 4.7 copy.99
  219.9 6.6 copy.102
  226.5 3.0 copy.98
  229.5 6.6 copy.101
  236.2 40.7 %while.39 = (s32[]{:T(128)}, bf16[12,128,64]{1,2,0:T(8,128)(2,1)S(1)}, f32[12,128]{1,0:T(8,128)S(1)}, bf16[12,128,64]{2,1,0:T(8,128)(2,1)}, bf16[12,2048,64]{2,1...) while((s32[]{:T(128)}, ...), condition=%wide.region_8.9_spmd.clone, body=%wide.region_5.8_spmd.clone.sunk | while | flops 69992320 | bytes 4284545 | solution.py:134
  277.5 1.7 fusion.131
  279.5 4.3 convert_reduce_fusion
  283.8 5.6 multiply_reduce_fusion.1
  291.5 1.8 convolution_convert_fusion
  297.7 5.2 fusion.119
  303.6 54.4 %while.40 = (s32[]{:T(128)}, bf16[12,128,64]{1,2,0:T(8,128)(2,1)S(1)}, f32[12,128]{1,0:T(8,128)S(1)}, bf16[12,128,64]{2,1,0:T(8,128)(2,1)}, bf16[12,2048,64]{2,1...) while((s32[]{:T(128)}, ...), condition=%wide.region_15.16_spmd.clone, body=%wide.region_13.15_spmd.clone.sunk | while | flops 103554944 | bytes 6921877 | solution.py:197
  359.3 19.4 %all_gather.23 = f32[24,2048]{1,0:T(8,128)S(1)} all-gather(f32[24,128]{1,0:T(8,128)S(1)} %pad_maximum_fusion.7), channel_id=1, replica_groups=mesh['replica'=8,'shard'=16] {'shard'}, dimensions={1}, use_global_device_ids=true | all-gather | bytes 208896 | tf_op jit(solution)/shard_map/all_gather | solution.py:23
  378.7 1.9 fusion.133
  381.3 5.1 fusion.118
  386.5 5.0 fusion.128
  391.5 4.9 copy.110
  396.3 3.0 copy.108
  399.4 86.2 %while.41 = (s32[]{:T(128)}, bf16[12,128,64]{1,2,0:T(8,128)(2,1)S(1)}, bf16[12,128,64]{1,2,0:T(8,128)(2,1)S(1)}, bf16[12,2048,64]{1,2,0:T(8,128)(2,1)}, bf16[12,...) while((s32[]{:T(128)}, ...), condition=%wide.region_17.18_spmd.clone, body=%wide.region_16.17_spmd.clone.sunk | while | flops 136847360 | bytes 4363409 | solution.py:227
  400.4 3.4 fusion.181
  403.8 1.7 fusion.182
  407.7 3.4 fusion.181
  411.0 1.7 fusion.182
  414.8 3.4 fusion.181
  422.0 3.4 fusion.181
  429.2 3.4 fusion.181
  436.4 3.4 fusion.181
  443.6 3.4 fusion.181
  450.7 3.4 fusion.181
  457.9 3.4 fusion.181
  465.1 3.4 fusion.181
  472.2 3.4 fusion.181
  479.4 3.4 fusion.181
  487.4 10.9 %pad_maximum_fusion = f32[768,6144]{1,0:T(8,128)} fusion(f32[768,3072]{1,0:T(8,128)} %fusion.118, f32[768,768]{1,0:T(8,128)S(1)} %copy-done, f32[768,2304]{1,0:T(8,128)S(1)} %fusion.109), kind=kLoop, calls=%fused_computation.77 | loop fusion | flops 9437184 | bytes 37748736 | tf_op jit(solution)/shard_map/concatenate | solution.py:252
  500.6 3.4 fusion.120
  505.6 60.8 %all-reduce = f32[12,768]{1,0:T(8,128)S(1)} all-reduce(f32[12,768]{1,0:T(8,128)S(1)} %concatenate.26), channel_id=4, replica_groups=mesh['replica'=8,'shard'=16] {'shard'}, use_global_device_ids=true, to_apply=%region_31.32.clone | all-reduce | flops 9216 | bytes 73728
  567.7 56.0 %reduce-scatter.4.cloned.1.call-done = f32[48,6144]{1,0:T(8,128)} async-done(((f32[768,6144]{1,0:T(8,128)}), f32[48,6144]{1,0:T(8,128)}) %reduce-scatter.4.cloned.1.call-update) | async-done | bytes 1179664 | tf_op jit(solution)/shard_map/reduce_scatter | solution.py:272
  627.6 4.1 fusion.91
  631.7 57.0 %all-reduce.3.cloned.1.call-done = f32[442944]{0:T(1024)} async-done(((f32[442944]{0:T(1024)}), f32[442944]{0:T(1024)}) %all-reduce.3.cloned.1.call-update) | async-done | bytes 1771792 | tf_op jit(solution)/shard_map/psum | solution.py:32
  692.6 2.7 multiply_subtract_fusion.1
  695.3 2.4 multiply_subtract_fusion
  (379 shorter events, 166.8 us)
Async XLA Ops:
  7.2 3.2 copy-start.29
  7.2 25.4 %copy-start.1 = (bf16[128,768]{1,0:T(8,128)(2,1)S(1)}, bf16[128,768]{1,0:T(8,128)(2,1)}, u32[]{:S(2)}) copy-start(bf16[128,768]{1,0:T(8,128)(2,1)} %param.19) | copy-start | bytes 589828
  7.2 82.9 %all-gather.6.cloned.1.call-start = ((), (), s32[]{:S(2)}) async-start(), calls=%async_computation.2 | async-start | bytes 10027008 | tf_op jit(solution)/shard_map/all_gather | solution.py:91
  9.5 137.1 %all-gather.10.cloned.1.call-start = ((), (), s32[]{:S(2)}) async-start(), calls=%async_computation.4 | async-start | bytes 5013504 | tf_op jit(solution)/shard_map/all_gather | solution.py:92
  10.3 200.0 %all-gather.8.cloned.1.call-start = ((), (), s32[]{:S(2)}) async-start(), calls=%async_computation.3 | async-start | bytes 6684672 | tf_op jit(solution)/shard_map/all_gather | solution.py:23
  32.7 57.4 %copy-start.35 = (f32[128]{0:T(128)}, f32[128]{0:T(128)S(1)}, u32[]{:S(2)}) copy-start(f32[128]{0:T(128)S(1)} %broadcast_multiply_fusion.1) | copy-start | bytes 1540
  32.9 57.2 %copy-start.57 = (f32[128]{0:T(128)}, f32[128]{0:T(128)S(1)}, u32[]{:S(2)}) copy-start(f32[128]{0:T(128)S(1)} %fusion.104) | copy-start | bytes 1540
  32.9 57.2 %copy-start.39 = (f32[128]{0:T(128)}, f32[128]{0:T(128)S(1)}, u32[]{:S(2)}) copy-start(f32[128]{0:T(128)S(1)} %fusion.111) | copy-start | bytes 1540
  92.8 2.5 copy-start.43
  92.8 53.7 %copy-start.9 = (bf16[128,768]{1,0:T(8,128)(2,1)S(1)}, bf16[128,768]{1,0:T(8,128)(2,1)}, u32[]{:S(2)}) copy-start(bf16[128,768]{1,0:T(8,128)(2,1)} %param.20) | copy-start | bytes 589828
  92.9 58.8 %copy-start.16 = (bf16[128,768]{1,0:T(8,128)(2,1)}, bf16[128,768]{1,0:T(8,128)(2,1)S(1)}, u32[]{:S(2)}) copy-start(bf16[128,768]{1,0:T(8,128)(2,1)S(1)} %slice.161) | copy-start | bytes 589828
  93.0 58.7 %copy-start.14 = (bf16[128,768]{1,0:T(8,128)(2,1)}, bf16[128,768]{1,0:T(8,128)(2,1)S(1)}, u32[]{:S(2)}) copy-start(bf16[128,768]{1,0:T(8,128)(2,1)S(1)} %get-tuple-element.495) | copy-start | bytes 589828
  94.4 292.1 %all-gather.12.cloned.1.call-start = ((), (), s32[]{:S(2)}) async-start(), calls=%async_computation.5 | async-start | bytes 6684672 | tf_op jit(solution)/shard_map/all_gather | solution.py:23
  95.3 57.5 %copy-start.61 = (s32[128]{0:T(128)}, s32[128]{0:T(128)S(1)}, u32[]{:S(2)}) copy-start(s32[128]{0:T(128)S(1)} %dynamic-slice_bitcast_fusion) | copy-start | bytes 1540
  229.5 6.7 copy-start.44
  229.5 6.7 copy-start.47
  229.5 6.7 copy-start.62
  229.5 6.7 copy-start.66
  236.2 41.3 %copy-start.33 = (f32[768]{0:T(1024)S(1)}, f32[768]{0:T(1024)}, u32[]{:S(2)}) copy-start(f32[768]{0:T(1024)} %get-tuple-element.394) | copy-start | bytes 9220
  276.9 2.6 copy-start.20
  276.9 2.6 copy-start.38
  279.2 102.1 %copy-start.2 = (f32[128,768]{1,0:T(8,128)}, f32[128,768]{1,0:T(8,128)S(1)}, u32[]{:S(2)}) copy-start(f32[128,768]{1,0:T(8,128)S(1)} %get-tuple-element.501) | copy-start | bytes 1179652
  279.2 10.1 %copy-start.41 = (f32[128]{0:T(128)}, f32[128]{0:T(128)S(1)}, u32[]{:S(2)}) copy-start(f32[128]{0:T(128)S(1)} %broadcast_multiply_fusion) | copy-start | bytes 1540
  279.5 9.9 %copy-start.50 = (f32[128]{0:T(128)}, f32[128]{0:T(128)S(1)}, u32[]{:S(2)}) copy-start(f32[128]{0:T(128)S(1)} %fusion.112) | copy-start | bytes 1540
  283.7 5.6 copy-start.23
  283.8 13.9 %copy-start.7 = (f32[128,3072]{1,0:T(8,128)}, f32[128,3072]{1,0:T(8,128)S(1)}, u32[]{:S(2)}) copy-start(f32[128,3072]{1,0:T(8,128)S(1)} %get-tuple-element.502) | copy-start | bytes 4718596
  289.6 5.3 copy-start.5
  289.6 4.5 copy-start.15
  290.9 4.1 copy-start.13
  291.5 4.2 copy-start.17
  294.9 271.7 %reduce-scatter.6.cloned.1.call-start = ((), (), s32[]{:S(2)}) async-start(), calls=%async_computation.7 | async-start | bytes 10027008 | tf_op jit(solution)/shard_map/reduce_scatter | solution.py:273
  302.9 320.8 %reduce-scatter.4.cloned.1.call-start = ((), (), s32[]{:S(2)}) async-start(), calls=%async_computation.6 | async-start | bytes 20054016 | tf_op jit(solution)/shard_map/reduce_scatter | solution.py:272
  303.6 75.0 %copy-start.27 = (bf16[128,768]{1,0:T(8,128)(2,1)S(1)}, bf16[128,768]{1,0:T(8,128)(2,1)}, u32[]{:S(2)}) copy-start(bf16[128,768]{1,0:T(8,128)(2,1)} %copy-done.26) | copy-start | bytes 589828
  358.7 22.6 %copy-start.18 = (bf16[12,128,64]{1,2,0:T(8,128)(2,1)}, bf16[12,128,64]{1,2,0:T(8,128)(2,1)S(1)}, u32[]{:S(2)}) copy-start(bf16[12,128,64]{1,2,0:T(8,128)(2,1)S(1)} %get-tuple-element.152) | copy-start | bytes 589828
  378.6 2.7 copy-start.24
  378.6 2.7 copy-start.42
  378.7 2.7 copy-start.51
  396.3 3.0 copy-start.65
  399.4 86.3 %copy-start.19 = (bf16[12,128,64]{1,2,0:T(8,128)(2,1)S(1)}, bf16[12,128,64]{1,2,0:T(8,128)(2,1)}, u32[]{:S(2)}) copy-start(bf16[12,128,64]{1,2,0:T(8,128)(2,1)} %copy-done.18) | copy-start | bytes 589828
  399.4 86.3 %copy-start.36 = (f32[128]{0:T(128)S(1)}, f32[128]{0:T(128)}, u32[]{:S(2)}) copy-start(f32[128]{0:T(128)} %copy-done.35) | copy-start | bytes 1540
  399.4 86.3 %copy-start.40 = (f32[128]{0:T(128)S(1)}, f32[128]{0:T(128)}, u32[]{:S(2)}) copy-start(f32[128]{0:T(128)} %copy-done.39) | copy-start | bytes 1540
  498.4 190.4 %all-reduce.3.cloned.1.call-start = ((), (), s32[]{:S(2)}) async-start(), calls=%async_computation.8 | async-start | bytes 3547136 | tf_op jit(solution)/shard_map/psum | solution.py:32
  500.5 3.5 copy-start.58
  500.5 3.8 copy-start.6
  500.6 3.8 copy-start.56
  692.6 2.7 copy-start.4
  692.6 2.7 copy-start.21
  692.6 2.7 copy-start.22
  (30 other events, 35.5 us)
Sparse Core Ops, SparseCore 0:
  10.8 79.2 all-gather.5
  92.8 53.6 all-gather.9
  149.3 60.9 all-gather.7
  295.0 60.9 all-gather.11
  359.3 86.6 reduce-scatter.5
  498.5 125.2 reduce-scatter.3
  626.7 62.0 all-reduce.2
where the time goes:
time: 712 us; the launch traced here: 705 us
  waiting for transfers between devices  278 us (39%)
  matrix products  207 us (29%)
  blocking collectives  102 us (14%)
  local copies, waits for them, and re-layouts  69.4 us (10%)
  other arithmetic  31.5 us (4%)
  between operations  15.6 us (2%)
    unnamed x1, blocking collectives  60.8 us
    all_gather x2, waiting for transfers between devices, sent_together(): whole, at, done = (lax.all_gather(both, axis, axis=dim, tiled=True), 0, [])  57.5 us
    all_gather x1, waiting for transfers between devices, per_device(): lax.all_gather(low_weights[0], 'shard', axis=0, tiled=True)  57.2 us
    psum x1, waiting for transfers between devices, packed_total(): total = lax.psum(ravelled, axis)  57 us
    reduce_scatter x1, waiting for transfers between devices, per_device(): lax.psum_scatter(grad_rows_local, 'shard', scatter_dimension=0, tiled=True)  56 us
    all_gather x1, waiting for transfers between devices, per_device(): lax.all_gather(low_weights[1], 'shard', axis=0, tiled=True)  49.9 us
    dot_general x12, matrix products, attend_key(): jnp.einsum('qd,kd->qk', query_one, key_one, preferred_element_type=jnp.fl...  40.5 us
    slice x7, local copies, waits for them, and re-layouts, sent_together(): done.append(lax.slice_in_dim(whole, at, at + a.shape[along], axis=along))  26.2 us
  transfers between devices with their start and end apart: 7, of which 5 were waited for; matrix products, arithmetic and copies ran while one was open for 29% of the time, Pallas kernels for 0%

commit v1 on v0

v1 whole, which is shorter than its diff:
```python
import functools

import jax
import jax.numpy as jnp
from jax import lax
from jax.experimental import pallas as pl
from jax.experimental.pallas import tpu as pltpu
from jax.sharding import PartitionSpec as P

H = 12
HD = 64
STEP = 10
D = 768
FF = 3072
OWN = 128
GROUP = 2048
NEIGHBOURS = 4
TILE = 256
CHUNK = 256
MIB = 1 << 20

EPS_NORM = 1e-05
BETA_ONE = 0.9
BETA_TWO = 0.95
EPS_ADAM = 1e-08
LR_MATRIX = 0.02
LR_VECTOR = 0.3
DECAY = 0.1
HUGE_NEG = -1e30

BF = jnp.bfloat16
F32 = jnp.float32
MESH = pl.DeviceIdType.MESH
VMEM = pl.BlockSpec(memory_space=pltpu.VMEM)
ANY = pl.BlockSpec(memory_space=pl.ANY)


def step4(i, d):
    return lax.rem(i + d, 4)


class Place:
    def __init__(self):
        self.r = lax.axis_index("replica")
        self.s = lax.axis_index("shard")
        self.x = lax.div(self.r, 2)
        self.c = lax.rem(self.r, 2)
        self.z = lax.div(self.s, 4)
        self.y = lax.rem(self.s, 4)

    def ydev(self, d):
        return (self.r, self.z * 4 + step4(self.y, d))

    def zdev(self, d):
        return (self.r, step4(self.z, d) * 4 + self.y)

    def xdev(self, d):
        return (step4(self.x, d) * 2 + self.c, self.s)

    def sibling(self):
        return (self.x * 2 + 1 - self.c, self.s)


def greet(devices):
    barrier = pltpu.get_barrier_semaphore()
    for device in devices:
        pl.semaphore_signal(barrier, inc=1, device_id=device, device_id_type=MESH)
    pl.semaphore_wait(barrier, len(devices))


class Wire:
    def __init__(self, send_sems, recv_sems, local_sems):
        self.send_sems, self.recv_sems, self.local_sems = send_sems, recv_sems, local_sems
        self.sent, self.moved = 0, 0

    def push(self, src, dst, device):
        k = self.sent
        self.sent += 1
        copy = pltpu.make_async_remote_copy(
            src_ref=src,
            dst_ref=dst,
            send_sem=self.send_sems.at[k],
            recv_sem=self.recv_sems.at[k],
            device_id=device,
            device_id_type=MESH,
        )
        copy.start()
        return copy

    def local(self, src, dst):
        k = self.moved
        self.moved += 1
        copy = pltpu.make_async_copy(src, dst, self.local_sems.at[k])
        copy.start()
        return copy


def sems(remote, local):
    return [
        pltpu.SemaphoreType.DMA((remote,)),
        pltpu.SemaphoreType.DMA((remote,)),
        pltpu.SemaphoreType.DMA((max(local, 1),)),
    ]


def cut(axis, base, size):
    if axis == 0:
        return (pl.ds(pl.multiple_of(base, 16), size), slice(None))
    return (slice(None), pl.ds(pl.multiple_of(base, 128), size))


class Gather:
    def __init__(self, wire, place, shard, full, axis, base, size, y_first):
        self.wire, self.place, self.shard, self.full = wire, place, shard, full
        self.region = cut(axis, base, size)
        self.y_first = y_first

    def slab(self, d):
        p = self.place
        if self.y_first:
            return self.full.at[(step4(p.z, 4 - d), slice(None)) + self.region]
        return self.full.at[(slice(None), step4(p.y, 4 - d)) + self.region]

    def first(self):
        p, w = self.place, self.wire
        src = self.shard.at[self.region]
        dst = self.full.at[(p.z, p.y) + self.region]
        self.own = w.local(src, dst)
        self.one = [w.push(src, dst, p.ydev(d) if self.y_first else p.zdev(d)) for d in (1, 3, 2)]

    def second(self):
        p, w = self.place, self.wire
        self.own.wait()
        for copy in self.one:
            copy.wait_recv()
        slab = self.slab(0)
        self.two = [(d, w.push(slab, slab, p.zdev(d) if self.y_first else p.ydev(d))) for d in (1, 3, 2)]
        self.across = [w.push(slab, slab, p.sibling())]

    def third(self):
        p, w = self.place, self.wire
        for d, copy in self.two:
            copy.wait_recv()
            slab = self.slab(d)
            self.across.append(w.push(slab, slab, p.sibling()))

    def end(self):
        for copy in self.across:
            copy.wait_recv()
        for copy in self.one + [copy for _, copy in self.two] + self.across:
            copy.wait_send()


GATHER_SENDS = 10


def scatter_shapes(rows, cols, shared, dtype):
    shapes = [
        pltpu.VMEM((4, 4, rows, cols), dtype),
        pltpu.VMEM((4, 4, rows, cols), dtype),
        pltpu.VMEM((3, 4, rows, cols), dtype),
        pltpu.VMEM((4, rows, cols), dtype),
        pltpu.VMEM((3, rows, cols), dtype),
        pltpu.VMEM((4, rows, cols), dtype),
    ]
    return shapes


class Scatter:
    def __init__(self, wire, place, grad, out, axis, half, offset, size, z_first, shared, scratch):
        self.wire, self.place, self.grad, self.out = wire, place, grad, out
        self.shared, self.z_first = shared, z_first
        if shared:
            self.mine = cut(axis, place.c * half + offset, size)
            self.other = cut(axis, (1 - place.c) * half + offset, size)
        else:
            self.mine = self.other = (slice(None), slice(None))
        self.held, self.in0, self.in1, self.part, self.in2, self.in3 = scratch
        self.sends = []

    def push(self, src, dst, device):
        copy = self.wire.push(src, dst, device)
        self.sends.append(copy)
        return copy

    def p0(self):
        every = (slice(None), slice(None))
        self.load = self.wire.local(self.grad.at[every + self.mine], self.held)
        self.wait = [self.push(self.grad.at[every + self.other], self.in0, self.place.sibling())]

    def p1(self):
        p = self.place
        self.load.wait()
        self.wait[0].wait_recv()

        def add(i, carry):
            a, b = lax.div(i, 4), lax.rem(i, 4)
            both = self.held[a, b].astype(F32) + self.in0[a, b].astype(F32)
            self.held[a, b] = both.astype(self.held.dtype)
            return carry

        lax.fori_loop(0, 16, add, 0)
        self.wait = []
        for d in (1, 3, 2):
            if self.z_first:
                src, device = self.held.at[step4(p.z, d)], p.zdev(d)
            else:
                src, device = self.held.at[:, step4(p.y, d)], p.ydev(d)
            self.wait.append(self.push(src, self.in1.at[d - 1], device))

    def p2(self):
        p = self.place
        for copy in self.wait:
            copy.wait_recv()

        def add(i, carry):
            own = self.held[p.z, i] if self.z_first else self.held[i, p.y]
            total = own.astype(F32)
            for k in range(3):
                total = total + self.in1[k, i].astype(F32)
            self.part[i] = total.astype(self.part.dtype)
            return carry

        lax.fori_loop(0, 4, add, 0)
        self.wait = []
        for d in (1, 3, 2):
            if self.z_first:
                src, device = self.part.at[step4(p.y, d)], p.ydev(d)
            else:
                src, device = self.part.at[step4(p.z, d)], p.zdev(d)
            self.wait.append(self.push(src, self.in2.at[d - 1], device))

    def p3(self):
        p = self.place
        for copy in self.wait:
            copy.wait_recv()
        total = self.part[p.y if self.z_first else p.z].astype(F32)
        for k in range(3):
            total = total + self.in2[k].astype(F32)
        self.in3[p.x] = total.astype(self.in3.dtype)
        self.wait = [self.push(self.in3.at[p.x], self.in3.at[p.x], p.xdev(d)) for d in (1, 3, 2)]

    def p4(self):
        for copy in self.wait:
            copy.wait_recv()
        total = self.in3[0].astype(F32)
        for k in range(1, 4):
            total = total + self.in3[k].astype(F32)
        self.out[self.mine] = total
        self.wait = []
        if self.shared:
            here = self.out.at[self.mine]
            self.wait = [self.push(here, here, self.place.sibling())]

    def end(self):
        for copy in self.wait:
            copy.wait_recv()
        for copy in self.sends:
            copy.wait_send()


SCATTER_SENDS = 11


def all_peers(p):
    rings = [p.ydev(d) for d in (1, 2, 3)] + [p.zdev(d) for d in (1, 2, 3)]
    return rings + [p.sibling()]


def x_peers(p):
    return [p.xdev(d) for d in (1, 2, 3)]


def gather_first_kernel(shard, full, send_sems, recv_sems, local_sems):
    p = Place()
    w = Wire(send_sems, recv_sems, local_sems)
    greet(all_peers(p))
    half = shard.shape[1] // 2
    size = half // 2
    parts = [
        Gather(w, p, shard, full, 1, p.c * half, size, True),
        Gather(w, p, shard, full, 1, p.c * half + size, size, False),
    ]
    for part in parts:
        part.first()
    for part in parts:
        part.second()
    for part in parts:
        part.third()
    for part in parts:
        part.end()


def gather_first(shard):
    rows, cols = shard.shape
    full = pl.pallas_call(
        gather_first_kernel,
        out_shape=jax.ShapeDtypeStruct((4, 4, rows, cols), BF),
        in_specs=[VMEM],
        out_specs=VMEM,
        scratch_shapes=sems(2 * GATHER_SENDS, 2),
        compiler_params=pltpu.CompilerParams(
            collective_id=0, has_side_effects=True, vmem_limit_bytes=20 * MIB
        ),
        name="gather_first",
    )(shard)
    return full.reshape(16 * rows, cols)


def half_lanes(value, right):
    lane = lax.broadcasted_iota(jnp.int32, value.shape, 1)
    keep = lane >= HD if right else lane < HD
    return jnp.where(keep, value, jnp.zeros_like(value))


def rows_max(value):
    return jnp.max(value.reshape(-1, 8, value.shape[1]), axis=0)


def rows_sum(value):
    return jnp.sum(value.reshape(-1, 8, value.shape[1]), axis=0)


def dot_lanes(left, right):
    return lax.dot_general(left, right, (((1,), (1,)), ((), ())), preferred_element_type=F32)


def dot_plain(left, right):
    return jnp.dot(left, right, preferred_element_type=F32)


def fill_bias(key_place, query_place, bias):
    def body(i, carry):
        rows = pl.ds(pl.multiple_of(i * CHUNK, CHUNK), CHUNK)
        keys = key_place[rows, :]
        ok = (keys <= query_place[0:1, :]) & (keys >= query_place[1:2, :])
        bias[rows, :] = jnp.where(ok, 0.0, HUGE_NEG).astype(F32)
        return carry

    lax.fori_loop(0, GROUP // CHUNK, body, 0)


def key_chunk(packed, i, head):
    a, b = lax.div(i, 2), lax.rem(i, 2) * 2
    return packed[a, pl.ds(b, 2), :, head * 128 : head * 128 + 128].reshape(CHUNK, 128)


def chunk_rows(i):
    return pl.ds(pl.multiple_of(i * CHUNK, CHUNK), CHUNK)


def turn_keys(packed, head, turned):
    def body(i, carry):
        turned[:, chunk_rows(i)] = key_chunk(packed, i, head).T
        return carry

    lax.fori_loop(0, GROUP // CHUNK, body, 0)


def forward_kernel(
    packed, rest, down, key_place, query_place,
    full_rest, full_down, kv, attended, lse,
    bias, scores, turned, head_out, out_send, send_sems, recv_sems, local_sems,
):
    p = Place()
    w = Wire(send_sems, recv_sems, local_sems)
    greet(all_peers(p))
    kv[p.z, p.y] = packed[p.y]
    to_y = [
        w.push(packed.at[step4(p.y, d)], kv.at[p.z, p.y], p.ydev(d)) for d in (1, 3, 2)
    ]
    rest_half, down_half = rest.shape[1] // 2, down.shape[0] // 2
    rest_one = 1024
    parts = [
        Gather(w, p, rest, full_rest, 1, p.c * rest_half, rest_one, True),
        Gather(w, p, rest, full_rest, 1, p.c * rest_half + rest_one, rest_half - rest_one, False),
        Gather(w, p, down, full_down, 0, p.c * down_half, down_half // 2, True),
        Gather(w, p, down, full_down, 0, p.c * down_half + down_half // 2, down_half // 2, False),
    ]
    for part in parts:
        part.first()
    for copy in to_y:
        copy.wait_recv()
    mine = kv.at[p.z, :, :, pl.ds(0, 384)]
    to_z = [w.push(mine, mine, p.zdev(d)) for d in (1, 3, 2)]
    for part in parts:
        part.second()
    fill_bias(key_place, query_place, bias)
    for copy in to_z:
        copy.wait_recv()
    head_out[128:192, :] = jnp.zeros((64, 512), F32)
    lse[...] = jnp.zeros_like(lse)
    for head in range(3):
        turn_keys(kv, head, turned)
        for tile in range(2):
            cols = slice(tile * TILE, tile * TILE + TILE)
            query = kv[p.z, 2 * tile : 2 * tile + 2, :, 384 + head // 2 * 128 : 512 + head // 2 * 128]
            query = half_lanes(query.reshape(TILE, 128), head == 1)

            def score(i, top):
                part = dot_lanes(key_chunk(kv, i, head), query) + bias[chunk_rows(i), cols]
                scores[chunk_rows(i), :] = part
                return jnp.maximum(top, rows_max(part))

            top = lax.fori_loop(0, GROUP // CHUNK, score, jnp.full((8, TILE), -jnp.inf, F32))
            top = jnp.max(top, axis=0, keepdims=True)

            def mix(i, carry):
                total, acc = carry
                raised = jnp.exp(scores[chunk_rows(i), :] - top)
                acc = acc + dot_plain(turned[:, chunk_rows(i)], raised.astype(BF))
                return total + rows_sum(raised), acc

            total, acc = lax.fori_loop(
                0, GROUP // CHUNK, mix, (jnp.zeros((8, TILE), F32), jnp.zeros((128, TILE), F32))
            )
            total = jnp.sum(total, axis=0, keepdims=True)
            acc = acc / total
            if head == 0:
                head_out[64:128, cols] = acc[64:128, :]
            elif head == 1:
                head_out[0:64, cols] = acc[0:64, :]
            else:
                head_out[192:256, cols] = acc[64:128, :]
            lse[head : head + 1, cols] = top + jnp.log(total)
        if head == 1:
            for part in parts:
                part.third()
    for k in range(4):
        turned_out = head_out[:, k * OWN : k * OWN + OWN].T
        out_send[k] = turned_out.astype(BF)
    attended[p.y] = out_send[p.y]
    back = [
        w.push(out_send.at[step4(p.y, d)], attended.at[p.y], p.ydev(d)) for d in (1, 3, 2)
    ]
    for copy in back:
        copy.wait_recv()
    for part in parts:
        part.end()
    for copy in to_y + to_z + back:
        copy.wait_send()


def forward_attention(packed, rest, down, key_place, query_place):
    rows, cols = rest.shape
    drows, dcols = down.shape
    out = pl.pallas_call(
        forward_kernel,
        out_shape=(
            jax.ShapeDtypeStruct((4, 4, rows, cols), BF),
            jax.ShapeDtypeStruct((4, 4, drows, dcols), BF),
            jax.ShapeDtypeStruct((4, 4, OWN, 640), BF),
            jax.ShapeDtypeStruct((4, OWN, 256), BF),
            jax.ShapeDtypeStruct((8, 512), F32),
        ),
        in_specs=[VMEM] * 5,
        out_specs=(VMEM, VMEM, VMEM, VMEM, VMEM),
        scratch_shapes=[
            pltpu.VMEM((GROUP, 512), F32),
            pltpu.VMEM((GROUP, TILE), F32),
            pltpu.VMEM((128, GROUP), BF),
            pltpu.VMEM((256, 512), F32),
            pltpu.VMEM((4, OWN, 256), BF),
        ]
        + sems(4 * GATHER_SENDS + 9, 4),
        compiler_params=pltpu.CompilerParams(
            collective_id=1, has_side_effects=True, vmem_limit_bytes=40 * MIB
        ),
        name="forward_attention",
    )(packed, rest, down, key_place, query_place)
    full_rest, full_down, kv, attended, lse = out
    return full_rest.reshape(16 * rows, cols), full_down.reshape(16 * drows, dcols), kv, attended, lse


def backward_kernel(
    grad_att, kv, lse, key_place, query_place, g_down, g_first, g_out,
    grad_packed, o_down, o_first, o_out, *scratch,
):
    (bias, probs, grad_probs, turned, dob, acc, part_send, part_in, dq, packed_send) = scratch[:10]
    send_sems, recv_sems, local_sems = scratch[-3:]
    blocks = scratch[10:-3]
    p = Place()
    w = Wire(send_sems, recv_sems, local_sems)
    greet(all_peers(p) + x_peers(p))
    dob[p.y] = grad_att[p.y]
    to_y = [
        w.push(grad_att.at[step4(p.y, d)], dob.at[p.y], p.ydev(d)) for d in (1, 3, 2)
    ]
    parts = [
        Scatter(w, p, g_down, o_down, 0, 96, 0, 48, True, True, blocks[0:6]),
        Scatter(w, p, g_down, o_down, 0, 96, 48, 48, False, True, blocks[6:12]),
        Scatter(w, p, g_first, o_first, 1, 1536, 0, 768, True, True, blocks[12:18]),
        Scatter(w, p, g_first, o_first, 1, 1536, 768, 768, False, True, blocks[18:24]),
        Scatter(w, p, g_out, o_out, 1, 384, 0, 384, True, True, blocks[24:30]),
    ]
    for part in parts:
        part.p0()
    fill_bias(key_place, query_place, bias)
    for copy in to_y:
        copy.wait_recv()
    stages = [
        lambda: [part.p1() for part in parts[:2]],
        lambda: [part.p1() for part in parts[2:]],
        lambda: [part.p2() for part in parts[:2]],
        lambda: [part.p2() for part in parts[2:]],
        lambda: [part.p3() for part in parts],
        lambda: [part.p4() for part in parts],
    ]
    to_z = []
    for head in range(3):
        turn_keys(kv, head, turned)
        for tile in range(2):
            cols = slice(tile * TILE, tile * TILE + TILE)
            block = head // 2 * 128
            query = kv[p.z, 2 * tile : 2 * tile + 2, :, 384 + block : 512 + block]
            query = half_lanes(query.reshape(TILE, 128), head == 1)
            dout = dob[2 * tile : 2 * tile + 2, :, block : block + 128]
            dout = half_lanes(dout.reshape(TILE, 128), head != 1)
            total = lse[head : head + 1, cols]

            def weigh(i, inner):
                keys = key_chunk(kv, i, head)
                prob = jnp.exp(dot_lanes(keys, query) + bias[chunk_rows(i), cols] - total)
                gprob = dot_lanes(keys, dout)
                probs[chunk_rows(i), :] = prob
                grad_probs[chunk_rows(i), :] = gprob
                return inner + rows_sum(prob * gprob)

            inner = lax.fori_loop(0, GROUP // CHUNK, weigh, jnp.zeros((8, TILE), F32))
            inner = jnp.sum(inner, axis=0, keepdims=True)

            def back(i, total_dq):
                prob = probs[chunk_rows(i), :]
                gscore = (prob * (grad_probs[chunk_rows(i), :] - inner)).astype(BF)
                both = dot_plain(gscore, query) + dot_plain(prob.astype(BF), dout)
                if tile == 0:
                    acc[chunk_rows(i), :] = both
                else:
                    part_send[head, lax.div(i, 2), pl.ds(pl.multiple_of(lax.rem(i, 2) * CHUNK, CHUNK), CHUNK), :] = (
                        acc[chunk_rows(i), :] + both
                    ).astype(BF)
                return total_dq + dot_plain(turned[:, chunk_rows(i)], gscore)

            total_dq = lax.fori_loop(0, GROUP // CHUNK, back, jnp.zeros((128, TILE), F32))
            total_dq = total_dq * (HD ** (-0.5))
            if head == 0:
                dq[0:64, cols] = total_dq[0:64, :]
            elif head == 1:
                dq[64:128, cols] = total_dq[64:128, :]
            else:
                dq[128:192, cols] = total_dq[0:64, :]
            stages[head * 2 + tile]()
        to_z.append(
            [
                w.push(part_send.at[head, step4(p.z, d)], part_in.at[head, d - 1], p.zdev(d))
                for d in (1, 3, 2)
            ]
        )
    dq[192:256, :] = jnp.zeros((64, 512), F32)
    for k in range(4):
        packed_send[k, :, 384:640] = dq[:, k * OWN : k * OWN + OWN].T.astype(BF)
    for head in range(3):
        for copy in to_z[head]:
            copy.wait_recv()
        for k in range(4):
            rows = slice(k * OWN, k * OWN + OWN)
            total = part_send[head, p.z, rows, :].astype(F32)
            for d in range(3):
                total = total + part_in[head, d, rows, :].astype(F32)
            packed_send[k, :, head * 128 : head * 128 + 128] = total.astype(BF)
    grad_packed[p.y] = packed_send[p.y]
    back_y = [
        w.push(packed_send.at[step4(p.y, d)], grad_packed.at[p.y], p.ydev(d)) for d in (1, 3, 2)
    ]
    for copy in back_y:
        copy.wait_recv()
    for part in parts:
        part.end()
    for copy in to_y + back_y + sum(to_z, []):
        copy.wait_send()


def backward_attention(grad_att, kv, lse, key_place, query_place, g_down, g_first, g_out):
    shapes = []
    for rows, cols in ((48, 768), (48, 768), (48, 768), (48, 768), (48, 384)):
        shapes += scatter_shapes(rows, cols, True, BF)
    return pl.pallas_call(
        backward_kernel,
        out_shape=(
            jax.ShapeDtypeStruct((4, OWN, 640), BF),
            jax.ShapeDtypeStruct((192, 768), F32),
            jax.ShapeDtypeStruct((48, 3072), F32),
            jax.ShapeDtypeStruct((48, 768), F32),
        ),
        in_specs=[VMEM] * 5 + [ANY] * 3,
        out_specs=(VMEM,) * 4,
        scratch_shapes=[
            pltpu.VMEM((GROUP, 512), F32),
            pltpu.VMEM((GROUP, TILE), F32),
            pltpu.VMEM((GROUP, TILE), F32),
            pltpu.VMEM((128, GROUP), BF),
            pltpu.VMEM((4, OWN, 256), BF),
            pltpu.VMEM((GROUP, 128), F32),
            pltpu.VMEM((3, 4, 512, 128), BF),
            pltpu.VMEM((3, 3, 512, 128), BF),
            pltpu.VMEM((256, 512), F32),
            pltpu.VMEM((4, OWN, 640), BF),
        ]
        + shapes
        + sems(5 * SCATTER_SENDS + 15, 5),
        compiler_params=pltpu.CompilerParams(
            collective_id=2, has_side_effects=True, vmem_limit_bytes=52 * MIB
        ),
        name="backward_attention",
    )(
        grad_att, kv, lse, key_place, query_place,
        g_down.reshape(4, 4, 192, 768), g_first.reshape(4, 4, 48, 3072), g_out.reshape(4, 4, 48, 768),
    )


def scatter_last_kernel(g_qkv, g_vec, o_qkv, o_vec, *scratch):
    send_sems, recv_sems, local_sems = scratch[-3:]
    p = Place()
    w = Wire(send_sems, recv_sems, local_sems)
    greet(all_peers(p) + x_peers(p))
    parts = [
        Scatter(w, p, g_qkv, o_qkv, 1, 1152, 0, 640, True, True, scratch[0:6]),
        Scatter(w, p, g_qkv, o_qkv, 1, 1152, 640, 512, False, True, scratch[6:12]),
        Scatter(w, p, g_vec, o_vec, 1, 0, 0, 128, False, False, scratch[12:18]),
    ]
    for stage in (Scatter.p0, Scatter.p1, Scatter.p2, Scatter.p3, Scatter.p4, Scatter.end):
        for part in parts:
            stage(part)


def scatter_last(g_qkv, g_vec):
    shapes = scatter_shapes(48, 640, True, BF) + scatter_shapes(48, 512, True, BF)
    shapes += scatter_shapes(48, 128, False, F32)
    return pl.pallas_call(
        scatter_last_kernel,
        out_shape=(jax.ShapeDtypeStruct((48, 2304), F32), jax.ShapeDtypeStruct((48, 128), F32)),
        in_specs=[ANY] * 2,
        out_specs=(VMEM,) * 2,
        scratch_shapes=shapes + sems(3 * SCATTER_SENDS, 3),
        compiler_params=pltpu.CompilerParams(
            collective_id=3, has_side_effects=True, vmem_limit_bytes=24 * MIB
        ),
        name="scatter_last",
    )(g_qkv.reshape(4, 4, 48, 2304), g_vec.reshape(4, 4, 48, 128))


def layer_norm(inputs, gain, shift):
    average = jnp.mean(inputs, -1, keepdims=True)
    centred = inputs - average
    spread = jnp.mean(centred * centred, -1, keepdims=True)
    return centred * lax.rsqrt(spread + EPS_NORM) * gain + shift


def gelu_tanh(inputs):
    return jax.nn.gelu(inputs, approximate=True)


def adamw(weight, moment, second, grad, rate, decay):
    moment_new = BETA_ONE * moment + (1.0 - BETA_ONE) * grad
    second_new = BETA_TWO * second + (1.0 - BETA_TWO) * grad * grad
    moment_hat = moment_new / (1.0 - BETA_ONE**STEP)
    second_hat = second_new / (1.0 - BETA_TWO**STEP)
    weight_new = weight - rate * (moment_hat / (jnp.sqrt(second_hat) + EPS_ADAM) + decay * weight)
    return (weight_new, moment_new, second_new)


def pack_groups(queries, keys, values):
    blank = jnp.zeros((queries.shape[0], HD), queries.dtype)
    groups = []
    for g in range(4):
        q, k, v = ([a[:, (3 * g + j) * HD : (3 * g + j + 1) * HD] for j in range(3)] for a in (queries, keys, values))
        groups.append(jnp.concatenate([k[0], v[0], v[1], k[1], k[2], v[2], q[0], q[1], q[2], blank], 1))
    return jnp.stack(groups)


def unpack_groups(packed):
    dq, dk, dv = [], [], []
    for g in range(4):
        col = [packed[g][:, j * HD : (j + 1) * HD] for j in range(9)]
        dk += [col[0], col[3], col[4]]
        dv += [col[1], col[2], col[5]]
        dq += [col[6], col[7], col[8]]
    return jnp.concatenate(dq + dk + dv, 1)


def pack_outs(matrix):
    blank = jnp.zeros((matrix.shape[0], HD), matrix.dtype)
    groups = []
    for g in range(4):
        o = [matrix[:, (3 * g + j) * HD : (3 * g + j + 1) * HD] for j in range(3)]
        groups.append(jnp.concatenate([o[1], o[0], blank, o[2]], 1))
    return jnp.stack(groups)


def unpack_outs(packed):
    parts = []
    for g in range(4):
        parts += [packed[g][:, HD : 2 * HD], packed[g][:, :HD], packed[g][:, 3 * HD :]]
    return jnp.concatenate(parts, 1)


def per_device(
    tokens,
    cotangent,
    lengths,
    positions,
    w_rows,
    w_down,
    vectors,
    moment_rows,
    second_rows,
    moment_down,
    second_down,
    moment_vectors,
    second_vectors,
):
    tok_rows, model_dim = tokens.shape
    scale = HD ** (-0.5)
    shard_index = lax.axis_index("shard")
    low_rows = w_rows.astype(BF)
    low_vecs = jnp.pad(vectors.astype(BF).T, ((0, 0), (0, 244)))
    full_qkv = gather_first(jnp.concatenate([low_rows[:, : 3 * model_dim], low_vecs], 1))
    vec_vals = full_qkv[:, 3 * model_dim : 3 * model_dim + 12].T.astype(F32)
    gain_one, shift_one, bias_query, bias_value = (
        vec_vals[0],
        vec_vals[1],
        vec_vals[2],
        vec_vals[3],
    )
    bias_out, gain_two, shift_two, bias_down = (vec_vals[4], vec_vals[5], vec_vals[6], vec_vals[7])
    bias_first = vec_vals[8:].reshape(-1)
    w_query_kv = full_qkv[:, : 3 * model_dim]
    place_all = positions[0]
    seq_ends = jnp.cumsum(lengths[0])
    place_quarter = lax.dynamic_slice_in_dim(place_all, lax.div(shard_index, 4) * 512, 512)
    seq_start = jnp.max(
        jnp.where(place_quarter[None, :] >= seq_ends[:, None], seq_ends[:, None], 0), axis=0
    )
    key_place = place_all[:, None]
    query_place = jnp.pad(jnp.stack([place_quarter, seq_start]), ((0, 6), (0, 0)))
    inputs = tokens.astype(F32)
    normed = layer_norm(inputs, gain_one, shift_one).astype(BF)
    projected = jnp.dot(normed, w_query_kv, preferred_element_type=F32)
    queries = (projected[:, :model_dim] + bias_query).astype(BF)
    key_rows = projected[:, model_dim : 2 * model_dim].astype(BF)
    value_rows = (projected[:, 2 * model_dim :] + bias_value).astype(BF)
    packed = pack_groups(queries * jnp.asarray(scale, BF), key_rows, value_rows)
    full_rest, full_down, kv, attended_packed, lse = forward_attention(
        packed, low_rows[:, 3 * model_dim :], w_down.astype(BF), key_place, query_place
    )
    attended = unpack_outs(attended_packed)
    w_out = full_rest[:, :model_dim]
    w_first = full_rest[:, model_dim:]
    middle = inputs + jnp.dot(attended, w_out, preferred_element_type=F32) + bias_out
    normed_two = layer_norm(middle, gain_two, shift_two).astype(BF)
    pre_act = jnp.dot(normed_two, w_first, preferred_element_type=F32) + bias_first
    hidden = gelu_tanh(pre_act).astype(BF)
    outputs = (
        middle + jnp.dot(hidden, full_down, preferred_element_type=F32) + bias_down
    ).astype(BF)
    grad_out = cotangent.astype(F32)
    grad_down = jnp.einsum("ti,to->io", hidden, cotangent, preferred_element_type=F32).astype(BF)
    grad_bias_down = jnp.sum(grad_out, 0)
    grad_hidden = jnp.einsum("to,io->ti", cotangent, full_down, preferred_element_type=F32)
    gelu_back = jax.vjp(gelu_tanh, pre_act)[1]
    grad_pre = gelu_back(grad_hidden)[0].astype(BF)
    grad_first = jnp.einsum("td,ti->di", normed_two, grad_pre, preferred_element_type=F32).astype(BF)
    grad_bias_first = jnp.sum(grad_pre.astype(F32), 0)
    grad_normed_two = jnp.einsum("ti,di->td", grad_pre, w_first, preferred_element_type=F32)
    norm_two_back = jax.vjp(layer_norm, middle, gain_two, shift_two)[1]
    grad_mid_norm, grad_gain_two, grad_shift_two = norm_two_back(grad_normed_two)
    grad_middle = grad_out + grad_mid_norm
    grad_branch = grad_middle.astype(BF)
    grad_out_proj = jnp.einsum("td,to->do", attended, grad_branch, preferred_element_type=F32).astype(BF)
    grad_bias_out = jnp.sum(grad_branch.astype(F32), 0)
    grad_attended = jnp.einsum("to,do->td", grad_branch, w_out, preferred_element_type=F32).astype(BF)
    grad_packed, sum_down, sum_first, sum_out = backward_attention(
        pack_outs(grad_attended), kv, lse, key_place, query_place, grad_down, grad_first, grad_out_proj
    )
    grad_projected = unpack_groups(grad_packed)
    grad_query_kv = jnp.einsum("td,tj->dj", normed, grad_projected, preferred_element_type=F32).astype(BF)
    grad_bias_query = jnp.sum(grad_projected[:, :model_dim].astype(F32), 0)
    grad_bias_value = jnp.sum(grad_projected[:, 2 * model_dim :].astype(F32), 0)
    grad_normed = jnp.einsum("tj,dj->td", grad_projected, w_query_kv, preferred_element_type=F32)
    norm_one_back = jax.vjp(layer_norm, inputs, gain_one, shift_one)[1]
    grad_in_norm, grad_gain_one, grad_shift_one = norm_one_back(grad_normed)
    grad_input = (grad_middle + grad_in_norm).astype(BF)
    grad_vec_local = jnp.concatenate(
        [
            jnp.stack(
                [
                    grad_gain_one,
                    grad_shift_one,
                    grad_bias_query,
                    grad_bias_value,
                    grad_bias_out,
                    grad_gain_two,
                    grad_shift_two,
                    grad_bias_down,
                ]
            ),
            grad_bias_first.reshape(-1, model_dim),
        ],
        0,
    )
    sum_qkv, sum_vec = scatter_last(grad_query_kv, jnp.pad(grad_vec_local.T, ((0, 0), (0, 116))))
    grad_rows = jnp.concatenate([sum_qkv, sum_out, sum_first], 1)
    rows_new = adamw(w_rows, moment_rows, second_rows, grad_rows, LR_MATRIX, DECAY)
    down_new = adamw(w_down, moment_down, second_down, sum_down, LR_MATRIX, DECAY)
    vec_new = adamw(vectors, moment_vectors, second_vectors, sum_vec[:, :12].T, LR_VECTOR, 0.0)
    return (
        outputs,
        grad_input,
        rows_new[0],
        rows_new[1],
        rows_new[2],
        down_new[0],
        down_new[1],
        down_new[2],
        vec_new[0],
        vec_new[1],
        vec_new[2],
    )


def solution(mesh):
    return jax.shard_map(
        per_device,
        mesh=mesh,
        in_specs=(
            P(("replica", "shard"), None),
            P(("replica", "shard"), None),
            P("replica", None),
            P("replica", None),
            P("shard", None),
            P("shard", None),
            P(None, "shard"),
            P("shard", None),
            P("shard", None),
            P("shard", None),
            P("shard", None),
            P(None, "shard"),
            P(None, "shard"),
        ),
        out_specs=(
            P(("replica", "shard"), None),
            P(("replica", "shard"), None),
            P("shard", None),
            P("shard", None),
            P("shard", None),
            P("shard", None),
            P("shard", None),
            P("shard", None),
            P(None, "shard"),
            P(None, "shard"),
            P(None, "shard"),
        ),
        check_vma=False,
    )
```

time: 712 us -> 289 us (0.41)
  waiting for transfers between devices: 278 us -> 0 us
  Pallas kernels: 0 us -> 216 us
  matrix products: 207 us -> 29.4 us
  blocking collectives: 102 us -> 0 us
  local copies, waits for them, and re-layouts: 69.4 us -> 30.8 us
  other arithmetic: 31.5 us -> 9.86 us
  between operations: 15.6 us -> 1.55 us
    pallas_call x0 -> x4, Pallas kernels: none -> 216 us  [the longest x1 80 us: backward_attention(): pl.pallas_call(backward_kernel, out_shape=(jax.ShapeDtypeStruct((4, OWN,...]
    dot_general x107 -> x11, matrix products: 204 us -> 25.8 us  [the longest x1 3.77 us: per_device(): jnp.einsum('ti,to->io', hidden, cotangent, preferred_element_type=F32)]
    all_gather x4 -> x0, waiting for transfers between devices: 165 us -> none  [the longest x2 57.5 us: sent_together(): whole, at, done = (lax.all_gather(both, axis, axis=dim, tiled=True), 0, [])]
    unnamed x1 -> x0, blocking collectives: 60.8 us -> none
    psum x1 -> x0, waiting for transfers between devices: 57 us -> none  [packed_total(): total = lax.psum(ravelled, axis)]
    reduce_scatter x2 -> x0, waiting for transfers between devices: 56 us -> none  [the longest x1 56 us: per_device(): lax.psum_scatter(grad_rows_local, 'shard', scatter_dimension=0, tiled=True)]
    all_gather x2 -> x0, blocking collectives: 40.8 us -> none  [the longest x1 21.4 us: per_device(): lax.all_gather(low_weights[2], 'shard', axis=1, tiled=True)]
    slice x14 -> x23, local copies, waits for them, and re-layouts: 29 us -> 1.58 us  [the longest x12 0.71 us: unpack_groups(): col = [packed[g][:, j * HD:(j + 1) * HD] for j in range(9)]]
  transfers between devices with their start and end apart: 7 -> 0, of which waited for: 5 -> 0; matrix products, arithmetic and copies ran while one was open for 29% -> 0% of each run, Pallas kernels for 0% -> 0%
where the time goes in v1:
time: 289 us; the launch traced here: 288 us
  Pallas kernels  216 us (75%)
  local copies, waits for them, and re-layouts  30.8 us (11%)
  matrix products  29.4 us (10%)
  other arithmetic  9.86 us (3%)
    pallas_call x1, Pallas kernels, backward_attention(): pl.pallas_call(backward_kernel, out_shape=(jax.ShapeDtypeStruct((4, OWN,...  80 us
    pallas_call x1, Pallas kernels, forward_attention(): pl.pallas_call(forward_kernel, out_shape=(jax.ShapeDtypeStruct((4, 4, row...  72.6 us
    pallas_call x1, Pallas kernels, scatter_last(): pl.pallas_call(scatter_last_kernel, out_shape=(jax.ShapeDtypeStruct((48,...  37.7 us
    pallas_call x1, Pallas kernels, gather_first(): pl.pallas_call(gather_first_kernel, out_shape=jax.ShapeDtypeStruct((4, 4,...  26 us
    unnamed x110, local copies, waits for them, and re-layouts  14.8 us

profile of v1, /device:TPU:1, one launch (start us, length us, event | category | flops | bytes accessed | tf_op | source)
XLA Modules:
  0.0 287.9 jit_solution(10647105017573980200)
XLA Ops:
  0.6 0.7 convert_element_type.82
  1.5 1.3 convert_element_type.81
  2.9 26.0 %gather_first.1 = bf16[4,4,48,2560]{3,2,1,0:T(8,128)(2,1)S(1)} custom-call(bf16[48,2560]{1,0:T(8,128)(2,1)S(1)} %fusion.40.shard), custom_call_target="tpu_custom_call" | custom-call | tf_op jit(solution)/shard_map/gather_first/pallas_call | solution.py:296
  28.8 2.0 copy-done
  31.4 2.7 fusion.82
  35.3 0.4 copy-done.18
  36.5 72.6 %forward_attention.1 = (bf16[4,4,48,3840]{3,2,1,0:T(8,128)(2,1)}, bf16[4,4,192,768]{3,2,1,0:T(8,128)(2,1)S(1)}, bf16[4,4,128,640]{3,2,1,0:T(8,128)(2,1)S(1)}, bf...) custom-call(bf16[4,128,640]{2,1,0:T(8,128)(2,1)S(1)} %pad_maximum_fusion.packed, bf16[48,3840]{1,0:T(8,128)(2,1)S(1)} %slice.504.rest, ...), custom_call_target="tpu_custom_call" | custom-call | tf_op jit(solution)/shard_map/forward_attention/pallas_call | solution.py:447
  109.1 1.5 copy-done.2
  110.6 2.2 copy-done.11
  113.4 1.7 fusion.83
  115.3 3.3 %fusion.4 = f32[128,3072]{1,0:T(8,128)S(1)} fusion(bf16[768,3840]{1,0:T(8,128)(2,1)} %bitcast.89, f32[3072]{0:T(1024)S(1)} %add.186, f32[128,768]{1,0:T(8,128)S(1)} %get-tuple-element.182, f32[768]{0:T(1024)S(1)} %get-tuple-element.86, f32[768]{0:T(1024)S(1)} %get-tuple-element.84, f32[128]{0:T(128)S(1)} %fusion.53, f32[128]{0:T(128)S(1)} %broadcast_multiply_fusion), kind=kOutput, calls=%fused_computation.8 | convolution fusion | flops 604864512 | bytes 6704128 | tf_op jit(solution)/shard_map/dot_general | solution.py:761
  119.1 1.8 fusion.21
  120.9 2.6 convert_reduce_fusion
  123.5 2.3 multiply_reduce_fusion
  126.2 0.5 convolution_convert_fusion.4
  127.1 3.8 %convolution_convert_fusion.2 = bf16[3072,768]{1,0:T(8,128)(2,1)} fusion(bf16[128,768]{1,0:T(8,128)(2,1)S(1)} %copy-done.20, f32[128,3072]{1,0:T(8,128)S(1)} %fusion.4), kind=kOutput, calls=%fused_computation.2 | convolution fusion | flops 609878016 | bytes 6488064 | tf_op jit(solution)/shard_map/ti,to->io/dot_general | solution.py:767
  130.8 3.7 %convolution_convert_fusion.1 = bf16[768,3072]{1,0:T(8,128)(2,1)} fusion(bf16[128,3072]{1,0:T(8,128)(2,1)S(1)} %get-tuple-element.186, f32[128,768]{1,0:T(8,128)S(1)} %get-tuple-element.182, f32[768]{0:T(1024)S(1)} %get-tuple-element.86, f32[768]{0:T(1024)S(1)} %get-tuple-element.84, f32[128]{0:T(128)S(1)} %fusion.53, f32[128]{0:T(128)S(1)} %broadcast_multiply_fusion), kind=kOutput, calls=%fused_computation.1 | convolution fusion | flops 606830592 | bytes 5905408 | tf_op jit(solution)/shard_map/td,ti->di/dot_general | solution.py:772
  134.5 1.5 convolution_convert_fusion.3
  136.0 80.0 %backward_attention.1 = (bf16[4,128,640]{2,1,0:T(8,128)(2,1)}, f32[192,768]{1,0:T(8,128)S(1)}, f32[48,3072]{1,0:T(8,128)S(1)}, f32[48,768]{1,0:T(8,128)S(1)}) custom-call(bf16[4,128,256]{2,1,0:T(8,128)(2,1)S(1)} %pad_maximum_fusion.1.grad_att, bf16[4,4,128,640]{3,2,1,0:T(8,128)(2,1)} %copy-done.2, f32[8,512]{1,0:T(8,128)S(1)} %get-tuple-element.26.lse, ...), custom_call_target="tpu_custom_call" | custom-call | tf_op jit(solution)/shard_map/backward_attention/pallas_call | solution.py:587
  216.1 0.8 copy-done.3
  216.9 0.8 copy-done.5
  217.7 0.7 copy-done.7
  218.4 1.2 slice_bitcast_fusion
  221.2 3.6 %fusion.57 = (f32[768]{0:T(1024)S(1)}, f32[128]{0:T(128)S(1)}, f32[128,768]{1,0:T(8,128)S(1)}) fusion(f32[768]{0:T(1024)S(1)} %get-tuple-element.91, f32[128]{0:T(128)S(1)} %broadcast_multiply_fusion.1, bf16[128,768]{1,0:T(8,128)(2,1)S(1)} %copy-done.13, bf16[128,2304]{1,0:T(8,128)(2,1)S(1)} %concatenate.63, bf16[768,2560]{1,0:T(8,128)(2,1)} %bitcast.70), kind=kOutput, calls=%fused_computation.128 | convolution fusion | flops 453573760 | bytes 4725760 | tf_op jit(solution)/shard_map/tj,dj->td/dot_general | solution.py:789
  225.2 0.9 convert_reduce_fusion.2
  226.1 1.9 convolution_convert_fusion
  228.1 0.6 reshape.153
  228.6 0.6 reshape.154
  229.4 0.6 stack.65
  230.0 1.7 concatenate.65
  231.6 1.0 convert_reduce_fusion.4
  232.6 0.6 stack.66
  233.2 0.6 stack.67
  233.8 1.3 reshape.155
  235.1 1.3 reshape.156
  236.3 0.6 stack.68
  236.9 0.7 reshape.157
  237.6 2.0 concatenate.66
  239.7 1.7 copy.70
  241.4 1.0 pad.14.clone
  242.4 37.7 %scatter_last.1 = (f32[48,2304]{1,0:T(8,128)S(1)}, f32[48,128]{1,0:T(8,128)S(1)}) custom-call(bf16[4,4,48,2304]{3,2,1,0:T(8,128)(2,1)S(1)} %bitcast.71, f32[4,4,48,128]{3,2,1,0:T(8,128)S(1)} %bitcast.72), custom_call_target="tpu_custom_call" | custom-call | tf_op jit(solution)/shard_map/scatter_last/pallas_call | solution.py:639
  280.3 0.5 copy-done.9
  280.8 0.5 copy-done.4
  281.6 2.4 multiply_subtract_fusion
  284.1 1.5 multiply_subtract_fusion.1
  285.9 0.7 copy.66
  286.5 0.7 copy.67
  287.2 0.7 copy.68
  (164 shorter events, 7.1 us)
Async XLA Ops:
  2.8 28.2 %copy-start.13 = (bf16[128,768]{1,0:T(8,128)(2,1)S(1)}, bf16[128,768]{1,0:T(8,128)(2,1)}, u32[]{:S(2)}) copy-start(bf16[128,768]{1,0:T(8,128)(2,1)} %param.13) | copy-start | bytes 589828
  28.8 2.0 copy-start
  31.2 193.9 %copy-start.42 = (f32[128]{0:T(128)}, f32[128]{0:T(128)S(1)}, u32[]{:S(2)}) copy-start(f32[128]{0:T(128)S(1)} %broadcast_multiply_fusion.1) | copy-start | bytes 1540
  31.4 193.7 %copy-start.44 = (f32[128]{0:T(128)}, f32[128]{0:T(128)S(1)}, u32[]{:S(2)}) copy-start(f32[128]{0:T(128)S(1)} %fusion.52) | copy-start | bytes 1540
  34.7 1.1 copy-start.18
  35.0 0.8 copy-start.43
  35.3 0.9 copy-start.47
  36.2 76.7 %copy-start.1 = (s32[2048,1]{1,0:T(8,128)}, s32[2048,1]{1,0:T(8,128)S(1)}, u32[]{:S(2)}) copy-start(s32[2048,1]{1,0:T(8,128)S(1)} %copy.58.key_place) | copy-start | bytes 24580
  109.1 1.5 copy-start.2
  110.6 2.2 copy-start.11
  115.3 3.8 %copy-start.12 = (bf16[4,4,192,768]{3,2,1,0:T(8,128)(2,1)S(1)}, bf16[4,4,192,768]{3,2,1,0:T(8,128)(2,1)}, u32[]{:S(2)}) copy-start(bf16[4,4,192,768]{3,2,1,0:T(8,128)(2,1)} %copy-done.11) | copy-start | bytes 14155780
  119.1 1.8 copy-start.20
  119.1 4.4 %slice-start = ((s8[5898240]{0:T(1024)(128)(4,1)}), s8[4194304]{0:T(1024)(128)(4,1)S(1)}, s32[]{:S(2)}) async-start(s8[5898240]{0:T(1024)(128)(4,1)} %bitcast.90), calls=%async_computation | async-start | bytes 8388608
  120.9 2.6 slice-start.1
  216.1 0.8 copy-start.3
  216.9 0.8 copy-start.5
  217.7 0.7 copy-start.7
  219.6 0.8 copy-start.25
  219.6 0.8 copy-start.27
  219.6 0.8 copy-start.29
  219.7 0.8 copy-start.31
  219.8 6.3 %copy-start.33 = (bf16[128,64]{1,0:T(8,128)(2,1)}, bf16[128,64]{1,0:T(8,128)(2,1)S(1)}, u32[]{:S(2)}) copy-start(bf16[128,64]{1,0:T(8,128)(2,1)S(1)} %get-tuple-element.159) | copy-start | bytes 49156
  219.9 0.6 copy-start.34
  220.0 0.6 copy-start.36
  220.1 0.6 copy-start.37
  220.2 4.5 %copy-start.38 = (bf16[128,128]{1,0:T(8,128)(2,1)}, bf16[128,128]{1,0:T(8,128)(2,1)S(1)}, u32[]{:S(2)}) copy-start(bf16[128,128]{1,0:T(8,128)(2,1)S(1)} %get-tuple-element.153) | copy-start | bytes 98308
  220.3 4.5 %copy-start.39 = (bf16[128,64]{1,0:T(8,128)(2,1)}, bf16[128,64]{1,0:T(8,128)(2,1)S(1)}, u32[]{:S(2)}) copy-start(bf16[128,64]{1,0:T(8,128)(2,1)S(1)} %get-tuple-element.147) | copy-start | bytes 49156
  220.4 4.4 %copy-start.40 = (bf16[128,128]{1,0:T(8,128)(2,1)}, bf16[128,128]{1,0:T(8,128)(2,1)S(1)}, u32[]{:S(2)}) copy-start(bf16[128,128]{1,0:T(8,128)(2,1)S(1)} %get-tuple-element.149) | copy-start | bytes 98308
  221.2 3.6 %copy-start.16 = (bf16[128,2304]{1,0:T(8,128)(2,1)}, bf16[128,2304]{1,0:T(8,128)(2,1)S(1)}, u32[]{:S(2)}) copy-start(bf16[128,2304]{1,0:T(8,128)(2,1)S(1)} %concatenate.63) | copy-start | bytes 1769476
  224.8 1.3 copy-start.14
  224.8 1.3 copy-start.17
  226.1 3.1 %copy-start.26 = (bf16[128,192]{1,0:T(8,128)(2,1)S(1)}, bf16[128,192]{1,0:T(8,128)(2,1)}, u32[]{:S(2)}) copy-start(bf16[128,192]{1,0:T(8,128)(2,1)} %copy-done.25) | copy-start | bytes 147460
  226.1 3.1 %copy-start.28 = (bf16[128,192]{1,0:T(8,128)(2,1)S(1)}, bf16[128,192]{1,0:T(8,128)(2,1)}, u32[]{:S(2)}) copy-start(bf16[128,192]{1,0:T(8,128)(2,1)} %copy-done.27) | copy-start | bytes 147460
  226.1 3.1 %copy-start.30 = (bf16[128,192]{1,0:T(8,128)(2,1)S(1)}, bf16[128,192]{1,0:T(8,128)(2,1)}, u32[]{:S(2)}) copy-start(bf16[128,192]{1,0:T(8,128)(2,1)} %copy-done.29) | copy-start | bytes 147460
  226.1 3.1 %copy-start.32 = (bf16[128,192]{1,0:T(8,128)(2,1)S(1)}, bf16[128,192]{1,0:T(8,128)(2,1)}, u32[]{:S(2)}) copy-start(bf16[128,192]{1,0:T(8,128)(2,1)} %copy-done.31) | copy-start | bytes 147460
  242.4 37.8 %copy-start.8 = (f32[48,768]{1,0:T(8,128)S(1)}, f32[48,768]{1,0:T(8,128)}, u32[]{:S(2)}) copy-start(f32[48,768]{1,0:T(8,128)} %copy-done.7) | copy-start | bytes 442372
  242.4 38.9 %copy-start.21 = (f32[48,6144]{1,0:T(8,128)S(1)}, f32[48,6144]{1,0:T(8,128)}, u32[]{:S(2)}) copy-start(f32[48,6144]{1,0:T(8,128)} %param.20) | copy-start | bytes 3538948
  242.4 38.9 %copy-start.22 = (f32[48,6144]{1,0:T(8,128)S(1)}, f32[48,6144]{1,0:T(8,128)}, u32[]{:S(2)}) copy-start(f32[48,6144]{1,0:T(8,128)} %param.21) | copy-start | bytes 3538948
  280.2 1.1 copy-start.4
  280.2 1.4 copy-start.15
  281.6 2.4 copy-start.6
  281.6 2.4 copy-start.19
  281.6 2.4 copy-start.23
  281.6 2.4 copy-start.24
  284.0 1.5 copy-start.41
  284.0 1.6 copy-start.45
  284.0 1.7 copy-start.46
  284.0 1.8 copy-start.10
  (2 other events, 1.2 us)

commit v2 on v1

--- a/solution.py
+++ b/solution.py
@@ -17,6 +17,7 @@
 NEIGHBOURS = 4
 TILE = 256
 CHUNK = 256
+STEPS = GROUP // CHUNK
 MIB = 1 << 20
 
 EPS_NORM = 1e-05
@@ -47,6 +48,10 @@
         self.c = lax.rem(self.r, 2)
         self.z = lax.div(self.s, 4)
         self.y = lax.rem(self.s, 4)
+        self.u = self.y + self.c * (self.z - self.y)
+        self.v = self.z + self.c * (self.y - self.z)
+        self.u_step = 1 + 3 * self.c
+        self.v_step = 4 - 3 * self.c
 
     def ydev(self, d):
         return (self.r, self.z * 4 + step4(self.y, d))
@@ -56,6 +61,12 @@
 
     def xdev(self, d):
         return (step4(self.x, d) * 2 + self.c, self.s)
+
+    def udev(self, d):
+        return (self.r, step4(self.u, d) * self.u_step + self.v * self.v_step)
+
+    def vdev(self, d):
+        return (self.r, self.u * self.u_step + step4(self.v, d) * self.v_step)
 
     def sibling(self):
         return (self.x * 2 + 1 - self.c, self.s)
@@ -334,10 +345,10 @@
         rows = pl.ds(pl.multiple_of(i * CHUNK, CHUNK), CHUNK)
         keys = key_place[rows, :]
         ok = (keys <= query_place[0:1, :]) & (keys >= query_place[1:2, :])
-        bias[rows, :] = jnp.where(ok, 0.0, HUGE_NEG).astype(F32)
+        bias[rows, :] = jnp.where(ok, 0.0, HUGE_NEG).astype(BF)
         return carry
 
-    lax.fori_loop(0, GROUP // CHUNK, body, 0)
+    lax.fori_loop(0, STEPS, body, 0, unroll=True)
 
 
 def key_chunk(packed, i, head):
@@ -354,7 +365,7 @@
         turned[:, chunk_rows(i)] = key_chunk(packed, i, head).T
         return carry
 
-    lax.fori_loop(0, GROUP // CHUNK, body, 0)
+    lax.fori_loop(0, STEPS, body, 0, unroll=True)
 
 
 def forward_kernel(
@@ -365,9 +376,9 @@
     p = Place()
     w = Wire(send_sems, recv_sems, local_sems)
     greet(all_peers(p))
-    kv[p.z, p.y] = packed[p.y]
+    kv[p.v, p.u] = packed[p.u]
     to_y = [
-        w.push(packed.at[step4(p.y, d)], kv.at[p.z, p.y], p.ydev(d)) for d in (1, 3, 2)
+        w.push(packed.at[step4(p.u, d)], kv.at[p.v, p.u], p.udev(d)) for d in (1, 3, 2)
     ]
     rest_half, down_half = rest.shape[1] // 2, down.shape[0] // 2
     rest_one = 1024
@@ -381,8 +392,8 @@
         part.first()
     for copy in to_y:
         copy.wait_recv()
-    mine = kv.at[p.z, :, :, pl.ds(0, 384)]
-    to_z = [w.push(mine, mine, p.zdev(d)) for d in (1, 3, 2)]
+    mine = kv.at[p.v, :, :, pl.ds(0, 384)]
+    to_z = [w.push(mine, mine, p.vdev(d)) for d in (1, 3, 2)]
     for part in parts:
         part.second()
     fill_bias(key_place, query_place, bias)
@@ -394,15 +405,17 @@
         turn_keys(kv, head, turned)
         for tile in range(2):
             cols = slice(tile * TILE, tile * TILE + TILE)
-            query = kv[p.z, 2 * tile : 2 * tile + 2, :, 384 + head // 2 * 128 : 512 + head // 2 * 128]
+            query = kv[p.v, 2 * tile : 2 * tile + 2, :, 384 + head // 2 * 128 : 512 + head // 2 * 128]
             query = half_lanes(query.reshape(TILE, 128), head == 1)
 
             def score(i, top):
-                part = dot_lanes(key_chunk(kv, i, head), query) + bias[chunk_rows(i), cols]
+                part = dot_lanes(key_chunk(kv, i, head), query) + bias[chunk_rows(i), cols].astype(F32)
                 scores[chunk_rows(i), :] = part
                 return jnp.maximum(top, rows_max(part))
 
-            top = lax.fori_loop(0, GROUP // CHUNK, score, jnp.full((8, TILE), -jnp.inf, F32))
+            top = lax.fori_loop(
+                0, STEPS, score, jnp.full((8, TILE), -jnp.inf, F32), unroll=True
+            )
             top = jnp.max(top, axis=0, keepdims=True)
 
             def mix(i, carry):
@@ -412,7 +425,7 @@
                 return total + rows_sum(raised), acc
 
             total, acc = lax.fori_loop(
-                0, GROUP // CHUNK, mix, (jnp.zeros((8, TILE), F32), jnp.zeros((128, TILE), F32))
+                0, STEPS, mix, (jnp.zeros((8, TILE), F32), jnp.zeros((128, TILE), F32)), unroll=True
             )
             total = jnp.sum(total, axis=0, keepdims=True)
             acc = acc / total
@@ -429,9 +442,9 @@
     for k in range(4):
         turned_out = head_out[:, k * OWN : k * OWN + OWN].T
         out_send[k] = turned_out.astype(BF)
-    attended[p.y] = out_send[p.y]
+    attended[p.u] = out_send[p.u]
     back = [
-        w.push(out_send.at[step4(p.y, d)], attended.at[p.y], p.ydev(d)) for d in (1, 3, 2)
+        w.push(out_send.at[step4(p.u, d)], attended.at[p.u], p.udev(d)) for d in (1, 3, 2)
     ]
     for copy in back:
         copy.wait_recv()
@@ -456,7 +469,7 @@
         in_specs=[VMEM] * 5,
         out_specs=(VMEM, VMEM, VMEM, VMEM, VMEM),
         scratch_shapes=[
-            pltpu.VMEM((GROUP, 512), F32),
+            pltpu.VMEM((GROUP, 512), BF),
             pltpu.VMEM((GROUP, TILE), F32),
             pltpu.VMEM((128, GROUP), BF),
             pltpu.VMEM((256, 512), F32),
@@ -482,9 +495,9 @@
     p = Place()
     w = Wire(send_sems, recv_sems, local_sems)
     greet(all_peers(p) + x_peers(p))
-    dob[p.y] = grad_att[p.y]
+    dob[p.u] = grad_att[p.u]
     to_y = [
-        w.push(grad_att.at[step4(p.y, d)], dob.at[p.y], p.ydev(d)) for d in (1, 3, 2)
+        w.push(grad_att.at[step4(p.u, d)], dob.at[p.u], p.udev(d)) for d in (1, 3, 2)
     ]
     parts = [
         Scatter(w, p, g_down, o_down, 0, 96, 0, 48, True, True, blocks[0:6]),
@@ -512,7 +525,7 @@
         for tile in range(2):
             cols = slice(tile * TILE, tile * TILE + TILE)
             block = head // 2 * 128
-            query = kv[p.z, 2 * tile : 2 * tile + 2, :, 384 + block : 512 + block]
+            query = kv[p.v, 2 * tile : 2 * tile + 2, :, 384 + block : 512 + block]
             query = half_lanes(query.reshape(TILE, 128), head == 1)
             dout = dob[2 * tile : 2 * tile + 2, :, block : block + 128]
             dout = half_lanes(dout.reshape(TILE, 128), head != 1)
@@ -520,13 +533,13 @@
 
             def weigh(i, inner):
                 keys = key_chunk(kv, i, head)
-                prob = jnp.exp(dot_lanes(keys, query) + bias[chunk_rows(i), cols] - total)
+                prob = jnp.exp(dot_lanes(keys, query) + bias[chunk_rows(i), cols].astype(F32) - total)
                 gprob = dot_lanes(keys, dout)
                 probs[chunk_rows(i), :] = prob
                 grad_probs[chunk_rows(i), :] = gprob
                 return inner + rows_sum(prob * gprob)
 
-            inner = lax.fori_loop(0, GROUP // CHUNK, weigh, jnp.zeros((8, TILE), F32))
+            inner = lax.fori_loop(0, STEPS, weigh, jnp.zeros((8, TILE), F32), unroll=True)
             inner = jnp.sum(inner, axis=0, keepdims=True)
 
             def back(i, total_dq):
@@ -541,7 +554,7 @@
                     ).astype(BF)
                 return total_dq + dot_plain(turned[:, chunk_rows(i)], gscore)
 
-            total_dq = lax.fori_loop(0, GROUP // CHUNK, back, jnp.zeros((128, TILE), F32))
+            total_dq = lax.fori_loop(0, STEPS, back, jnp.zeros((128, TILE), F32), unroll=True)
             total_dq = total_dq * (HD ** (-0.5))
             if head == 0:
                 dq[0:64, cols] = total_dq[0:64, :]
@@ -552,7 +565,7 @@
             stages[head * 2 + tile]()
         to_z.append(
             [
-                w.push(part_send.at[head, step4(p.z, d)], part_in.at[head, d - 1], p.zdev(d))
+                w.push(part_send.at[head, step4(p.v, d)], part_in.at[head, d - 1], p.vdev(d))
                 for d in (1, 3, 2)
             ]
         )
@@ -564,13 +577,13 @@
             copy.wait_recv()
         for k in range(4):
             rows = slice(k * OWN, k * OWN + OWN)
-            total = part_send[head, p.z, rows, :].astype(F32)
+            total = part_send[head, p.v, rows, :].astype(F32)
             for d in range(3):
                 total = total + part_in[head, d, rows, :].astype(F32)
             packed_send[k, :, head * 128 : head * 128 + 128] = total.astype(BF)
-    grad_packed[p.y] = packed_send[p.y]
+    grad_packed[p.u] = packed_send[p.u]
     back_y = [
-        w.push(packed_send.at[step4(p.y, d)], grad_packed.at[p.y], p.ydev(d)) for d in (1, 3, 2)
+        w.push(packed_send.at[step4(p.u, d)], grad_packed.at[p.u], p.udev(d)) for d in (1, 3, 2)
     ]
     for copy in back_y:
         copy.wait_recv()
@@ -595,7 +608,7 @@
         in_specs=[VMEM] * 5 + [ANY] * 3,
         out_specs=(VMEM,) * 4,
         scratch_shapes=[
-            pltpu.VMEM((GROUP, 512), F32),
+            pltpu.VMEM((GROUP, 512), BF),
             pltpu.VMEM((GROUP, TILE), F32),
             pltpu.VMEM((GROUP, TILE), F32),
             pltpu.VMEM((128, GROUP), BF),
@@ -735,9 +748,12 @@
     bias_out, gain_two, shift_two, bias_down = (vec_vals[4], vec_vals[5], vec_vals[6], vec_vals[7])
     bias_first = vec_vals[8:].reshape(-1)
     w_query_kv = full_qkv[:, : 3 * model_dim]
-    place_all = positions[0]
+    core = lax.rem(lax.axis_index("replica"), 2)
+    place_blocks = positions.reshape(4, 4, OWN)
+    place_all = jnp.where(core == 0, place_blocks, place_blocks.transpose(1, 0, 2)).reshape(GROUP)
+    own_quarter = jnp.where(core == 0, lax.div(shard_index, 4), lax.rem(shard_index, 4))
     seq_ends = jnp.cumsum(lengths[0])
-    place_quarter = lax.dynamic_slice_in_dim(place_all, lax.div(shard_index, 4) * 512, 512)
+    place_quarter = lax.dynamic_slice_in_dim(place_all, own_quarter * 512, 512)
     seq_start = jnp.max(
         jnp.where(place_quarter[None, :] >= seq_ends[:, None], seq_ends[:, None], 0), axis=0
     )

time: 289 us -> 278 us (0.962)
  Pallas kernels: 216 us -> 202 us
    pallas_call x1, Pallas kernels: 72.6 us -> 61.8 us  [forward_attention(): pl.pallas_call(forward_kernel, out_shape=(jax.ShapeDtypeStruct((4, 4, row...]
    pallas_call x1, Pallas kernels: 80 us -> 74.6 us  [backward_attention(): pl.pallas_call(backward_kernel, out_shape=(jax.ShapeDtypeStruct((4, OWN,...]
where the time goes in v2:
time: 278 us; the launch traced here: 274 us
  Pallas kernels  202 us (73%)
  local copies, waits for them, and re-layouts  30.9 us (11%)
  matrix products  29.6 us (11%)
  other arithmetic  9.86 us (4%)
    pallas_call x1, Pallas kernels, backward_attention(): pl.pallas_call(backward_kernel, out_shape=(jax.ShapeDtypeStruct((4, OWN,...  74.6 us
    pallas_call x1, Pallas kernels, forward_attention(): pl.pallas_call(forward_kernel, out_shape=(jax.ShapeDtypeStruct((4, 4, row...  61.8 us
    pallas_call x1, Pallas kernels, scatter_last(): pl.pallas_call(scatter_last_kernel, out_shape=(jax.ShapeDtypeStruct((48,...  39.5 us
    pallas_call x1, Pallas kernels, gather_first(): pl.pallas_call(gather_first_kernel, out_shape=jax.ShapeDtypeStruct((4, 4,...  26 us
    unnamed x110, local copies, waits for them, and re-layouts  14.8 us

profile of v2, /device:TPU:1, one launch (start us, length us, event | category | flops | bytes accessed | tf_op | source)
XLA Modules:
  0.0 274.2 jit_solution(10866425634362563283)
XLA Ops:
  0.6 0.7 convert_element_type.82
  1.5 1.3 convert_element_type.81
  2.9 26.0 %gather_first.1 = bf16[4,4,48,2560]{3,2,1,0:T(8,128)(2,1)S(1)} custom-call(bf16[48,2560]{1,0:T(8,128)(2,1)S(1)} %fusion.40.shard), custom_call_target="tpu_custom_call" | custom-call | tf_op jit(solution)/shard_map/gather_first/pallas_call | solution.py:307
  28.8 2.0 copy-done
  31.4 2.7 fusion.82
  35.3 0.4 copy-done.18
  36.7 61.8 %forward_attention.1 = (bf16[4,4,48,3840]{3,2,1,0:T(8,128)(2,1)}, bf16[4,4,192,768]{3,2,1,0:T(8,128)(2,1)S(1)}, bf16[4,4,128,640]{3,2,1,0:T(8,128)(2,1)S(1)}, bf...) custom-call(bf16[4,128,640]{2,1,0:T(8,128)(2,1)S(1)} %pad_maximum_fusion.packed, bf16[48,3840]{1,0:T(8,128)(2,1)S(1)} %slice.504.rest, ...), custom_call_target="tpu_custom_call" | custom-call | tf_op jit(solution)/shard_map/forward_attention/pallas_call | solution.py:460
  98.5 1.5 copy-done.2
  100.0 2.2 copy-done.11
  102.7 1.7 fusion.83
  104.7 3.3 %fusion.4 = f32[128,3072]{1,0:T(8,128)S(1)} fusion(bf16[768,3840]{1,0:T(8,128)(2,1)} %bitcast.95, f32[3072]{0:T(1024)S(1)} %add.186, f32[128,768]{1,0:T(8,128)S(1)} %get-tuple-element.182, f32[768]{0:T(1024)S(1)} %get-tuple-element.86, f32[768]{0:T(1024)S(1)} %get-tuple-element.84, f32[128]{0:T(128)S(1)} %fusion.53, f32[128]{0:T(128)S(1)} %broadcast_multiply_fusion), kind=kOutput, calls=%fused_computation.8 | convolution fusion | flops 604864512 | bytes 6704128 | tf_op jit(solution)/shard_map/dot_general | solution.py:777
  108.4 1.8 fusion.21
  110.2 2.6 convert_reduce_fusion
  112.9 2.4 multiply_reduce_fusion
  115.7 0.5 convolution_convert_fusion.4
  116.6 3.8 %convolution_convert_fusion.2 = bf16[3072,768]{1,0:T(8,128)(2,1)} fusion(bf16[128,768]{1,0:T(8,128)(2,1)S(1)} %copy-done.20, f32[128,3072]{1,0:T(8,128)S(1)} %fusion.4), kind=kOutput, calls=%fused_computation.2 | convolution fusion | flops 609878016 | bytes 6488064 | tf_op jit(solution)/shard_map/ti,to->io/dot_general | solution.py:783
  120.4 3.7 %convolution_convert_fusion.1 = bf16[768,3072]{1,0:T(8,128)(2,1)} fusion(bf16[128,3072]{1,0:T(8,128)(2,1)S(1)} %get-tuple-element.186, f32[128,768]{1,0:T(8,128)S(1)} %get-tuple-element.182, f32[768]{0:T(1024)S(1)} %get-tuple-element.86, f32[768]{0:T(1024)S(1)} %get-tuple-element.84, f32[128]{0:T(128)S(1)} %fusion.53, f32[128]{0:T(128)S(1)} %broadcast_multiply_fusion), kind=kOutput, calls=%fused_computation.1 | convolution fusion | flops 606830592 | bytes 5905408 | tf_op jit(solution)/shard_map/td,ti->di/dot_general | solution.py:788
  124.0 1.5 convolution_convert_fusion.3
  125.5 74.6 %backward_attention.1 = (bf16[4,128,640]{2,1,0:T(8,128)(2,1)}, f32[192,768]{1,0:T(8,128)S(1)}, f32[48,3072]{1,0:T(8,128)S(1)}, f32[48,768]{1,0:T(8,128)S(1)}) custom-call(bf16[4,128,256]{2,1,0:T(8,128)(2,1)S(1)} %pad_maximum_fusion.1.grad_att, bf16[4,4,128,640]{3,2,1,0:T(8,128)(2,1)} %copy-done.2, f32[8,512]{1,0:T(8,128)S(1)} %get-tuple-element.26.lse, ...), custom_call_target="tpu_custom_call" | custom-call | tf_op jit(solution)/shard_map/backward_attention/pallas_call | solution.py:600
  200.1 0.8 copy-done.3
  200.9 0.8 copy-done.5
  201.8 0.7 copy-done.7
  202.4 1.2 slice_bitcast_fusion
  205.2 3.6 %fusion.57 = (f32[768]{0:T(1024)S(1)}, f32[128]{0:T(128)S(1)}, f32[128,768]{1,0:T(8,128)S(1)}) fusion(f32[768]{0:T(1024)S(1)} %get-tuple-element.91, f32[128]{0:T(128)S(1)} %broadcast_multiply_fusion.1, bf16[128,768]{1,0:T(8,128)(2,1)S(1)} %copy-done.13, bf16[128,2304]{1,0:T(8,128)(2,1)S(1)} %concatenate.63, bf16[768,2560]{1,0:T(8,128)(2,1)} %bitcast.74), kind=kOutput, calls=%fused_computation.128 | convolution fusion | flops 453573760 | bytes 4725760 | tf_op jit(solution)/shard_map/tj,dj->td/dot_general | solution.py:805
  209.2 0.9 convert_reduce_fusion.2
  210.2 1.9 convolution_convert_fusion
  212.1 0.6 reshape.160
  212.7 0.6 reshape.161
  213.4 0.6 stack.68
  214.0 1.7 concatenate.65
  215.7 1.0 convert_reduce_fusion.4
  216.7 0.6 stack.69
  217.3 0.6 stack.70
  217.8 1.3 reshape.162
  219.1 1.3 reshape.163
  220.4 0.6 stack.71
  221.0 0.7 reshape.164
  221.7 2.0 concatenate.66
  223.7 1.7 copy.74
  225.4 1.0 pad.14.clone
  226.5 39.5 %scatter_last.1 = (f32[48,2304]{1,0:T(8,128)S(1)}, f32[48,128]{1,0:T(8,128)S(1)}) custom-call(bf16[4,4,48,2304]{3,2,1,0:T(8,128)(2,1)S(1)} %bitcast.75, f32[4,4,48,128]{3,2,1,0:T(8,128)S(1)} %bitcast.76), custom_call_target="tpu_custom_call" | custom-call | tf_op jit(solution)/shard_map/scatter_last/pallas_call | solution.py:652
  266.2 0.5 copy-done.9
  266.7 0.5 copy-done.4
  267.5 2.4 multiply_subtract_fusion
  270.0 1.5 multiply_subtract_fusion.1
  271.8 0.7 copy.70
  272.4 0.7 copy.71
  273.1 0.7 copy.72
  (165 shorter events, 7.2 us)
Async XLA Ops:
  2.8 28.2 %copy-start.13 = (bf16[128,768]{1,0:T(8,128)(2,1)S(1)}, bf16[128,768]{1,0:T(8,128)(2,1)}, u32[]{:S(2)}) copy-start(bf16[128,768]{1,0:T(8,128)(2,1)} %param.13) | copy-start | bytes 589828
  28.8 2.0 copy-start
  31.2 178.0 %copy-start.42 = (f32[128]{0:T(128)}, f32[128]{0:T(128)S(1)}, u32[]{:S(2)}) copy-start(f32[128]{0:T(128)S(1)} %broadcast_multiply_fusion.1) | copy-start | bytes 1540
  31.4 177.8 %copy-start.43 = (f32[128]{0:T(128)}, f32[128]{0:T(128)S(1)}, u32[]{:S(2)}) copy-start(f32[128]{0:T(128)S(1)} %fusion.52) | copy-start | bytes 1540
  34.7 1.1 copy-start.18
  35.2 0.7 copy-start.44
  35.3 1.1 copy-start.47
  36.3 66.0 %copy-start.1 = (s32[2048,1]{1,0:T(8,128)}, s32[2048,1]{1,0:T(8,128)S(1)}, u32[]{:S(2)}) copy-start(s32[2048,1]{1,0:T(8,128)S(1)} %copy.62.key_place) | copy-start | bytes 24580
  98.5 1.5 copy-start.2
  100.0 2.2 copy-start.11
  104.7 3.8 %copy-start.12 = (bf16[4,4,192,768]{3,2,1,0:T(8,128)(2,1)S(1)}, bf16[4,4,192,768]{3,2,1,0:T(8,128)(2,1)}, u32[]{:S(2)}) copy-start(bf16[4,4,192,768]{3,2,1,0:T(8,128)(2,1)} %copy-done.11) | copy-start | bytes 14155780
  108.4 1.8 copy-start.20
  108.4 4.4 %slice-start = ((s8[5898240]{0:T(1024)(128)(4,1)}), s8[4194304]{0:T(1024)(128)(4,1)S(1)}, s32[]{:S(2)}) async-start(s8[5898240]{0:T(1024)(128)(4,1)} %bitcast.96), calls=%async_computation | async-start | bytes 8388608
  110.2 2.6 slice-start.1
  200.1 0.8 copy-start.3
  200.9 0.8 copy-start.5
  201.8 0.7 copy-start.7
  203.6 0.8 copy-start.25
  203.7 0.8 copy-start.27
  203.7 0.8 copy-start.29
  203.7 0.8 copy-start.31
  203.8 6.3 %copy-start.33 = (bf16[128,64]{1,0:T(8,128)(2,1)}, bf16[128,64]{1,0:T(8,128)(2,1)S(1)}, u32[]{:S(2)}) copy-start(bf16[128,64]{1,0:T(8,128)(2,1)S(1)} %get-tuple-element.159) | copy-start | bytes 49156
  203.9 0.6 copy-start.34
  204.1 0.6 copy-start.36
  204.2 0.6 copy-start.37
  204.3 4.6 %copy-start.38 = (bf16[128,128]{1,0:T(8,128)(2,1)}, bf16[128,128]{1,0:T(8,128)(2,1)S(1)}, u32[]{:S(2)}) copy-start(bf16[128,128]{1,0:T(8,128)(2,1)S(1)} %get-tuple-element.153) | copy-start | bytes 98308
  204.4 4.5 %copy-start.39 = (bf16[128,64]{1,0:T(8,128)(2,1)}, bf16[128,64]{1,0:T(8,128)(2,1)S(1)}, u32[]{:S(2)}) copy-start(bf16[128,64]{1,0:T(8,128)(2,1)S(1)} %get-tuple-element.147) | copy-start | bytes 49156
  204.5 4.4 %copy-start.40 = (bf16[128,128]{1,0:T(8,128)(2,1)}, bf16[128,128]{1,0:T(8,128)(2,1)S(1)}, u32[]{:S(2)}) copy-start(bf16[128,128]{1,0:T(8,128)(2,1)S(1)} %get-tuple-element.149) | copy-start | bytes 98308
  205.2 3.6 %copy-start.16 = (bf16[128,2304]{1,0:T(8,128)(2,1)}, bf16[128,2304]{1,0:T(8,128)(2,1)S(1)}, u32[]{:S(2)}) copy-start(bf16[128,2304]{1,0:T(8,128)(2,1)S(1)} %concatenate.63) | copy-start | bytes 1769476
  208.9 1.3 copy-start.14
  208.9 1.3 copy-start.17
  210.2 3.1 %copy-start.26 = (bf16[128,192]{1,0:T(8,128)(2,1)S(1)}, bf16[128,192]{1,0:T(8,128)(2,1)}, u32[]{:S(2)}) copy-start(bf16[128,192]{1,0:T(8,128)(2,1)} %copy-done.25) | copy-start | bytes 147460
  210.2 3.1 %copy-start.28 = (bf16[128,192]{1,0:T(8,128)(2,1)S(1)}, bf16[128,192]{1,0:T(8,128)(2,1)}, u32[]{:S(2)}) copy-start(bf16[128,192]{1,0:T(8,128)(2,1)} %copy-done.27) | copy-start | bytes 147460
  210.2 3.1 %copy-start.30 = (bf16[128,192]{1,0:T(8,128)(2,1)S(1)}, bf16[128,192]{1,0:T(8,128)(2,1)}, u32[]{:S(2)}) copy-start(bf16[128,192]{1,0:T(8,128)(2,1)} %copy-done.29) | copy-start | bytes 147460
  210.2 3.1 %copy-start.32 = (bf16[128,192]{1,0:T(8,128)(2,1)S(1)}, bf16[128,192]{1,0:T(8,128)(2,1)}, u32[]{:S(2)}) copy-start(bf16[128,192]{1,0:T(8,128)(2,1)} %copy-done.31) | copy-start | bytes 147460
  226.5 39.7 %copy-start.8 = (f32[48,768]{1,0:T(8,128)S(1)}, f32[48,768]{1,0:T(8,128)}, u32[]{:S(2)}) copy-start(f32[48,768]{1,0:T(8,128)} %copy-done.7) | copy-start | bytes 442372
  226.5 40.7 %copy-start.21 = (f32[48,6144]{1,0:T(8,128)S(1)}, f32[48,6144]{1,0:T(8,128)}, u32[]{:S(2)}) copy-start(f32[48,6144]{1,0:T(8,128)} %param.20) | copy-start | bytes 3538948
  226.5 40.7 %copy-start.22 = (f32[48,6144]{1,0:T(8,128)S(1)}, f32[48,6144]{1,0:T(8,128)}, u32[]{:S(2)}) copy-start(f32[48,6144]{1,0:T(8,128)} %param.21) | copy-start | bytes 3538948
  266.1 1.1 copy-start.4
  266.1 1.4 copy-start.15
  267.5 2.4 copy-start.6
  267.5 2.4 copy-start.19
  267.5 2.4 copy-start.23
  267.5 2.4 copy-start.24
  269.9 1.5 copy-start.41
  269.9 1.6 copy-start.45
  269.9 1.7 copy-start.46
  270.0 1.8 copy-start.10
  (2 other events, 1.2 us)

commit v3 on v2

v3 whole, which is shorter than its diff:
```python
import functools

import jax
import jax.numpy as jnp
from jax import lax
from jax.experimental import pallas as pl
from jax.experimental.pallas import tpu as pltpu
from jax.sharding import PartitionSpec as P

H = 12
HD = 64
STEP = 10
D = 768
FF = 3072
OWN = 128
GROUP = 2048
NEIGHBOURS = 4
TILE = 256
CHUNK = 256
STEPS = GROUP // CHUNK
MIB = 1 << 20

EPS_NORM = 1e-05
BETA_ONE = 0.9
BETA_TWO = 0.95
EPS_ADAM = 1e-08
LR_MATRIX = 0.02
LR_VECTOR = 0.3
DECAY = 0.1
HUGE_NEG = -1e30

BF = jnp.bfloat16
F32 = jnp.float32
MESH = pl.DeviceIdType.MESH
VMEM = pl.BlockSpec(memory_space=pltpu.VMEM)
ANY = pl.BlockSpec(memory_space=pl.ANY)


def step4(i, d):
    return lax.rem(i + d, 4)


class Place:
    def __init__(self):
        self.r = lax.axis_index("replica")
        self.s = lax.axis_index("shard")
        self.x = lax.div(self.r, 2)
        self.c = lax.rem(self.r, 2)
        self.z = lax.div(self.s, 4)
        self.y = lax.rem(self.s, 4)
        self.u = self.y + self.c * (self.z - self.y)
        self.v = self.z + self.c * (self.y - self.z)
        self.u_step = 1 + 3 * self.c
        self.v_step = 4 - 3 * self.c

    def ydev(self, d):
        return (self.r, self.z * 4 + step4(self.y, d))

    def zdev(self, d):
        return (self.r, step4(self.z, d) * 4 + self.y)

    def xdev(self, d):
        return (step4(self.x, d) * 2 + self.c, self.s)

    def udev(self, d):
        return (self.r, step4(self.u, d) * self.u_step + self.v * self.v_step)

    def vdev(self, d):
        return (self.r, self.u * self.u_step + step4(self.v, d) * self.v_step)

    def sibling(self):
        return (self.x * 2 + 1 - self.c, self.s)


def greet(devices):
    barrier = pltpu.get_barrier_semaphore()
    for device in devices:
        pl.semaphore_signal(barrier, inc=1, device_id=device, device_id_type=MESH)
    pl.semaphore_wait(barrier, len(devices))


class Wire:
    def __init__(self, send_sems, recv_sems, local_sems):
        self.send_sems, self.recv_sems, self.local_sems = send_sems, recv_sems, local_sems
        self.sent, self.moved = 0, 0

    def push(self, src, dst, device):
        k = self.sent
        self.sent += 1
        copy = pltpu.make_async_remote_copy(
            src_ref=src,
            dst_ref=dst,
            send_sem=self.send_sems.at[k],
            recv_sem=self.recv_sems.at[k],
            device_id=device,
            device_id_type=MESH,
        )
        copy.start()
        return copy

    def local(self, src, dst):
        k = self.moved
        self.moved += 1
        copy = pltpu.make_async_copy(src, dst, self.local_sems.at[k])
        copy.start()
        return copy


def sems(remote, local):
    return [
        pltpu.SemaphoreType.DMA((remote,)),
        pltpu.SemaphoreType.DMA((remote,)),
        pltpu.SemaphoreType.DMA((max(local, 1),)),
    ]


def region(row, rows, col, cols):
    row_cut = slice(None) if rows is None else pl.ds(row, rows)
    col_cut = slice(None) if cols is None else pl.ds(pl.multiple_of(col, 128), cols)
    return (row_cut, col_cut)


class Gather:
    def __init__(self, wire, place, shard, full, cut, y_first):
        self.wire, self.place, self.shard, self.full, self.cut = wire, place, shard, full, cut
        self.y_first = y_first
        self.near = place.ydev if y_first else place.zdev
        self.far = place.zdev if y_first else place.ydev
        self.sends = []

    def push(self, src, dst, device):
        copy = self.wire.push(src, dst, device)
        self.sends.append(copy)
        return copy

    def slab(self, d, blocks=slice(None)):
        p = self.place
        if self.y_first:
            return self.full.at[(step4(p.z, 4 - d), blocks) + self.cut]
        return self.full.at[(blocks, step4(p.y, 4 - d)) + self.cut]

    def first(self):
        p = self.place
        src = self.shard.at[self.cut]
        dst = self.full.at[(p.z, p.y) + self.cut]
        self.own = self.wire.local(src, dst)
        self.one = [self.push(src, dst, self.near(d)) for d in (1, 3, 2)]

    def second(self):
        self.own.wait()
        for copy in self.one:
            copy.wait_recv()
        slab = self.slab(0)
        self.two = [self.push(slab, slab, self.far(d)) for d in (1, 3)]
        self.across = [self.push(slab, slab, self.place.sibling())]

    def third(self):
        self.two[0].wait_recv()
        half = self.slab(1, pl.ds(0, 2))
        self.three = [self.push(half, half, self.far(1))]
        self.two[1].wait_recv()
        half = self.slab(3, pl.ds(2, 2))
        self.three.append(self.push(half, half, self.far(3)))
        for d in (1, 3):
            slab = self.slab(d)
            self.across.append(self.push(slab, slab, self.place.sibling()))

    def fourth(self):
        for copy in self.three:
            copy.wait_recv()
        slab = self.slab(2)
        self.across.append(self.push(slab, slab, self.place.sibling()))

    def end(self):
        for copy in self.across:
            copy.wait_recv()
        for copy in self.sends:
            copy.wait_send()


GATHER_SENDS = 11


def scatter_shapes(rows, cols, dtype):
    return [
        pltpu.VMEM((4, 4, rows, cols), dtype),
        pltpu.VMEM((3, 4, rows, cols), dtype),
        pltpu.VMEM((4, rows, cols), dtype),
        pltpu.VMEM((3, rows, cols), dtype),
        pltpu.VMEM((4, rows, cols), dtype),
    ]


class Scatter:
    def __init__(self, wire, place, grad, out, mine, other, z_first, shared, scratch):
        self.wire, self.place, self.grad, self.out = wire, place, grad, out
        self.shared, self.z_first = shared, z_first
        self.mine, self.other = mine, other
        self.in0, self.in1, self.part, self.in2, self.in3 = scratch
        self.sends, self.wait = [], []

    def push(self, src, dst, device):
        copy = self.wire.push(src, dst, device)
        self.sends.append(copy)
        return copy

    def p0(self):
        every = (slice(None), slice(None))
        self.wait.append(self.push(self.grad.at[every + self.other], self.in0, self.place.sibling()))

    def p0_slab(self, i):
        here = self.grad.at[(i, slice(None)) + self.other]
        self.wait.append(self.push(here, self.in0.at[i], self.place.sibling()))

    def p1(self):
        p = self.place
        for copy in self.wait:
            copy.wait_recv()
        if not self.shared:
            for copy in self.sends:
                copy.wait_send()
            self.sends = []

        def add(i, carry):
            at = (lax.div(i, 4), lax.rem(i, 4))
            both = self.grad[at + self.mine].astype(F32) + self.in0[at].astype(F32)
            self.grad[at + self.mine] = both.astype(self.grad.dtype)
            return carry

        lax.fori_loop(0, 16, add, 0)
        self.wait = []
        for d in (1, 3, 2):
            if self.z_first:
                src, device = self.grad.at[(step4(p.z, d), slice(None)) + self.mine], p.zdev(d)
            else:
                src, device = self.grad.at[(slice(None), step4(p.y, d)) + self.mine], p.ydev(d)
            self.wait.append(self.push(src, self.in1.at[d - 1], device))

    def p2(self):
        p = self.place
        for copy in self.wait:
            copy.wait_recv()

        def add(i, carry):
            at = (p.z, i) if self.z_first else (i, p.y)
            total = self.grad[at + self.mine].astype(F32)
            for k in range(3):
                total = total + self.in1[k, i].astype(F32)
            self.part[i] = total.astype(self.part.dtype)
            return carry

        lax.fori_loop(0, 4, add, 0)
        self.wait = []
        for d in (1, 3, 2):
            if self.z_first:
                src, device = self.part.at[step4(p.y, d)], p.ydev(d)
            else:
                src, device = self.part.at[step4(p.z, d)], p.zdev(d)
            self.wait.append(self.push(src, self.in2.at[d - 1], device))

    def p3(self):
        p = self.place
        for copy in self.wait:
            copy.wait_recv()
        total = self.part[p.y if self.z_first else p.z].astype(F32)
        for k in range(3):
            total = total + self.in2[k].astype(F32)
        self.in3[p.x] = total.astype(self.in3.dtype)
        self.wait = [self.push(self.in3.at[p.x], self.in3.at[p.x], p.xdev(d)) for d in (1, 3, 2)]

    def p4(self):
        for copy in self.wait:
            copy.wait_recv()
        total = self.in3[0].astype(F32)
        for k in range(1, 4):
            total = total + self.in3[k].astype(F32)
        self.out[self.mine] = total
        self.wait = []
        if self.shared:
            here = self.out.at[self.mine]
            self.wait = [self.push(here, here, self.place.sibling())]

    def end(self):
        for copy in self.wait:
            copy.wait_recv()
        for copy in self.sends:
            copy.wait_send()


SCATTER_SENDS = 14


def all_peers(p):
    rings = [p.ydev(d) for d in (1, 2, 3)] + [p.zdev(d) for d in (1, 2, 3)]
    return rings + [p.sibling()]


def x_peers(p):
    return [p.xdev(d) for d in (1, 2, 3)]


def owner(p, u, v):
    return v * p.v_step + u * p.u_step


def first_kernel(x, w_qkv, vec, x_all, w_all, vec_all, send_sems, recv_sems, local_sems):
    p = Place()
    w = Wire(send_sems, recv_sems, local_sems)
    greet(all_peers(p))
    one = [(d, w.push(w_qkv.at[step4(p.u, d)], w_all.at[p.s], p.udev(d))) for d in (1, 3, 2)]
    vec_one = [w.push(vec, vec_all.at[p.s], p.ydev(d)) for d in (1, 3, 2)]
    w_all[p.s] = w_qkv[p.u]
    vec_all[p.s] = vec[...]
    two = [w.push(w_all.at[p.s], w_all.at[p.s], p.vdev(e)) for e in (1, 3, 2)]
    rows = [w.push(x, x_all.at[p.u], p.udev(d)) for d in (1, 3, 2)]
    x_all[p.u] = x[...]
    for d, copy in one:
        copy.wait_recv()
        block = w_all.at[owner(p, step4(p.u, 4 - d), p.v)]
        two += [w.push(block, block, p.vdev(e)) for e in (1, 3, 2)]
    for copy in vec_one:
        copy.wait_recv()
    slab = vec_all.at[pl.ds(p.z * 4, 4)]
    vec_two = [w.push(slab, slab, p.zdev(d)) for d in (1, 3, 2)]
    for copy in two + rows + vec_two:
        copy.wait_recv()
    for copy in [c for _, c in one] + vec_one + two + rows + vec_two:
        copy.wait_send()


def gather_first(x, w_qkv, vec):
    return pl.pallas_call(
        first_kernel,
        out_shape=(
            jax.ShapeDtypeStruct((4, OWN, D), BF),
            jax.ShapeDtypeStruct((16, 48, 640), BF),
            jax.ShapeDtypeStruct((16, 16, 128), BF),
        ),
        in_specs=[VMEM] * 3,
        out_specs=(VMEM,) * 3,
        scratch_shapes=sems(24, 1),
        compiler_params=pltpu.CompilerParams(
            collective_id=0, has_side_effects=True, vmem_limit_bytes=20 * MIB
        ),
        name="gather_first",
    )(x, w_qkv, vec)

def half_lanes(value, right):
    lane = lax.broadcasted_iota(jnp.int32, value.shape, 1)
    keep = lane >= HD if right else lane < HD
    return jnp.where(keep, value, jnp.zeros_like(value))


def rows_max(value):
    return jnp.max(value.reshape(-1, 8, value.shape[1]), axis=0)


def rows_sum(value):
    return jnp.sum(value.reshape(-1, 8, value.shape[1]), axis=0)


def dot_lanes(left, right):
    return lax.dot_general(left, right, (((1,), (1,)), ((), ())), preferred_element_type=F32)


def dot_plain(left, right):
    return jnp.dot(left, right, preferred_element_type=F32)


def fill_bias(key_place, query_place, bias):
    def body(i, carry):
        rows = pl.ds(pl.multiple_of(i * CHUNK, CHUNK), CHUNK)
        keys = key_place[rows, :]
        ok = (keys <= query_place[0:1, :]) & (keys >= query_place[1:2, :])
        bias[rows, :] = jnp.where(ok, 0.0, HUGE_NEG).astype(BF)
        return carry

    lax.fori_loop(0, STEPS, body, 0, unroll=True)


def key_chunk(kv, i, head):
    a, b = lax.div(i, 2), lax.rem(i, 2) * CHUNK
    return kv[a, pl.ds(pl.multiple_of(b, CHUNK), CHUNK), head * 128 : head * 128 + 128]


def chunk_rows(i):
    return pl.ds(pl.multiple_of(i * CHUNK, CHUNK), CHUNK)


def turn_keys(kv, head, turned):
    def body(i, carry):
        turned[head, :, chunk_rows(i)] = key_chunk(kv, i, head).T
        return carry

    lax.fori_loop(0, STEPS, body, 0, unroll=True)


def query_tile(kv, p, head, tile):
    block = 384 + head // 2 * 128
    return half_lanes(kv[p.v, tile * TILE : tile * TILE + TILE, block : block + 128], head != 1)


def attend(kv, p, head, tile, bias, scores, turned, head_out, lse):
    cols = slice(tile * TILE, tile * TILE + TILE)
    query = query_tile(kv, p, head, tile)

    def score(i, top):
        part = dot_lanes(key_chunk(kv, i, head), query) + bias[chunk_rows(i), cols].astype(F32)
        scores[chunk_rows(i), :] = part
        return jnp.maximum(top, rows_max(part))

    top = lax.fori_loop(0, STEPS, score, jnp.full((8, TILE), -jnp.inf, F32), unroll=True)
    top = jnp.max(top, axis=0, keepdims=True)

    def mix(i, carry):
        total, acc = carry
        raised = jnp.exp(scores[chunk_rows(i), :] - top)
        acc = acc + dot_plain(turned[head, :, chunk_rows(i)], raised.astype(BF))
        return total + rows_sum(raised), acc

    total, acc = lax.fori_loop(
        0, STEPS, mix, (jnp.zeros((8, TILE), F32), jnp.zeros((128, TILE), F32)), unroll=True
    )
    total = jnp.sum(total, axis=0, keepdims=True)
    acc = acc / total
    at = 64 if head == 1 else 0
    head_out[head * 64 : head * 64 + 64, cols] = acc[at : at + 64, :]
    lse[head : head + 1, cols] = top + jnp.log(total)


def attend_back(kv, p, head, tile, bias, probs, grad_probs, turned, dob, lse, acc, part_send, dq):
    cols = slice(tile * TILE, tile * TILE + TILE)
    query = query_tile(kv, p, head, tile)
    block = head // 2 * 128
    dout = dob[2 * tile : 2 * tile + 2, :, block : block + 128]
    dout = half_lanes(dout.reshape(TILE, 128), head == 1)
    total = lse[head : head + 1, cols]

    def weigh(i, inner):
        keys = key_chunk(kv, i, head)
        prob = jnp.exp(dot_lanes(keys, query) + bias[chunk_rows(i), cols].astype(F32) - total)
        gprob = dot_lanes(keys, dout)
        probs[chunk_rows(i), :] = prob
        grad_probs[chunk_rows(i), :] = gprob
        return inner + rows_sum(prob * gprob)

    inner = lax.fori_loop(0, STEPS, weigh, jnp.zeros((8, TILE), F32), unroll=True)
    inner = jnp.sum(inner, axis=0, keepdims=True)

    def back(i, total_dq):
        prob = probs[chunk_rows(i), :]
        gscore = (prob * (grad_probs[chunk_rows(i), :] - inner)).astype(BF)
        both = dot_plain(gscore, query) + dot_plain(prob.astype(BF), dout)
        if tile == 0:
            acc[chunk_rows(i), :] = both
        else:
            rows = pl.ds(pl.multiple_of(lax.rem(i, 2) * CHUNK, CHUNK), CHUNK)
            part_send[head, lax.div(i, 2), rows, :] = (acc[chunk_rows(i), :] + both).astype(BF)
        return total_dq + dot_plain(turned[head, :, chunk_rows(i)], gscore)

    total_dq = lax.fori_loop(0, STEPS, back, jnp.zeros((128, TILE), F32), unroll=True)
    total_dq = total_dq * (HD ** (-0.5))
    at = 0 if head == 1 else 64
    row = (64, 0, 192)[head]
    dq[row : row + 64, cols] = total_dq[at : at + 64, :]


def col_sum(value):
    return jnp.sum(value, axis=0, keepdims=True)


def normalise(value):
    average = jnp.mean(value, -1, keepdims=True)
    centred = value - average
    spread = jnp.mean(centred * centred, -1, keepdims=True)
    inverse = lax.rsqrt(spread + EPS_NORM)
    return centred * inverse, inverse


def normalise_back(grad, unit, inverse, gain):
    g = grad * gain
    return inverse * (
        g - jnp.mean(g, -1, keepdims=True) - unit * jnp.mean(g * unit, -1, keepdims=True)
    )


GELU_A = 0.7978845608028654
GELU_B = 0.044715


def out_rows(full_rest, g):
    own = full_rest[g, :, :, 0:D].reshape(192, D)
    return jnp.concatenate([own, jnp.zeros((64, D), BF)], 0)


def layer_kernel(
    packed, x, cot, rest, down, key_place, query_place, vecs, bias_first,
    grad_packed, outputs, grad_middle, grad_vecs, o_down, o_first, o_out, *scratch,
):
    (
        full_rest, full_down, kv, bias, probs, grad_probs, turned, head_out, out_send, attended, lse,
        g_down, g_first, g_out, grad_send, dob, acc, part_send, part_in, dq, total_out, total_dc, low,
    ) = scratch[:23]
    blocks = scratch[23:-3]
    p = Place()
    w = Wire(*scratch[-3:])
    greet(all_peers(p) + x_peers(p))

    kv[p.v] = packed[...]
    mine = kv.at[p.v, :, pl.ds(0, 384)]
    to_v = [w.push(mine, mine, p.vdev(d)) for d in (1, 3, 2)]
    half = p.c * 1920
    parts = [
        Gather(w, p, rest, full_rest, region(0, None, half, 1024), True),
        Gather(w, p, rest, full_rest, region(0, None, half + 1024, 896), False),
        Gather(w, p, down, full_down, region(pl.multiple_of(p.c * 96, 16), 48, 0, None), True),
        Gather(w, p, down, full_down, region(pl.multiple_of(p.c * 96 + 48, 16), 48, 0, None), False),
    ]
    for part in parts:
        part.first()
    fill_bias(key_place, query_place, bias)
    for part in parts:
        part.second()
    for copy in to_v:
        copy.wait_recv()
    head_out[192:256, :] = jnp.zeros((64, 512), F32)
    for head in range(3):
        turn_keys(kv, head, turned)
        for tile in range(2):
            attend(kv, p, head, tile, bias, probs, turned, head_out, lse)
        if head == 1:
            for part in parts[:2]:
                part.third()
    for k in range(4):
        out_send[k] = head_out[:, k * OWN : k * OWN + OWN].T.astype(BF)
    attended[p.u] = out_send[p.u]
    out_back = [w.push(out_send.at[step4(p.u, d)], attended.at[p.u], p.udev(d)) for d in (1, 3, 2)]
    for part in parts[2:]:
        part.third()
    for part in parts:
        part.fourth()
    for copy in out_back:
        copy.wait_recv()
    for part in parts:
        part.end()
    for copy in to_v + out_back:
        copy.wait_send()

    grad_y = cot[...].astype(F32)
    middle = x[...].astype(F32) + vecs[4:5, :]
    for g in range(4):
        middle = middle + dot_plain(attended[g], out_rows(full_rest, g))
    unit, inverse = normalise(middle)
    low[0] = (unit * vecs[5:6, :] + vecs[6:7, :]).astype(BF)
    total_out[...] = middle + vecs[7:8, :]
    total_dc[...] = jnp.zeros((OWN, D), F32)
    low_turned = low[0].T

    def first_part(i):
        at = i * D + p.c * 384
        to = i * D + (1 - p.c) * 384
        return Scatter(
            w, p, g_first, o_first, region(0, None, at, 384), region(0, None, to, 384),
            i % 2 == 0, True, blocks[5 * i : 5 * i + 5],
        )

    firsts = [first_part(i) for i in range(4)]
    at, to = p.c * 384, (1 - p.c) * 384
    downs = [
        Scatter(w, p, g_down, o_down, region(0, 96, at, 384), region(0, 96, to, 384), True, True, blocks[20:25]),
        Scatter(w, p, g_down, o_down, region(96, 96, at, 384), region(96, 96, to, 384), False, True, blocks[25:30]),
    ]
    outs = [
        Scatter(w, p, g_out, o_out, region(0, None, at, 384), region(0, None, to, 384), False, True, blocks[30:35])
    ]
    for i in range(4):
        w_first = full_rest[:, :, :, D + i * D : 2 * D + i * D].reshape(D, D)
        w_down = full_down[i].reshape(D, D)
        act = dot_plain(low[0], w_first) + bias_first[i : i + 1, :]
        square = act * act
        bent = jnp.tanh(GELU_A * (act + GELU_B * act * square))
        hidden = (0.5 * act * (1.0 + bent)).astype(BF)
        slope = 0.5 * (1.0 + bent) + 0.5 * act * (1.0 - bent * bent) * (
            GELU_A * (1.0 + 3.0 * GELU_B * square)
        )
        g_down[i] = dot_plain(hidden.T, cot[...]).astype(BF).reshape(4, 192, D)
        for part in downs:
            part.p0_slab(i)
        grad_act = (dot_lanes(cot[...], w_down) * slope).astype(BF)
        grad_vecs[8 + i : 9 + i, :] = col_sum(grad_act.astype(F32))
        g_first[:, :, :, i * D : i * D + D] = (
            dot_plain(low_turned, grad_act).astype(BF).reshape(4, 4, 48, D)
        )
        firsts[i].p0()
        total_dc[...] += dot_lanes(grad_act, w_first)
        total_out[...] += dot_plain(hidden, w_down)
        if i > 0:
            firsts[i - 1].p1()
    outputs[...] = total_out[...].astype(BF)

    grad_c = total_dc[...]
    grad_m = grad_y + normalise_back(grad_c, unit, inverse, vecs[5:6, :])
    grad_middle[...] = grad_m
    low[1] = grad_m.astype(BF)
    for g in range(4):
        grad_send[g] = dot_lanes(low[1], out_rows(full_rest, g)).astype(BF)
    dob[p.u] = grad_send[p.u]
    to_u = [w.push(grad_send.at[step4(p.u, d)], dob.at[p.u], p.udev(d)) for d in (1, 3, 2)]
    for g in range(4):
        g_out[g] = dot_plain(attended[g].T, low[1])[0:192, :].astype(BF).reshape(4, 48, D)
    outs[0].p0()
    grad_vecs[0:4, :] = jnp.zeros((4, D), F32)
    grad_vecs[4:5, :] = col_sum(low[1].astype(F32))
    grad_vecs[5:6, :] = col_sum(grad_c * unit)
    grad_vecs[6:7, :] = col_sum(grad_c)
    grad_vecs[7:8, :] = col_sum(grad_y)
    grad_vecs[12:16, :] = jnp.zeros((4, D), F32)
    for copy in to_u:
        copy.wait_recv()

    stages = [
        lambda: [part.p1() for part in firsts[3:] + downs],
        lambda: [part.p2() for part in firsts[:2]] + [outs[0].p1()],
        lambda: [part.p2() for part in firsts[2:]] + [part.p3() for part in firsts[:2]],
        lambda: [part.p2() for part in downs],
        lambda: [part.p3() for part in firsts[2:]] + [outs[0].p2()] + [part.p4() for part in firsts[:2]],
        lambda: [part.p3() for part in downs + outs],
    ]
    to_v_back = []
    for head in range(3):
        for tile in range(2):
            attend_back(
                kv, p, head, tile, bias, probs, grad_probs, turned, dob, lse, acc, part_send, dq
            )
            if tile == 1:
                to_v_back.append(
                    [
                        w.push(part_send.at[head, step4(p.v, d)], part_in.at[head, d - 1], p.vdev(d))
                        for d in (1, 3, 2)
                    ]
                )
            stages[head * 2 + tile]()
    dq[128:192, :] = jnp.zeros((64, 512), F32)
    for k in range(4):
        rows = slice(k * OWN, k * OWN + OWN)
        grad_packed[rows, 384:640] = dq[:, rows].T.astype(BF)
    for head in range(3):
        for copy in to_v_back[head]:
            copy.wait_recv()
        for k in range(4):
            rows = slice(k * OWN, k * OWN + OWN)
            total = part_send[head, p.v, rows, :].astype(F32)
            for d in range(3):
                total = total + part_in[head, d, rows, :].astype(F32)
            grad_packed[rows, head * 128 : head * 128 + 128] = total.astype(BF)
    for part in firsts[2:] + downs + outs:
        part.p4()
    for part in firsts + downs + outs:
        part.end()
    for copy in to_u + sum(to_v_back, []):
        copy.wait_send()


def layer(packed, x, cot, rest, down, key_place, query_place, vecs, bias_first):
    shapes = [
        pltpu.VMEM((4, 4, 48, 5 * D), BF),
        pltpu.VMEM((4, 4, 192, D), BF),
        pltpu.VMEM((4, 512, 640), BF),
        pltpu.VMEM((GROUP, 512), BF),
        pltpu.VMEM((GROUP, TILE), F32),
        pltpu.VMEM((GROUP, TILE), F32),
        pltpu.VMEM((3, 128, GROUP), BF),
        pltpu.VMEM((256, 512), F32),
        pltpu.VMEM((4, OWN, 256), BF),
        pltpu.VMEM((4, OWN, 256), BF),
        pltpu.VMEM((8, 512), F32),
        pltpu.VMEM((4, 4, 192, D), BF),
        pltpu.VMEM((4, 4, 48, FF), BF),
        pltpu.VMEM((4, 4, 48, D), BF),
        pltpu.VMEM((4, OWN, 256), BF),
        pltpu.VMEM((4, OWN, 256), BF),
        pltpu.VMEM((GROUP, 128), F32),
        pltpu.VMEM((3, 4, 512, 128), BF),
        pltpu.VMEM((3, 3, 512, 128), BF),
        pltpu.VMEM((256, 512), F32),
        pltpu.VMEM((OWN, D), F32),
        pltpu.VMEM((OWN, D), F32),
        pltpu.VMEM((2, OWN, D), BF),
    ]
    for rows in (48, 48, 48, 48, 96, 96, 48):
        shapes += scatter_shapes(rows, 384, BF)
    return pl.pallas_call(
        layer_kernel,
        out_shape=(
            jax.ShapeDtypeStruct((512, 640), BF),
            jax.ShapeDtypeStruct((OWN, D), BF),
            jax.ShapeDtypeStruct((OWN, D), F32),
            jax.ShapeDtypeStruct((16, D), F32),
            jax.ShapeDtypeStruct((192, D), F32),
            jax.ShapeDtypeStruct((48, FF), F32),
            jax.ShapeDtypeStruct((48, D), F32),
        ),
        in_specs=[VMEM] * 9,
        out_specs=(VMEM,) * 7,
        scratch_shapes=shapes + sems(4 * GATHER_SENDS + 7 * SCATTER_SENDS + 18, 4),
        compiler_params=pltpu.CompilerParams(
            collective_id=1, has_side_effects=True, vmem_limit_bytes=60 * MIB
        ),
        name="layer",
    )(packed, x, cot, rest, down, key_place, query_place, vecs, bias_first)


def last_kernel(grad_a, g_qkv, g_vec, o_a, o_qkv, o_vec, *scratch):
    in_a, in1, part, in2, in0, held, in3 = scratch[:7]
    vec_blocks = scratch[7:12]
    p = Place()
    w = Wire(*scratch[-3:])
    greet(all_peers(p) + x_peers(p))
    vec = Scatter(
        w, p, g_vec, o_vec, (slice(None), slice(None)), (slice(None), slice(None)), False, False, vec_blocks
    )
    one = []
    for d in (1, 3, 2):
        for k in range(4):
            src = g_qkv.at[owner(p, k, step4(p.v, d))]
            one.append(w.push(src, in1.at[d - 1, k], p.vdev(d)))
    rows = [w.push(grad_a.at[step4(p.u, d)], in_a.at[d - 1], p.udev(d)) for d in (1, 3, 2)]
    vec.p0()
    for copy in one:
        copy.wait_recv()
    for k in range(4):
        total = g_qkv[owner(p, k, p.v)].astype(F32)
        for d in range(3):
            total = total + in1[d, k].astype(F32)
        part[k] = total.astype(BF)
    two = [w.push(part.at[step4(p.u, d)], in2.at[p.u], p.udev(d)) for d in (1, 3, 2)]
    in2[p.u] = part[p.u]
    vec.p1()
    for copy in two:
        copy.wait_recv()
    other = in2.at[pl.ds((1 - p.c) * 2, 2)]
    three = [w.push(other, in0, p.sibling())]
    vec.p2()
    three[0].wait_recv()
    for k in range(2):
        held[k] = (in2[p.c * 2 + k].astype(F32) + in0[k].astype(F32)).astype(BF)
    in3[p.x] = held[...]
    four = [w.push(held, in3.at[p.x], p.xdev(d)) for d in (1, 3, 2)]
    for copy in rows:
        copy.wait_recv()
    total = grad_a[p.u].astype(F32)
    for d in range(3):
        total = total + in_a[d].astype(F32)
    o_a[...] = total
    vec.p3()
    for copy in four:
        copy.wait_recv()
    for k in range(2):
        total = in3[0, k].astype(F32)
        for d in range(1, 4):
            total = total + in3[d, k].astype(F32)
        o_qkv[p.c * 2 + k] = total
    here = o_qkv.at[pl.ds(p.c * 2, 2)]
    five = [w.push(here, here, p.sibling())]
    vec.p4()
    five[0].wait_recv()
    vec.end()
    for copy in one + rows + two + three + four + five:
        copy.wait_send()


def scatter_last(grad_a, g_qkv, g_vec):
    shapes = [
        pltpu.VMEM((3, OWN, D), BF),
        pltpu.VMEM((3, 4, 48, 640), BF),
        pltpu.VMEM((4, 48, 640), BF),
        pltpu.VMEM((4, 48, 640), BF),
        pltpu.VMEM((2, 48, 640), BF),
        pltpu.VMEM((2, 48, 640), BF),
        pltpu.VMEM((4, 2, 48, 640), BF),
    ]
    shapes += scatter_shapes(16, 128, F32)
    return pl.pallas_call(
        last_kernel,
        out_shape=(
            jax.ShapeDtypeStruct((OWN, D), F32),
            jax.ShapeDtypeStruct((4, 48, 640), F32),
            jax.ShapeDtypeStruct((16, 128), F32),
        ),
        in_specs=[VMEM] * 3,
        out_specs=(VMEM,) * 3,
        scratch_shapes=shapes + sems(SCATTER_SENDS + 24, 1),
        compiler_params=pltpu.CompilerParams(
            collective_id=2, has_side_effects=True, vmem_limit_bytes=24 * MIB
        ),
        name="scatter_last",
    )(grad_a, g_qkv, g_vec)


def adamw(weight, moment, second, grad, rate, decay):
    moment_new = BETA_ONE * moment + (1.0 - BETA_ONE) * grad
    second_new = BETA_TWO * second + (1.0 - BETA_TWO) * grad * grad
    moment_hat = moment_new / (1.0 - BETA_ONE**STEP)
    second_hat = second_new / (1.0 - BETA_TWO**STEP)
    weight_new = weight - rate * (moment_hat / (jnp.sqrt(second_hat) + EPS_ADAM) + decay * weight)
    return (weight_new, moment_new, second_new)


def pack_groups(queries, keys, values):
    blank = jnp.zeros((queries.shape[0], HD), queries.dtype)
    groups = []
    for g in range(4):
        q, k, v = ([a[:, (3 * g + j) * HD : (3 * g + j + 1) * HD] for j in range(3)] for a in (queries, keys, values))
        groups.append(jnp.concatenate([v[0], k[0], k[1], v[1], v[2], k[2], q[1], q[0], blank, q[2]], 1))
    return jnp.stack(groups)


def unpack_group(packed):
    col = [packed[:, j * HD : (j + 1) * HD] for j in range(10)]
    return [jnp.concatenate([col[j] for j in order], 1) for order in ((7, 6, 9), (1, 2, 5), (0, 3, 4))]


def per_device(
    tokens,
    cotangent,
    lengths,
    positions,
    w_rows,
    w_down,
    vectors,
    moment_rows,
    second_rows,
    moment_down,
    second_down,
    moment_vectors,
    second_vectors,
):
    shard_index = lax.axis_index("shard")
    core = lax.rem(lax.axis_index("replica"), 2)
    z, y = lax.div(shard_index, 4), lax.rem(shard_index, 4)
    own_u, own_v = jnp.where(core == 0, y, z), jnp.where(core == 0, z, y)
    low_rows = w_rows.astype(BF)
    low_qkv = pack_groups(low_rows[:, :D], low_rows[:, D : 2 * D], low_rows[:, 2 * D : 3 * D])
    low_vecs = jnp.pad(vectors.astype(BF), ((0, 4), (0, 80)))
    x_quarter, w_qkv, vec_all = gather_first(tokens, low_qkv, low_vecs)
    w_qkv = w_qkv.reshape(D, 640)
    vecs = vec_all[:, :, :48].transpose(1, 0, 2).reshape(16, D).astype(F32)

    place_blocks = positions.reshape(4, 4, OWN)
    place_all = jnp.where(core == 0, place_blocks, place_blocks.transpose(1, 0, 2)).reshape(GROUP)
    seq_ends = jnp.cumsum(lengths[0])
    place_quarter = lax.dynamic_slice_in_dim(place_all, own_v * 512, 512)
    seq_start = jnp.max(
        jnp.where(place_quarter[None, :] >= seq_ends[:, None], seq_ends[:, None], 0), axis=0
    )
    key_place = place_all[:, None]
    query_place = jnp.pad(jnp.stack([place_quarter, seq_start]), ((0, 6), (0, 0)))

    unit_quarter, _ = normalise(x_quarter.reshape(512, D).astype(F32))
    normed = (unit_quarter * vecs[0:1] + vecs[1:2]).astype(BF)
    projected = jnp.dot(normed, w_qkv, preferred_element_type=F32)
    bias_all = pack_groups(vecs[2:3], jnp.zeros((1, D), F32), vecs[3:4])
    bias_own = lax.dynamic_index_in_dim(bias_all, own_u, 0, keepdims=False)
    scale = jnp.where(jnp.arange(640) < 384, 1.0, HD ** (-0.5)).astype(BF)
    packed = (projected + bias_own).astype(BF) * scale
    grad_packed, outputs, grad_middle, vec_grads, sum_down, sum_first, sum_out = layer(
        packed, tokens, cotangent, low_rows[:, 3 * D :], w_down.astype(BF), key_place, query_place,
        vecs, vecs[8:16],
    )

    grad_qkv = jnp.einsum("td,tj->dj", normed, grad_packed, preferred_element_type=F32).astype(BF)
    grad_a = jnp.einsum("tj,dj->td", grad_packed, w_qkv, preferred_element_type=F32)
    bias_sums = unpack_group(jnp.sum(grad_packed.astype(F32), 0, keepdims=True))
    column = own_u * 192
    blank = jnp.zeros((1, D), F32)
    vec_grads = vec_grads + jnp.concatenate(
        [
            jnp.sum(grad_a * unit_quarter, 0, keepdims=True),
            jnp.sum(grad_a, 0, keepdims=True),
            lax.dynamic_update_slice(blank, bias_sums[0], (0, column)),
            lax.dynamic_update_slice(blank, bias_sums[2], (0, column)),
            jnp.zeros((12, D), F32),
        ],
        0,
    )
    vec_send = jnp.pad(vec_grads.reshape(16, 16, 48).transpose(1, 0, 2), ((0, 0), (0, 0), (0, 80)))
    grad_normed, sum_qkv, sum_vec = scatter_last(
        grad_a.astype(BF).reshape(4, OWN, D), grad_qkv.reshape(16, 48, 640), vec_send.reshape(4, 4, 16, 128)
    )
    unit, inverse = normalise(tokens.astype(F32))
    grad_input = (grad_middle + normalise_back(grad_normed, unit, inverse, vecs[0:1])).astype(BF)
    groups = [unpack_group(sum_qkv[g]) for g in range(4)]
    grad_rows = jnp.concatenate(
        [groups[g][k] for k in range(3) for g in range(4)] + [sum_out, sum_first], 1
    )
    rows_new = adamw(w_rows, moment_rows, second_rows, grad_rows, LR_MATRIX, DECAY)
    down_new = adamw(w_down, moment_down, second_down, sum_down, LR_MATRIX, DECAY)
    vec_new = adamw(vectors, moment_vectors, second_vectors, sum_vec[:12, :48], LR_VECTOR, 0.0)
    return (
        outputs,
        grad_input,
        rows_new[0],
        rows_new[1],
        rows_new[2],
        down_new[0],
        down_new[1],
        down_new[2],
        vec_new[0],
        vec_new[1],
        vec_new[2],
    )


def solution(mesh):
    return jax.shard_map(
        per_device,
        mesh=mesh,
        in_specs=(
            P(("replica", "shard"), None),
            P(("replica", "shard"), None),
            P("replica", None),
            P("replica", None),
            P("shard", None),
            P("shard", None),
            P(None, "shard"),
            P("shard", None),
            P("shard", None),
            P("shard", None),
            P("shard", None),
            P(None, "shard"),
            P(None, "shard"),
        ),
        out_specs=(
            P(("replica", "shard"), None),
            P(("replica", "shard"), None),
            P("shard", None),
            P("shard", None),
            P("shard", None),
            P("shard", None),
            P("shard", None),
            P("shard", None),
            P(None, "shard"),
            P(None, "shard"),
            P(None, "shard"),
        ),
        check_vma=False,
    )
```

time: 278 us -> 205 us (0.74); the launches traced: 274 us -> 204 us
  Pallas kernels: 202 us -> 171 us
  matrix products: 29.6 us -> 6.66 us
  local copies, waits for them, and re-layouts: 30.9 us -> 13.5 us
    pallas_call x4 -> x3, Pallas kernels: 202 us -> 171 us  [the longest x1 120 us: layer(): pl.pallas_call(layer_kernel, out_shape=(jax.ShapeDtypeStruct((512, 640),...]
    dot_general x12 -> x3, matrix products: 29.6 us -> 6.66 us  [the longest x1 2.91 us: per_device(): jnp.einsum('tj,dj->td', grad_packed, w_qkv, preferred_element_type=F32)]
    unnamed x110 -> x39, local copies, waits for them, and re-layouts: 14.8 us -> 0.99 us
    slice x22 -> x15, local copies, waits for them, and re-layouts: 1.33 us -> 6.64 us  [the longest x10 5.12 us: unpack_group(): col = [packed[:, j * HD:(j + 1) * HD] for j in range(10)]]
    reshape x5 -> x2, local copies, waits for them, and re-layouts: 4.42 us -> 0.15 us  [per_device(): vec_grads.reshape(16, 16, 48).transpose(1, 0, 2)]
where the time goes in v3:
time: 205 us; the launch traced here: 204 us
  Pallas kernels  171 us (83%)
  local copies, waits for them, and re-layouts  13.5 us (7%)
  other arithmetic  12.3 us (6%)
  matrix products  6.66 us (3%)
    pallas_call x1, Pallas kernels, layer(): pl.pallas_call(layer_kernel, out_shape=(jax.ShapeDtypeStruct((512, 640),...  120 us
    pallas_call x1, Pallas kernels, scatter_last(): pl.pallas_call(last_kernel, out_shape=(jax.ShapeDtypeStruct((OWN, D), F32...  30.8 us
    pallas_call x1, Pallas kernels, gather_first(): pl.pallas_call(first_kernel, out_shape=(jax.ShapeDtypeStruct((4, OWN, D),...  19.8 us
    sub x3, other arithmetic, adamw(): weight - rate * (moment_hat / (jnp.sqrt(second_hat) + EPS_ADAM) + decay *...  6.18 us
    slice x10, local copies, waits for them, and re-layouts, unpack_group(): col = [packed[:, j * HD:(j + 1) * HD] for j in range(10)]  5.12 us

profile of v3, /device:TPU:1, one launch (start us, length us, event | category | flops | bytes accessed | tf_op | source)
XLA Modules:
  0.0 204.2 jit_solution(4980051816273473271)
XLA Ops:
  0.6 1.3 convert_element_type.64
  2.0 0.1 fusion.26
  2.2 0.1 concatenate.47
  2.3 0.1 concatenate.48
  2.5 0.1 concatenate.49
  2.6 0.1 concatenate.46
  2.8 0.1 copy-done
  2.9 19.8 %gather_first.1 = (bf16[4,128,768]{2,1,0:T(8,128)(2,1)S(1)}, bf16[16,48,640]{2,1,0:T(8,128)(2,1)S(1)}, bf16[16,16,128]{2,1,0:T(8,128)(2,1)S(1)}) custom-call(bf16[128,768]{1,0:T(8,128)(2,1)S(1)} %copy-done, bf16[4,48,640]{2,1,0:T(8,128)(2,1)S(1)} %pad_maximum_fusion.w_qkv, bf16[16,128]{1,0:T(8,128)(2,1)S(1)} %pad.12.vec), custom_call_target="tpu_custom_call" | custom-call | tf_op jit(solution)/shard_map/gather_first/pallas_call | solution.py:332
  22.8 0.1 convert_element_type.71.vecs
  23.1 0.1 concatenate.50
  23.2 0.1 concatenate.51
  23.3 0.1 concatenate.52
  23.4 0.1 concatenate.53
  23.5 0.2 convert_reduce_fusion
  23.7 0.4 multiply_reduce_fusion.1
  24.3 0.4 add_convert_fusion.1
  24.7 1.6 fusion.2.packed
  26.3 0.7 slice.439.bias_first
  27.1 0.2 reduce-window.8
  27.4 0.6 pad.13.query_place
  28.0 1.3 copy.36.key_place
  29.4 0.8 slice.528.rest
  30.1 0.7 convert_element_type.74.down
  30.9 120.1 %layer.1 = (bf16[512,640]{1,0:T(8,128)(2,1)}, bf16[128,768]{1,0:T(8,128)(2,1)}, f32[128,768]{1,0:T(8,128)}, f32[16,768]{1,0:T(8,128)}, f32[192,768]{1,0:T(8,128)...) custom-call(bf16[512,640]{1,0:T(8,128)(2,1)} %fusion.2.packed, bf16[128,768]{1,0:T(8,128)(2,1)} %x.9, bf16[128,768]{1,0:T(8,128)(2,1)} %cot.1, ...), custom_call_target="tpu_custom_call" | custom-call | tf_op jit(solution)/shard_map/layer/pallas_call | solution.py:692
  151.0 1.2 convert_reduce_fusion.1
  152.4 0.1 dynamic_update_slice.7
  152.6 0.2 dynamic_update_slice.6
  152.7 2.9 %fusion.22 = (f32[768]{0:T(1024)S(1)}, f32[768]{0:T(1024)S(1)}, bf16[512,768]{1,0:T(8,128)(2,1)S(1)}, bf16[512,768]{1,0:T(8,128)(2,1)}) fusion(f32[512]{0:T(512)S(1)} %get-tuple-element.139, f32[512]{0:T(512)S(1)} %get-tuple-element.137, bf16[4,128,768]{2,1,0:T(8,128)(2,1)S(1)} %get-tuple-element.24, f32[768]{0:T(1024)S(1)} %add.119, f32[768]{0:T(1024)S(1)} %mul.193, ...), kind=kOutput, calls=%fused_computation.69 | convolution fusion | flops 507247104 | bytes 4014080 | tf_op jit(solution)/shard_map/tj,dj->td/dot_general | solution.py:872
  155.7 0.2 concatenate.56
  155.9 0.1 reshape.165
  156.0 2.1 %convolution_convert_fusion = bf16[768,640]{1,0:T(8,128)(2,1)S(1)} fusion(bf16[512,768]{1,0:T(8,128)(2,1)} %get-tuple-element.53, bf16[512,640]{1,0:T(8,128)(2,1)} %get-tuple-element.29), kind=kOutput, calls=%fused_computation.8 | convolution fusion | flops 503808000 | bytes 2424832 | tf_op jit(solution)/shard_map/td,tj->dj/dot_general | solution.py:871
  158.2 30.8 %scatter_last.1 = (f32[128,768]{1,0:T(8,128)S(1)}, f32[4,48,640]{2,1,0:T(8,128)S(1)}, f32[16,128]{1,0:T(8,128)S(1)}) custom-call(bf16[4,128,768]{2,1,0:T(8,128)(2,1)S(1)} %bitcast.54, bf16[16,48,640]{2,1,0:T(8,128)(2,1)S(1)} %bitcast.53, f32[4,4,16,128]{3,2,1,0:T(8,128)S(1)} %bitcast.55), custom_call_target="tpu_custom_call" | custom-call | tf_op jit(solution)/shard_map/scatter_last/pallas_call | solution.py:783
  189.0 0.7 fusion.33
  189.7 0.7 fusion.35
  190.4 0.7 fusion.29
  191.1 0.7 fusion.31
  191.9 0.7 fusion.34
  192.6 0.7 fusion.28
  193.3 0.7 fusion.30
  194.0 1.7 concatenate.57
  195.8 4.1 %multiply_subtract_fusion = (f32[48,6144]{1,0:T(8,128)}, f32[48,6144]{1,0:T(8,128)}, f32[48,6144]{1,0:T(8,128)}) fusion(f32[48,6144]{1,0:T(8,128)S(1)} %copy-done.2, f32[48,6144]{1,0:T(8,128)S(1)} %concatenate.57, f32[48,6144]{1,0:T(8,128)} %param.20, f32[48,6144]{1,0:T(8,128)} %param.21), kind=kLoop, calls=%fused_computation.14 | loop fusion | flops 4423680 | bytes 8257536 | tf_op jit(solution)/shard_map/sub | solution.py:805
  199.9 0.1 convert_reduce_fusion.2
  200.0 0.2 fusion.14
  200.2 0.2 multiply_reduce_fusion.2
  200.5 0.9 fusion.13
  201.3 0.6 multiply_subtract_fusion.2
  202.0 1.5 multiply_subtract_fusion.1
  203.5 0.7 copy.45
  (80 shorter events, 1.4 us)
Async XLA Ops:
  2.0 0.8 copy-start.13
  2.0 0.9 copy-start
  22.9 1.7 copy-start.8
  24.3 128.4 %copy-start.10 = (f32[768]{0:T(1024)}, f32[768]{0:T(1024)S(1)}, u32[]{:S(2)}) copy-start(f32[768]{0:T(1024)S(1)} %mul.193) | copy-start | bytes 9220
  24.7 2.4 %copy-start.17 = (s32[1,2048]{1,0:T(1,128)S(1)}, s32[1,2048]{1,0:T(1,128)}, u32[]{:S(2)}) copy-start(s32[1,2048]{1,0:T(1,128)} %param.16) | copy-start | bytes 24580
  24.7 2.4 %copy-start.18 = (s32[1,3]{1,0:T(1,128)S(1)}, s32[1,3]{1,0:T(1,128)}, u32[]{:S(2)}) copy-start(s32[1,3]{1,0:T(1,128)} %param.15) | copy-start | bytes 40
  26.3 3.8 %copy-start.3 = (f32[192,768]{1,0:T(8,128)S(1)}, f32[192,768]{1,0:T(8,128)}, u32[]{:S(2)}) copy-start(f32[192,768]{1,0:T(8,128)} %param.18) | copy-start | bytes 1769476
  152.7 3.1 %copy-start.12 = (f32[16,768]{1,0:T(8,128)S(1)}, f32[16,768]{1,0:T(8,128)}, u32[]{:S(2)}) copy-start(f32[16,768]{1,0:T(8,128)} %get-tuple-element.30) | copy-start | bytes 147460
  194.0 1.8 copy-start.2
  195.8 4.1 %copy-start.1 = (bf16[128,768]{1,0:T(8,128)(2,1)S(1)}, bf16[128,768]{1,0:T(8,128)(2,1)}, u32[]{:S(2)}) copy-start(bf16[128,768]{1,0:T(8,128)(2,1)} %x.9) | copy-start | bytes 589828
  195.8 4.4 %copy-start.11 = (f32[768]{0:T(1024)S(1)}, f32[768]{0:T(1024)}, u32[]{:S(2)}) copy-start(f32[768]{0:T(1024)} %copy-done.10) | copy-start | bytes 9220
  195.8 4.7 %copy-start.7 = (f32[128,768]{1,0:T(8,128)S(1)}, f32[128,768]{1,0:T(8,128)}, u32[]{:S(2)}) copy-start(f32[128,768]{1,0:T(8,128)} %get-tuple-element.28) | copy-start | bytes 1179652
  199.8 1.5 copy-start.14
  199.8 1.5 copy-start.15
  199.8 1.5 copy-start.16
  199.8 2.1 %copy-start.4 = (f32[192,768]{1,0:T(8,128)S(1)}, f32[192,768]{1,0:T(8,128)}, u32[]{:S(2)}) copy-start(f32[192,768]{1,0:T(8,128)} %param.22) | copy-start | bytes 1769476
  199.9 2.1 %copy-start.5 = (f32[192,768]{1,0:T(8,128)S(1)}, f32[192,768]{1,0:T(8,128)}, u32[]{:S(2)}) copy-start(f32[192,768]{1,0:T(8,128)} %param.23) | copy-start | bytes 1769476
  199.9 2.1 %copy-start.6 = (f32[192,768]{1,0:T(8,128)S(1)}, f32[192,768]{1,0:T(8,128)}, u32[]{:S(2)}) copy-start(f32[192,768]{1,0:T(8,128)} %get-tuple-element.35) | copy-start | bytes 1769476
  202.0 1.5 copy-start.9

commit v4 on v3

--- a/solution.py
+++ b/solution.py
@@ -192,10 +192,10 @@
 
 
 class Scatter:
-    def __init__(self, wire, place, grad, out, mine, other, z_first, shared, scratch):
+    def __init__(self, wire, place, grad, out, mine, other, to, z_first, scratch):
         self.wire, self.place, self.grad, self.out = wire, place, grad, out
-        self.shared, self.z_first = shared, z_first
-        self.mine, self.other = mine, other
+        self.z_first = z_first
+        self.mine, self.other, self.to = mine, other, to
         self.in0, self.in1, self.part, self.in2, self.in3 = scratch
         self.sends, self.wait = [], []
 
@@ -216,10 +216,6 @@
         p = self.place
         for copy in self.wait:
             copy.wait_recv()
-        if not self.shared:
-            for copy in self.sends:
-                copy.wait_send()
-            self.sends = []
 
         def add(i, carry):
             at = (lax.div(i, 4), lax.rem(i, 4))
@@ -274,11 +270,9 @@
         total = self.in3[0].astype(F32)
         for k in range(1, 4):
             total = total + self.in3[k].astype(F32)
-        self.out[self.mine] = total
-        self.wait = []
-        if self.shared:
-            here = self.out.at[self.mine]
-            self.wait = [self.push(here, here, self.place.sibling())]
+        self.out[self.to] = total
+        here = self.out.at[self.to]
+        self.wait = [self.push(here, here, self.place.sibling())]
 
     def end(self):
         for copy in self.wait:
@@ -303,48 +297,6 @@
     return v * p.v_step + u * p.u_step
 
 
-def first_kernel(x, w_qkv, vec, x_all, w_all, vec_all, send_sems, recv_sems, local_sems):
-    p = Place()
-    w = Wire(send_sems, recv_sems, local_sems)
-    greet(all_peers(p))
-    one = [(d, w.push(w_qkv.at[step4(p.u, d)], w_all.at[p.s], p.udev(d))) for d in (1, 3, 2)]
-    vec_one = [w.push(vec, vec_all.at[p.s], p.ydev(d)) for d in (1, 3, 2)]
-    w_all[p.s] = w_qkv[p.u]
-    vec_all[p.s] = vec[...]
-    two = [w.push(w_all.at[p.s], w_all.at[p.s], p.vdev(e)) for e in (1, 3, 2)]
-    rows = [w.push(x, x_all.at[p.u], p.udev(d)) for d in (1, 3, 2)]
-    x_all[p.u] = x[...]
-    for d, copy in one:
-        copy.wait_recv()
-        block = w_all.at[owner(p, step4(p.u, 4 - d), p.v)]
-        two += [w.push(block, block, p.vdev(e)) for e in (1, 3, 2)]
-    for copy in vec_one:
-        copy.wait_recv()
-    slab = vec_all.at[pl.ds(p.z * 4, 4)]
-    vec_two = [w.push(slab, slab, p.zdev(d)) for d in (1, 3, 2)]
-    for copy in two + rows + vec_two:
-        copy.wait_recv()
-    for copy in [c for _, c in one] + vec_one + two + rows + vec_two:
-        copy.wait_send()
-
-
-def gather_first(x, w_qkv, vec):
-    return pl.pallas_call(
-        first_kernel,
-        out_shape=(
-            jax.ShapeDtypeStruct((4, OWN, D), BF),
-            jax.ShapeDtypeStruct((16, 48, 640), BF),
-            jax.ShapeDtypeStruct((16, 16, 128), BF),
-        ),
-        in_specs=[VMEM] * 3,
-        out_specs=(VMEM,) * 3,
-        scratch_shapes=sems(24, 1),
-        compiler_params=pltpu.CompilerParams(
-            collective_id=0, has_side_effects=True, vmem_limit_bytes=20 * MIB
-        ),
-        name="gather_first",
-    )(x, w_qkv, vec)
-
 def half_lanes(value, right):
     lane = lax.broadcasted_iota(jnp.int32, value.shape, 1)
     keep = lane >= HD if right else lane < HD
@@ -370,9 +322,11 @@
 def fill_bias(key_place, query_place, bias):
     def body(i, carry):
         rows = pl.ds(pl.multiple_of(i * CHUNK, CHUNK), CHUNK)
-        keys = key_place[rows, :]
-        ok = (keys <= query_place[0:1, :]) & (keys >= query_place[1:2, :])
-        bias[rows, :] = jnp.where(ok, 0.0, HUGE_NEG).astype(BF)
+        keys = key_place[rows, 0:128]
+        for k in range(4):
+            cols = slice(k * 128, k * 128 + 128)
+            ok = (keys <= query_place[0:1, cols]) & (keys >= query_place[1:2, cols])
+            bias[rows, cols] = jnp.where(ok, 0.0, HUGE_NEG).astype(BF)
         return carry
 
     lax.fori_loop(0, STEPS, body, 0, unroll=True)
@@ -454,8 +408,9 @@
         if tile == 0:
             acc[chunk_rows(i), :] = both
         else:
-            rows = pl.ds(pl.multiple_of(lax.rem(i, 2) * CHUNK, CHUNK), CHUNK)
-            part_send[head, lax.div(i, 2), rows, :] = (acc[chunk_rows(i), :] + both).astype(BF)
+            total_kv = (acc[chunk_rows(i), :] + both).astype(BF)
+            lanes = slice(head * 128, head * 128 + 128)
+            part_send[lax.div(i, 2), pl.ds(lax.rem(i, 2) * 2, 2), 0:OWN, lanes] = total_kv.reshape(2, OWN, 128)
         return total_dq + dot_plain(turned[head, :, chunk_rows(i)], gscore)
 
     total_dq = lax.fori_loop(0, STEPS, back, jnp.zeros((128, TILE), F32), unroll=True)
@@ -493,22 +448,49 @@
     return jnp.concatenate([own, jnp.zeros((64, D), BF)], 0)
 
 
+def ordered_sum(blocks):
+    total = blocks[0].astype(F32)
+    for k in range(1, blocks.shape[0]):
+        total = total + blocks[k].astype(F32)
+    return total
+
+
+def natural_group(packed):
+    col = [packed[:, j * HD : (j + 1) * HD] for j in range(10)]
+    return [[col[j] for j in order] for order in ((7, 6, 9), (1, 2, 5), (0, 3, 4))]
+
+
 def layer_kernel(
-    packed, x, cot, rest, down, key_place, query_place, vecs, bias_first,
-    grad_packed, outputs, grad_middle, grad_vecs, o_down, o_first, o_out, *scratch,
+    x, cot, w_qkv, vec, lanes, rest, down, key_place, query_place,
+    outputs, grad_input, o_rows, o_down, o_vec, *scratch,
 ):
     (
         full_rest, full_down, kv, bias, probs, grad_probs, turned, head_out, out_send, attended, lse,
-        g_down, g_first, g_out, grad_send, dob, acc, part_send, part_in, dq, total_out, total_dc, low,
-    ) = scratch[:23]
-    blocks = scratch[23:-3]
+        g_down, g_first, g_out, dob, acc, part_in, total_out, total_dc, low,
+        x_all, w_all, normed, vec_y, vec_z, vecs, grad_vecs, vec_in, back, in_a, in1, part, in2, in0, held, in3, packed_sum,
+    ) = scratch[:37]
+    part_send, grad_send, dq = full_down, out_send, head_out
+    blocks = scratch[37:-3]
     p = Place()
     w = Wire(*scratch[-3:])
     greet(all_peers(p) + x_peers(p))
 
-    kv[p.v] = packed[...]
-    mine = kv.at[p.v, :, pl.ds(0, 384)]
-    to_v = [w.push(mine, mine, p.vdev(d)) for d in (1, 3, 2)]
+    places = w.local(key_place, grad_probs.at[:, pl.ds(0, 128)])
+    w_one = [(d, w.push(w_qkv.at[step4(p.u, d)], w_all.at[p.s], p.udev(d))) for d in (1, 3, 2)]
+    vec_one = [w.push(vec, vec_y.at[p.y], p.ydev(d)) for d in (1, 3, 2)]
+    w_all[p.s] = w_qkv[p.u]
+    vec_y[p.y] = vec[...]
+    w_two = [w.push(w_all.at[p.s], w_all.at[p.s], p.vdev(e)) for e in (1, 3, 2)]
+    x_one = [w.push(x, x_all.at[p.u], p.udev(d)) for d in (1, 3, 2)]
+    x_all[p.u] = x[...]
+    for d, copy in w_one:
+        copy.wait_recv()
+        block = w_all.at[owner(p, step4(p.u, 4 - d), p.v)]
+        w_two += [w.push(block, block, p.vdev(e)) for e in (1, 3, 2)]
+    for copy in vec_one:
+        copy.wait_recv()
+    vec_z[p.z] = ordered_sum(vec_y).astype(BF)
+    vec_two = [w.push(vec_z.at[p.z], vec_z.at[p.z], p.zdev(d)) for d in (1, 3, 2)]
     half = p.c * 1920
     parts = [
         Gather(w, p, rest, full_rest, region(0, None, half, 1024), True),
@@ -516,11 +498,33 @@
         Gather(w, p, down, full_down, region(pl.multiple_of(p.c * 96, 16), 48, 0, None), True),
         Gather(w, p, down, full_down, region(pl.multiple_of(p.c * 96 + 48, 16), 48, 0, None), False),
     ]
-    for part in parts:
-        part.first()
-    fill_bias(key_place, query_place, bias)
-    for part in parts:
-        part.second()
+    for part_ in parts:
+        part_.first()
+    places.wait()
+    fill_bias(grad_probs, query_place, bias)
+    for copy in x_one + vec_two:
+        copy.wait_recv()
+    vecs[...] = ordered_sum(vec_z)
+    low_vecs = vecs[...].astype(BF)
+
+    def pick(row, dtype):
+        column = lax.broadcasted_iota(jnp.int32, (D, 640), 0) - 192 * p.u
+        return (column == lanes[row : row + 1, :]).astype(dtype)
+
+    bias_own = dot_plain(low_vecs, pick(0, BF))[2:3, :] + dot_plain(low_vecs, pick(1, BF))[3:4, :]
+    scale = jnp.where(lax.broadcasted_iota(jnp.int32, (1, 640), 1) < 384, 1.0, HD ** (-0.5)).astype(F32)
+    for k in range(4):
+        unit, _ = normalise(x_all[k].astype(F32))
+        normed[k] = (unit * vecs[0:1, :] + vecs[1:2, :]).astype(BF)
+    for copy in w_two:
+        copy.wait_recv()
+    for k in range(4):
+        projected = dot_plain(normed[k], w_all[...].reshape(D, 640)) + bias_own
+        kv[p.v, k * OWN : k * OWN + OWN, :] = (projected.astype(BF).astype(F32) * scale).astype(BF)
+    mine = kv.at[p.v, :, pl.ds(0, 384)]
+    to_v = [w.push(mine, mine, p.vdev(d)) for d in (1, 3, 2)]
+    for part_ in parts:
+        part_.second()
     for copy in to_v:
         copy.wait_recv()
     head_out[192:256, :] = jnp.zeros((64, 512), F32)
@@ -529,21 +533,21 @@
         for tile in range(2):
             attend(kv, p, head, tile, bias, probs, turned, head_out, lse)
         if head == 1:
-            for part in parts[:2]:
-                part.third()
+            for part_ in parts[:2]:
+                part_.third()
     for k in range(4):
         out_send[k] = head_out[:, k * OWN : k * OWN + OWN].T.astype(BF)
     attended[p.u] = out_send[p.u]
     out_back = [w.push(out_send.at[step4(p.u, d)], attended.at[p.u], p.udev(d)) for d in (1, 3, 2)]
-    for part in parts[2:]:
-        part.third()
-    for part in parts:
-        part.fourth()
+    for part_ in parts[2:]:
+        part_.third()
+    for part_ in parts:
+        part_.fourth()
     for copy in out_back:
         copy.wait_recv()
-    for part in parts:
-        part.end()
-    for copy in to_v + out_back:
+    for part_ in parts:
+        part_.end()
+    for copy in to_v + out_back + x_one + w_two + vec_one + vec_two + [c for _, c in w_one]:
         copy.wait_send()
 
     grad_y = cot[...].astype(F32)
@@ -560,47 +564,61 @@
         at = i * D + p.c * 384
         to = i * D + (1 - p.c) * 384
         return Scatter(
-            w, p, g_first, o_first, region(0, None, at, 384), region(0, None, to, 384),
-            i % 2 == 0, True, blocks[5 * i : 5 * i + 5],
+            w, p, g_first, o_rows, region(0, None, at, 384), region(0, None, to, 384),
+            region(0, None, at + 4 * D, 384), i % 2 == 0, blocks[5 * i : 5 * i + 5],
         )
 
     firsts = [first_part(i) for i in range(4)]
     at, to = p.c * 384, (1 - p.c) * 384
     downs = [
-        Scatter(w, p, g_down, o_down, region(0, 96, at, 384), region(0, 96, to, 384), True, True, blocks[20:25]),
-        Scatter(w, p, g_down, o_down, region(96, 96, at, 384), region(96, 96, to, 384), False, True, blocks[25:30]),
+        Scatter(
+            w, p, g_down, o_down, region(0, 96, at, 384), region(0, 96, to, 384),
+            region(0, 96, at, 384), True, blocks[20:25],
+        ),
+        Scatter(
+            w, p, g_down, o_down, region(96, 96, at, 384), region(96, 96, to, 384),
+            region(96, 96, at, 384), False, blocks[25:30],
+        ),
     ]
     outs = [
-        Scatter(w, p, g_out, o_out, region(0, None, at, 384), region(0, None, to, 384), False, True, blocks[30:35])
+        Scatter(
+            w, p, g_out, o_rows, region(0, None, at, 384), region(0, None, to, 384),
+            region(0, None, at + 3 * D, 384), False, blocks[30:35],
+        )
     ]
     for i in range(4):
         w_first = full_rest[:, :, :, D + i * D : 2 * D + i * D].reshape(D, D)
         w_down = full_down[i].reshape(D, D)
-        act = dot_plain(low[0], w_first) + bias_first[i : i + 1, :]
+        act = dot_plain(low[0], w_first) + vecs[8 + i : 9 + i, :]
         square = act * act
         bent = jnp.tanh(GELU_A * (act + GELU_B * act * square))
         hidden = (0.5 * act * (1.0 + bent)).astype(BF)
         slope = 0.5 * (1.0 + bent) + 0.5 * act * (1.0 - bent * bent) * (
             GELU_A * (1.0 + 3.0 * GELU_B * square)
         )
-        g_down[i] = dot_plain(hidden.T, cot[...]).astype(BF).reshape(4, 192, D)
-        for part in downs:
-            part.p0_slab(i)
+        hidden_turned = hidden.T
+        for k in range(2):
+            rows = slice(k * 384, k * 384 + 384)
+            g_down[i, 2 * k : 2 * k + 2] = (
+                dot_plain(hidden_turned[rows], cot[...]).astype(BF).reshape(2, 192, D)
+            )
+        for part_ in downs:
+            part_.p0_slab(i)
         grad_act = (dot_lanes(cot[...], w_down) * slope).astype(BF)
         grad_vecs[8 + i : 9 + i, :] = col_sum(grad_act.astype(F32))
-        g_first[:, :, :, i * D : i * D + D] = (
-            dot_plain(low_turned, grad_act).astype(BF).reshape(4, 4, 48, D)
-        )
+        for k in range(2):
+            rows = slice(k * 384, k * 384 + 384)
+            g_first[2 * k : 2 * k + 2, :, :, i * D : i * D + D] = (
+                dot_plain(low_turned[rows], grad_act).astype(BF).reshape(2, 4, 48, D)
+            )
         firsts[i].p0()
         total_dc[...] += dot_lanes(grad_act, w_first)
         total_out[...] += dot_plain(hidden, w_down)
-        if i > 0:
-            firsts[i - 1].p1()
     outputs[...] = total_out[...].astype(BF)
 
     grad_c = total_dc[...]
     grad_m = grad_y + normalise_back(grad_c, unit, inverse, vecs[5:6, :])
-    grad_middle[...] = grad_m
+    total_out[...] = grad_m
     low[1] = grad_m.astype(BF)
     for g in range(4):
         grad_send[g] = dot_lanes(low[1], out_rows(full_rest, g)).astype(BF)
@@ -615,16 +633,18 @@
     grad_vecs[6:7, :] = col_sum(grad_c)
     grad_vecs[7:8, :] = col_sum(grad_y)
     grad_vecs[12:16, :] = jnp.zeros((4, D), F32)
+    for part_ in firsts[:2]:
+        part_.p1()
     for copy in to_u:
         copy.wait_recv()
 
     stages = [
-        lambda: [part.p1() for part in firsts[3:] + downs],
-        lambda: [part.p2() for part in firsts[:2]] + [outs[0].p1()],
-        lambda: [part.p2() for part in firsts[2:]] + [part.p3() for part in firsts[:2]],
-        lambda: [part.p2() for part in downs],
-        lambda: [part.p3() for part in firsts[2:]] + [outs[0].p2()] + [part.p4() for part in firsts[:2]],
-        lambda: [part.p3() for part in downs + outs],
+        lambda: [part_.p1() for part_ in firsts[2:3]],
+        lambda: [part_.p1() for part_ in firsts[3:]],
+        lambda: [part_.p1() for part_ in downs],
+        lambda: [part_.p2() for part_ in firsts[:2]],
+        lambda: [part_.p1() for part_ in outs],
+        lambda: [part_.p2() for part_ in firsts[2:]] + [part_.p3() for part_ in firsts[:2]],
     ]
     to_v_back = []
     for head in range(3):
@@ -635,33 +655,132 @@
             if tile == 1:
                 to_v_back.append(
                     [
-                        w.push(part_send.at[head, step4(p.v, d)], part_in.at[head, d - 1], p.vdev(d))
+                        w.push(
+                            part_send.at[step4(p.v, d), :, pl.ds(0, OWN), pl.ds(head * 128, 128)],
+                            part_in.at[head, d - 1],
+                            p.vdev(d),
+                        )
                         for d in (1, 3, 2)
                     ]
                 )
             stages[head * 2 + tile]()
     dq[128:192, :] = jnp.zeros((64, 512), F32)
     for k in range(4):
-        rows = slice(k * OWN, k * OWN + OWN)
-        grad_packed[rows, 384:640] = dq[:, rows].T.astype(BF)
+        back[k, :, 384:640] = dq[:, k * OWN : k * OWN + OWN].T.astype(BF)
     for head in range(3):
         for copy in to_v_back[head]:
             copy.wait_recv()
+        columns = slice(head * 128, head * 128 + 128)
         for k in range(4):
-            rows = slice(k * OWN, k * OWN + OWN)
-            total = part_send[head, p.v, rows, :].astype(F32)
+            total = part_send[p.v, k, 0:OWN, columns].astype(F32)
             for d in range(3):
-                total = total + part_in[head, d, rows, :].astype(F32)
-            grad_packed[rows, head * 128 : head * 128 + 128] = total.astype(BF)
-    for part in firsts[2:] + downs + outs:
-        part.p4()
-    for part in firsts + downs + outs:
-        part.end()
-    for copy in to_u + sum(to_v_back, []):
+                total = total + part_in[head, d, k].astype(F32)
+            back[k, :, columns] = total.astype(BF)
+
+    grad_qkv = back[...].reshape(512, 640)
+    for k in range(2):
+        turned_rows = normed[:, :, k * 384 : k * 384 + 384].reshape(512, 384).T
+        g_qkv = dot_plain(turned_rows, grad_qkv).astype(BF)
+        full_rest[2 * k : 2 * k + 2, :, :, 0:640] = g_qkv.reshape(2, 4, 48, 640)
+
+    def rows_of(u, v):
+        return full_rest.at[v + p.c * (u - v), u + p.c * (v - u), :, pl.ds(0, 640)]
+
+    one = []
+    for d in (1, 3, 2):
+        for k in range(4):
+            one.append(w.push(rows_of(k, step4(p.v, d)), in1.at[d - 1, k], p.vdev(d)))
+    grad_gain = jnp.zeros((1, D), F32)
+    grad_shift = jnp.zeros((1, D), F32)
+    for k in range(4):
+        grad_a = dot_lanes(back[k], w_all[...].reshape(D, 640))
+        unit_k, _ = normalise(x_all[k].astype(F32))
+        grad_gain = grad_gain + col_sum(grad_a * unit_k)
+        grad_shift = grad_shift + col_sum(grad_a)
+        normed[k] = grad_a.astype(BF)
+    a_one = [w.push(normed.at[step4(p.u, d)], in_a.at[d - 1], p.udev(d)) for d in (1, 3, 2)]
+    sums = jnp.broadcast_to(col_sum(grad_qkv.astype(F32)), (8, 640))
+    spread = (((1,), (1,)), ((), ()))
+    exact = lax.Precision.HIGHEST
+    bias_q = lax.dot_general(sums, pick(0, F32), spread, precision=exact, preferred_element_type=F32)
+    bias_v = lax.dot_general(sums, pick(1, F32), spread, precision=exact, preferred_element_type=F32)
+    grad_vecs[0:1, :] = grad_gain
+    grad_vecs[1:2, :] = grad_shift
+    grad_vecs[2:3, :] = bias_q[0:1, :]
+    grad_vecs[3:4, :] = bias_v[0:1, :]
+    vec_in[0, p.z] = grad_vecs[...]
+    vec_sends = [[w.push(grad_vecs, vec_in.at[0, p.z], p.zdev(d)) for d in (1, 3, 2)]]
+    for part_ in firsts[2:]:
+        part_.p3()
+    for part_ in downs + outs:
+        part_.p2()
+    for copy in one:
+        copy.wait_recv()
+    for k in range(4):
+        total = rows_of(k, p.v)[...].astype(F32)
+        for d in range(3):
+            total = total + in1[d, k].astype(F32)
+        part[k] = total.astype(BF)
+    two = [w.push(part.at[step4(p.u, d)], in2.at[p.u], p.udev(d)) for d in (1, 3, 2)]
+    in2[p.u] = part[p.u]
+    for copy in vec_sends[0]:
+        copy.wait_recv()
+    vec_in[1, p.y] = ordered_sum(vec_in.at[0])
+    vec_sends.append([w.push(vec_in.at[1, p.y], vec_in.at[1, p.y], p.ydev(d)) for d in (1, 3, 2)])
+    for part_ in firsts[:2]:
+        part_.p4()
+    for copy in two:
+        copy.wait_recv()
+    three = [w.push(in2.at[pl.ds((1 - p.c) * 2, 2)], in0, p.sibling())]
+    for copy in vec_sends[1]:
+        copy.wait_recv()
+    vec_in[2, p.x] = ordered_sum(vec_in.at[1])
+    vec_sends.append([w.push(vec_in.at[2, p.x], vec_in.at[2, p.x], p.xdev(d)) for d in (1, 3, 2)])
+    three[0].wait_recv()
+    for k in range(2):
+        held[k] = (in2[p.c * 2 + k].astype(F32) + in0[k].astype(F32)).astype(BF)
+    in3[p.x] = held[...]
+    four = [w.push(held, in3.at[p.x], p.xdev(d)) for d in (1, 3, 2)]
+    for part_ in downs + outs:
+        part_.p3()
+    for part_ in firsts[2:]:
+        part_.p4()
+    for copy in a_one:
+        copy.wait_recv()
+    grad_a = normed[p.u].astype(F32)
+    for d in range(3):
+        grad_a = grad_a + in_a[d].astype(F32)
+    unit, inverse = normalise(x[...].astype(F32))
+    grad_input[...] = (total_out[...] + normalise_back(grad_a, unit, inverse, vecs[0:1, :])).astype(BF)
+    for copy in vec_sends[2]:
+        copy.wait_recv()
+    vec_in[3, 0] = ordered_sum(vec_in.at[2])
+    vec_sends.append([w.push(vec_in.at[3, 0], vec_in.at[3, 1], p.sibling())])
+    for copy in four:
+        copy.wait_recv()
+    for k in range(2):
+        total = in3[0, k].astype(F32)
+        for d in range(1, 4):
+            total = total + in3[d, k].astype(F32)
+        packed_sum[p.c * 2 + k] = total
+    here = packed_sum.at[pl.ds(p.c * 2, 2)]
+    five = [w.push(here, here, p.sibling())]
+    for part_ in downs + outs:
+        part_.p4()
+    vec_sends[3][0].wait_recv()
+    o_vec[...] = vec_in[3, 0] + vec_in[3, 1]
+    five[0].wait_recv()
+    groups = [natural_group(packed_sum[g]) for g in range(4)]
+    for k in range(3):
+        o_rows[:, k * D : k * D + D] = jnp.concatenate(sum([groups[g][k] for g in range(4)], []), 1)
+    for part_ in firsts + downs + outs:
+        part_.end()
+    rest_sends = one + a_one + two + three + four + five + sum(vec_sends, [])
+    for copy in to_u + sum(to_v_back, []) + rest_sends:
         copy.wait_send()
 
 
-def layer(packed, x, cot, rest, down, key_place, query_place, vecs, bias_first):
+def layer(x, cot, w_qkv, vec, lanes, rest, down, key_place, query_place):
     shapes = [
         pltpu.VMEM((4, 4, 48, 5 * D), BF),
         pltpu.VMEM((4, 4, 192, D), BF),
@@ -678,99 +797,20 @@
         pltpu.VMEM((4, 4, 48, FF), BF),
         pltpu.VMEM((4, 4, 48, D), BF),
         pltpu.VMEM((4, OWN, 256), BF),
-        pltpu.VMEM((4, OWN, 256), BF),
         pltpu.VMEM((GROUP, 128), F32),
-        pltpu.VMEM((3, 4, 512, 128), BF),
-        pltpu.VMEM((3, 3, 512, 128), BF),
-        pltpu.VMEM((256, 512), F32),
+        pltpu.VMEM((3, 3, 4, OWN, 128), BF),
         pltpu.VMEM((OWN, D), F32),
         pltpu.VMEM((OWN, D), F32),
         pltpu.VMEM((2, OWN, D), BF),
-    ]
-    for rows in (48, 48, 48, 48, 96, 96, 48):
-        shapes += scatter_shapes(rows, 384, BF)
-    return pl.pallas_call(
-        layer_kernel,
-        out_shape=(
-            jax.ShapeDtypeStruct((512, 640), BF),
-            jax.ShapeDtypeStruct((OWN, D), BF),
-            jax.ShapeDtypeStruct((OWN, D), F32),
-            jax.ShapeDtypeStruct((16, D), F32),
-            jax.ShapeDtypeStruct((192, D), F32),
-            jax.ShapeDtypeStruct((48, FF), F32),
-            jax.ShapeDtypeStruct((48, D), F32),
-        ),
-        in_specs=[VMEM] * 9,
-        out_specs=(VMEM,) * 7,
-        scratch_shapes=shapes + sems(4 * GATHER_SENDS + 7 * SCATTER_SENDS + 18, 4),
-        compiler_params=pltpu.CompilerParams(
-            collective_id=1, has_side_effects=True, vmem_limit_bytes=60 * MIB
-        ),
-        name="layer",
-    )(packed, x, cot, rest, down, key_place, query_place, vecs, bias_first)
-
-
-def last_kernel(grad_a, g_qkv, g_vec, o_a, o_qkv, o_vec, *scratch):
-    in_a, in1, part, in2, in0, held, in3 = scratch[:7]
-    vec_blocks = scratch[7:12]
-    p = Place()
-    w = Wire(*scratch[-3:])
-    greet(all_peers(p) + x_peers(p))
-    vec = Scatter(
-        w, p, g_vec, o_vec, (slice(None), slice(None)), (slice(None), slice(None)), False, False, vec_blocks
-    )
-    one = []
-    for d in (1, 3, 2):
-        for k in range(4):
-            src = g_qkv.at[owner(p, k, step4(p.v, d))]
-            one.append(w.push(src, in1.at[d - 1, k], p.vdev(d)))
-    rows = [w.push(grad_a.at[step4(p.u, d)], in_a.at[d - 1], p.udev(d)) for d in (1, 3, 2)]
-    vec.p0()
-    for copy in one:
-        copy.wait_recv()
-    for k in range(4):
-        total = g_qkv[owner(p, k, p.v)].astype(F32)
-        for d in range(3):
-            total = total + in1[d, k].astype(F32)
-        part[k] = total.astype(BF)
-    two = [w.push(part.at[step4(p.u, d)], in2.at[p.u], p.udev(d)) for d in (1, 3, 2)]
-    in2[p.u] = part[p.u]
-    vec.p1()
-    for copy in two:
-        copy.wait_recv()
-    other = in2.at[pl.ds((1 - p.c) * 2, 2)]
-    three = [w.push(other, in0, p.sibling())]
-    vec.p2()
-    three[0].wait_recv()
-    for k in range(2):
-        held[k] = (in2[p.c * 2 + k].astype(F32) + in0[k].astype(F32)).astype(BF)
-    in3[p.x] = held[...]
-    four = [w.push(held, in3.at[p.x], p.xdev(d)) for d in (1, 3, 2)]
-    for copy in rows:
-        copy.wait_recv()
-    total = grad_a[p.u].astype(F32)
-    for d in range(3):
-        total = total + in_a[d].astype(F32)
-    o_a[...] = total
-    vec.p3()
-    for copy in four:
-        copy.wait_recv()
-    for k in range(2):
-        total = in3[0, k].astype(F32)
-        for d in range(1, 4):
-            total = total + in3[d, k].astype(F32)
-        o_qkv[p.c * 2 + k] = total
-    here = o_qkv.at[pl.ds(p.c * 2, 2)]
-    five = [w.push(here, here, p.sibling())]
-    vec.p4()
-    five[0].wait_recv()
-    vec.end()
-    for copy in one + rows + two + three + four + five:
-        copy.wait_send()
-
-
-def scatter_last(grad_a, g_qkv, g_vec):
-    shapes = [
+        pltpu.VMEM((4, OWN, D), BF),
+        pltpu.VMEM((16, 48, 640), BF),
+        pltpu.VMEM((4, OWN, D), BF),
+        pltpu.VMEM((4, 16, D), BF),
+        pltpu.VMEM((4, 16, D), BF),
+        pltpu.VMEM((16, D), F32),
+        pltpu.VMEM((16, D), F32),
+        pltpu.VMEM((4, 4, 16, D), F32),
+        pltpu.VMEM((4, OWN, 640), BF),
         pltpu.VMEM((3, OWN, D), BF),
         pltpu.VMEM((3, 4, 48, 640), BF),
         pltpu.VMEM((4, 48, 640), BF),
@@ -778,23 +818,27 @@
         pltpu.VMEM((2, 48, 640), BF),
         pltpu.VMEM((2, 48, 640), BF),
         pltpu.VMEM((4, 2, 48, 640), BF),
+        pltpu.VMEM((4, 48, 640), F32),
     ]
-    shapes += scatter_shapes(16, 128, F32)
+    for rows in (48, 48, 48, 48, 96, 96, 48):
+        shapes += scatter_shapes(rows, 384, BF)
     return pl.pallas_call(
-        last_kernel,
+        layer_kernel,
         out_shape=(
-            jax.ShapeDtypeStruct((OWN, D), F32),
-            jax.ShapeDtypeStruct((4, 48, 640), F32),
-            jax.ShapeDtypeStruct((16, 128), F32),
+            jax.ShapeDtypeStruct((OWN, D), BF),
+            jax.ShapeDtypeStruct((OWN, D), BF),
+            jax.ShapeDtypeStruct((48, 8 * D), F32),
+            jax.ShapeDtypeStruct((192, D), F32),
+            jax.ShapeDtypeStruct((16, D), F32),
         ),
-        in_specs=[VMEM] * 3,
-        out_specs=(VMEM,) * 3,
-        scratch_shapes=shapes + sems(SCATTER_SENDS + 24, 1),
+        in_specs=[VMEM] * 7 + [ANY, VMEM],
+        out_specs=(VMEM,) * 5,
+        scratch_shapes=shapes + sems(4 * GATHER_SENDS + 7 * SCATTER_SENDS + 80, 5),
         compiler_params=pltpu.CompilerParams(
-            collective_id=2, has_side_effects=True, vmem_limit_bytes=24 * MIB
+            collective_id=1, has_side_effects=True, vmem_limit_bytes=62 * MIB
         ),
-        name="scatter_last",
-    )(grad_a, g_qkv, g_vec)
+        name="layer",
+    )(x, cot, w_qkv, vec, lanes, rest, down, key_place, query_place)
 
 
 def adamw(weight, moment, second, grad, rate, decay):
@@ -813,11 +857,6 @@
         q, k, v = ([a[:, (3 * g + j) * HD : (3 * g + j + 1) * HD] for j in range(3)] for a in (queries, keys, values))
         groups.append(jnp.concatenate([v[0], k[0], k[1], v[1], v[2], k[2], q[1], q[0], blank, q[2]], 1))
     return jnp.stack(groups)
-
-
-def unpack_group(packed):
-    col = [packed[:, j * HD : (j + 1) * HD] for j in range(10)]
-    return [jnp.concatenate([col[j] for j in order], 1) for order in ((7, 6, 9), (1, 2, 5), (0, 3, 4))]
 
 
 def per_device(
@@ -838,14 +877,12 @@
     shard_index = lax.axis_index("shard")
     core = lax.rem(lax.axis_index("replica"), 2)
     z, y = lax.div(shard_index, 4), lax.rem(shard_index, 4)
-    own_u, own_v = jnp.where(core == 0, y, z), jnp.where(core == 0, z, y)
+    own_v = jnp.where(core == 0, z, y)
     low_rows = w_rows.astype(BF)
     low_qkv = pack_groups(low_rows[:, :D], low_rows[:, D : 2 * D], low_rows[:, 2 * D : 3 * D])
-    low_vecs = jnp.pad(vectors.astype(BF), ((0, 4), (0, 80)))
-    x_quarter, w_qkv, vec_all = gather_first(tokens, low_qkv, low_vecs)
-    w_qkv = w_qkv.reshape(D, 640)
-    vecs = vec_all[:, :, :48].transpose(1, 0, 2).reshape(16, D).astype(F32)
-
+    own_vecs = lax.dynamic_update_slice(
+        jnp.zeros((16, D), BF), vectors.astype(BF), (0, shard_index * 48)
+    )
     place_blocks = positions.reshape(4, 4, OWN)
     place_all = jnp.where(core == 0, place_blocks, place_blocks.transpose(1, 0, 2)).reshape(GROUP)
     seq_ends = jnp.cumsum(lengths[0])
@@ -853,49 +890,22 @@
     seq_start = jnp.max(
         jnp.where(place_quarter[None, :] >= seq_ends[:, None], seq_ends[:, None], 0), axis=0
     )
-    key_place = place_all[:, None]
-    query_place = jnp.pad(jnp.stack([place_quarter, seq_start]), ((0, 6), (0, 0)))
-
-    unit_quarter, _ = normalise(x_quarter.reshape(512, D).astype(F32))
-    normed = (unit_quarter * vecs[0:1] + vecs[1:2]).astype(BF)
-    projected = jnp.dot(normed, w_qkv, preferred_element_type=F32)
-    bias_all = pack_groups(vecs[2:3], jnp.zeros((1, D), F32), vecs[3:4])
-    bias_own = lax.dynamic_index_in_dim(bias_all, own_u, 0, keepdims=False)
-    scale = jnp.where(jnp.arange(640) < 384, 1.0, HD ** (-0.5)).astype(BF)
-    packed = (projected + bias_own).astype(BF) * scale
-    grad_packed, outputs, grad_middle, vec_grads, sum_down, sum_first, sum_out = layer(
-        packed, tokens, cotangent, low_rows[:, 3 * D :], w_down.astype(BF), key_place, query_place,
-        vecs, vecs[8:16],
+    key_place = jnp.broadcast_to(place_all.astype(F32)[:, None], (GROUP, 128))
+    query_place = jnp.pad(jnp.stack([place_quarter, seq_start]).astype(F32), ((0, 6), (0, 0)))
+
+    column = jnp.arange(640)
+    block, within = column // HD, column % HD
+    lanes = jnp.full((8, 640), -GROUP, jnp.int32)
+    for row, places in ((0, ((7, 0), (6, 1), (9, 2))), (1, ((0, 0), (3, 1), (4, 2)))):
+        for at, head in places:
+            lanes = lanes.at[row].set(jnp.where(block == at, within + head * HD, lanes[row]))
+    outputs, grad_input, grad_rows, grad_down, grad_vecs = layer(
+        tokens, cotangent, low_qkv, own_vecs, lanes, low_rows[:, 3 * D :], w_down.astype(BF), key_place, query_place
     )
-
-    grad_qkv = jnp.einsum("td,tj->dj", normed, grad_packed, preferred_element_type=F32).astype(BF)
-    grad_a = jnp.einsum("tj,dj->td", grad_packed, w_qkv, preferred_element_type=F32)
-    bias_sums = unpack_group(jnp.sum(grad_packed.astype(F32), 0, keepdims=True))
-    column = own_u * 192
-    blank = jnp.zeros((1, D), F32)
-    vec_grads = vec_grads + jnp.concatenate(
-        [
-            jnp.sum(grad_a * unit_quarter, 0, keepdims=True),
-            jnp.sum(grad_a, 0, keepdims=True),
-            lax.dynamic_update_slice(blank, bias_sums[0], (0, column)),
-            lax.dynamic_update_slice(blank, bias_sums[2], (0, column)),
-            jnp.zeros((12, D), F32),
-        ],
-        0,
-    )
-    vec_send = jnp.pad(vec_grads.reshape(16, 16, 48).transpose(1, 0, 2), ((0, 0), (0, 0), (0, 80)))
-    grad_normed, sum_qkv, sum_vec = scatter_last(
-        grad_a.astype(BF).reshape(4, OWN, D), grad_qkv.reshape(16, 48, 640), vec_send.reshape(4, 4, 16, 128)
-    )
-    unit, inverse = normalise(tokens.astype(F32))
-    grad_input = (grad_middle + normalise_back(grad_normed, unit, inverse, vecs[0:1])).astype(BF)
-    groups = [unpack_group(sum_qkv[g]) for g in range(4)]
-    grad_rows = jnp.concatenate(
-        [groups[g][k] for k in range(3) for g in range(4)] + [sum_out, sum_first], 1
-    )
+    own_grads = lax.dynamic_slice(grad_vecs, (0, shard_index * 48), (12, 48))
     rows_new = adamw(w_rows, moment_rows, second_rows, grad_rows, LR_MATRIX, DECAY)
-    down_new = adamw(w_down, moment_down, second_down, sum_down, LR_MATRIX, DECAY)
-    vec_new = adamw(vectors, moment_vectors, second_vectors, sum_vec[:12, :48], LR_VECTOR, 0.0)
+    down_new = adamw(w_down, moment_down, second_down, grad_down, LR_MATRIX, DECAY)
+    vec_new = adamw(vectors, moment_vectors, second_vectors, own_grads, LR_VECTOR, 0.0)
     return (
         outputs,
         grad_input,

time: 205 us -> 181 us (0.88)
  local copies, waits for them, and re-layouts: 13.5 us -> 5.62 us
  Pallas kernels: 171 us -> 164 us
  matrix products: 6.66 us -> 0 us
    dot_general x3 -> x0, matrix products: 6.66 us -> none  [the longest x1 2.91 us: per_device(): jnp.einsum('tj,dj->td', grad_packed, w_qkv, preferred_element_type=F32)]
    pallas_call x3 -> x1, Pallas kernels: 171 us -> 164 us  [layer(): pl.pallas_call(layer_kernel, out_shape=(jax.ShapeDtypeStruct((OWN, D), BF...]
    slice x14 -> x0, local copies, waits for them, and re-layouts: 5.88 us -> none  [the longest x10 5.12 us: unpack_group(): col = [packed[:, j * HD:(j + 1) * HD] for j in range(10)]]
    reduce_sum x6 -> x0, other arithmetic: 2.29 us -> none  [the longest x1 1.22 us: per_device(): bias_sums = unpack_group(jnp.sum(grad_packed.astype(F32), 0, keepdims=True))]
where the time goes in v4:
time: 181 us
  Pallas kernels  164 us (91%)
  other arithmetic  10.5 us (6%)
  local copies, waits for them, and re-layouts  5.62 us (3%)
    pallas_call x1, Pallas kernels, layer(): pl.pallas_call(layer_kernel, out_shape=(jax.ShapeDtypeStruct((OWN, D), BF...  164 us
    sub x3, other arithmetic, adamw(): weight - rate * (moment_hat / (jnp.sqrt(second_hat) + EPS_ADAM) + decay *...  7.35 us

profile of v4, /device:TPU:1, one launch (start us, length us, event | category | flops | bytes accessed | tf_op | source)
XLA Modules:
  0.0 181.1 jit_solution(13382452137844896429)
XLA Ops:
  0.6 1.3 convert_element_type.21
  2.0 0.0 copy-start.12
  2.0 0.0 copy-start.13
  2.0 0.1 fusion.6
  2.1 0.1 fusion.7
  2.2 0.0 copy-start.9
  2.2 0.1 concatenate.29
  2.3 0.1 concatenate.30
  2.5 0.1 concatenate.31
  2.6 0.1 concatenate.28
  2.7 0.0 copy-start.1
  2.7 0.7 pad_maximum_fusion.w_qkv
  3.5 0.0 copy-done.12
  3.5 0.1 dynamic_slice.6
  3.5 0.0 copy-done.13
  3.5 0.2 reduce-window.8
  3.7 0.1 select_reduce_fusion
  3.8 0.6 pad.17.query_place
  4.4 1.3 broadcast_in_dim.28.key_place
  5.8 0.0 copy-done.9
  5.8 0.4 dynamic_update_slice.3.vec
  6.2 0.0 copy-start.7
  6.2 0.1 scatter.21
  6.3 0.1 scatter.24
  6.4 0.1 scatter.25
  6.5 0.1 scatter.26
  6.6 0.1 scatter.29.lanes
  6.7 0.0 copy-start.8
  6.7 0.8 slice.297.rest
  7.4 0.0 copy-done.1
  7.4 0.7 convert_element_type.23.down
  8.2 0.0 copy-done.7
  8.2 0.0 copy-done.8
  8.2 164.1 %layer.1 = (bf16[128,768]{1,0:T(8,128)(2,1)}, bf16[128,768]{1,0:T(8,128)(2,1)}, f32[48,6144]{1,0:T(8,128)}, f32[192,768]{1,0:T(8,128)}, f32[16,768]{1,0:T(8,128)}) custom-call(bf16[128,768]{1,0:T(8,128)(2,1)} %x.5, bf16[128,768]{1,0:T(8,128)(2,1)} %cot.1, bf16[4,48,640]{2,1,0:T(8,128)(2,1)} %pad_maximum_fusion.w_qkv, bf16[16,768]{1,0:T(8,128)(2,1)} %copy-done.7, ...), custom_call_target="tpu_custom_call" | custom-call | tf_op jit(solution)/shard_map/layer/pallas_call | solution.py:825
  172.3 0.0 copy-done
  172.3 0.0 copy-start.2
  172.3 0.0 copy-start.3
  172.3 0.0 copy-start.4
  172.3 4.5 %multiply_subtract_fusion = (f32[48,6144]{1,0:T(8,128)}, f32[48,6144]{1,0:T(8,128)}, f32[48,6144]{1,0:T(8,128)}) fusion(f32[48,6144]{1,0:T(8,128)S(1)} %copy-done, f32[48,6144]{1,0:T(8,128)} %get-tuple-element.90, f32[48,6144]{1,0:T(8,128)} %param.32, f32[48,6144]{1,0:T(8,128)} %param.33), kind=kLoop, calls=%fused_computation.2 | loop fusion | flops 4423680 | bytes 8257536 | tf_op jit(solution)/shard_map/sub | solution.py:849
  176.8 0.0 copy-done.2
  176.8 0.0 copy-start.10
  176.8 0.0 copy-start.11
  176.8 0.0 copy-start.6
  176.8 0.0 copy-start.5
  176.8 1.5 multiply_subtract_fusion.1
  178.3 1.4 multiply_subtract_fusion.2
  179.7 0.7 copy.35
  180.4 0.7 copy.36
  (19 shorter events, 0.1 us)
Async XLA Ops:
  2.0 1.5 copy-start.12
  2.0 1.6 copy-start.13
  2.2 3.5 %copy-start.9 = (f32[12,48]{1,0:T(8,128)S(1)}, f32[12,48]{1,0:T(8,128)}, u32[]{:S(2)}) copy-start(f32[12,48]{1,0:T(8,128)} %param.31) | copy-start | bytes 6916
  2.7 4.7 %copy-start.1 = (f32[192,768]{1,0:T(8,128)S(1)}, f32[192,768]{1,0:T(8,128)}, u32[]{:S(2)}) copy-start(f32[192,768]{1,0:T(8,128)} %param.30) | copy-start | bytes 1769476
  6.2 2.0 %copy-start.7 = (bf16[16,768]{1,0:T(8,128)(2,1)}, bf16[16,768]{1,0:T(8,128)(2,1)S(1)}, u32[]{:S(2)}) copy-start(bf16[16,768]{1,0:T(8,128)(2,1)S(1)} %dynamic_update_slice.3.vec) | copy-start | bytes 73732
  6.7 1.5 copy-start.8
  8.2 164.1 %copy-start = (f32[48,6144]{1,0:T(8,128)S(1)}, f32[48,6144]{1,0:T(8,128)}, u32[]{:S(2)}) copy-start(f32[48,6144]{1,0:T(8,128)} %param.29) | copy-start | bytes 3538948
  172.3 4.5 %copy-start.2 = (f32[192,768]{1,0:T(8,128)S(1)}, f32[192,768]{1,0:T(8,128)}, u32[]{:S(2)}) copy-start(f32[192,768]{1,0:T(8,128)} %param.34) | copy-start | bytes 1769476
  172.3 4.5 %copy-start.3 = (f32[192,768]{1,0:T(8,128)S(1)}, f32[192,768]{1,0:T(8,128)}, u32[]{:S(2)}) copy-start(f32[192,768]{1,0:T(8,128)} %param.35) | copy-start | bytes 1769476
  172.3 4.5 %copy-start.4 = (f32[192,768]{1,0:T(8,128)S(1)}, f32[192,768]{1,0:T(8,128)}, u32[]{:S(2)}) copy-start(f32[192,768]{1,0:T(8,128)} %get-tuple-element.91) | copy-start | bytes 1769476
  176.8 1.5 copy-start.10
  176.8 1.5 copy-start.11
  176.8 2.9 %copy-start.6 = (bf16[128,768]{1,0:T(8,128)(2,1)S(1)}, bf16[128,768]{1,0:T(8,128)(2,1)}, u32[]{:S(2)}) copy-start(bf16[128,768]{1,0:T(8,128)(2,1)} %get-tuple-element.143) | copy-start | bytes 589828
  176.8 3.6 %copy-start.5 = (bf16[128,768]{1,0:T(8,128)(2,1)S(1)}, bf16[128,768]{1,0:T(8,128)(2,1)}, u32[]{:S(2)}) copy-start(bf16[128,768]{1,0:T(8,128)(2,1)} %get-tuple-element.144) | copy-start | bytes 589828

commit v5 on v4

--- a/solution.py
+++ b/solution.py
@@ -282,6 +282,155 @@
 
 
 SCATTER_SENDS = 14
+
+
+class GatherWide(Gather):
+    def __init__(self, wire, place, shard, full, rows, cols):
+        piece = (pl.ds(pl.multiple_of(place.x * rows, 16), rows), cols)
+        super().__init__(wire, place, shard, full, piece, True)
+        self.rows, self.cols = rows, cols
+        self.along_x = {}
+
+    def hand_on(self, d):
+        slab = self.slab(d)
+        self.along_x[d] = [self.push(slab, slab, self.place.xdev(e)) for e in (1, 3, 2)]
+
+    def second(self):
+        self.own.wait()
+        for copy in self.one:
+            copy.wait_recv()
+        slab = self.slab(0)
+        self.two = [self.push(slab, slab, self.far(d)) for d in (1, 3)]
+        self.hand_on(0)
+
+    def third(self):
+        self.two[0].wait_recv()
+        half = self.slab(1, pl.ds(0, 2))
+        self.three = [self.push(half, half, self.far(1))]
+        self.two[1].wait_recv()
+        half = self.slab(3, pl.ds(2, 2))
+        self.three.append(self.push(half, half, self.far(3)))
+        self.hand_on(1)
+        self.hand_on(3)
+
+    def fourth(self):
+        for copy in self.three:
+            copy.wait_recv()
+        self.hand_on(2)
+
+    def fifth(self, order):
+        self.across = []
+        for d in order:
+            for copy in self.along_x[d]:
+                copy.wait_recv()
+            slab = self.full.at[step4(self.place.z, 4 - d), :, :, self.cols]
+            self.across.append(self.push(slab, slab, self.place.sibling()))
+
+
+GATHER_WIDE_SENDS = 3 + 2 + 2 + 12 + 4
+
+
+def scatter_wide_shapes(rows, cols, dtype):
+    return [
+        pltpu.VMEM((4, 4, 4 * rows, cols), dtype),
+        pltpu.VMEM((3, 4, 4, rows, cols), dtype),
+        pltpu.VMEM((3, 4, rows, cols), dtype),
+        pltpu.VMEM((4, rows, cols), dtype),
+        pltpu.VMEM((3, rows, cols), dtype),
+    ]
+
+
+class ScatterWide:
+    def __init__(self, wire, place, grad, out, rows, mine, other, scratch):
+        self.wire, self.place, self.grad, self.out, self.rows = wire, place, grad, out, rows
+        self.mine, self.other = mine, other
+        self.in0, self.in_x, self.in1, self.part, self.in2 = scratch
+        self.sends, self.wait = [], []
+        self.piece = self.quarter(place.x)
+
+    def quarter(self, x):
+        return (pl.ds(pl.multiple_of(x * self.rows, 16), self.rows), self.mine)
+
+    def push(self, src, dst, device):
+        copy = self.wire.push(src, dst, device)
+        self.sends.append(copy)
+        return copy
+
+    def arrive(self):
+        for copy in self.wait:
+            copy.wait_recv()
+        self.wait = []
+
+    def p0_slab(self, i):
+        here = self.grad.at[i, :, :, self.other]
+        self.wait.append(self.push(here, self.in0.at[i], self.place.sibling()))
+
+    def p1(self):
+        p = self.place
+        self.arrive()
+
+        def add(i, carry):
+            at = (lax.div(i, 4), lax.rem(i, 4))
+            here = at + (slice(None), self.mine)
+            both = self.grad[here].astype(F32) + self.in0[at].astype(F32)
+            self.grad[here] = both.astype(self.grad.dtype)
+            return carry
+
+        lax.fori_loop(0, 16, add, 0)
+        for d in (1, 3, 2):
+            src = self.grad.at[(slice(None), slice(None)) + self.quarter(step4(p.x, d))]
+            self.wait.append(self.push(src, self.in_x.at[d - 1], p.xdev(d)))
+
+    def p2(self):
+        p = self.place
+        self.arrive()
+
+        def add(i, carry):
+            at = (lax.div(i, 4), lax.rem(i, 4))
+            total = self.grad[at + self.piece].astype(F32)
+            for k in range(3):
+                total = total + self.in_x[(k,) + at].astype(F32)
+            self.grad[at + self.piece] = total.astype(self.grad.dtype)
+            return carry
+
+        lax.fori_loop(0, 16, add, 0)
+        for d in (1, 3, 2):
+            src = self.grad.at[(step4(p.z, d), slice(None)) + self.piece]
+            self.wait.append(self.push(src, self.in1.at[d - 1], p.zdev(d)))
+
+    def p3(self):
+        p = self.place
+        self.arrive()
+        for i in range(4):
+            total = self.grad[(p.z, i) + self.piece].astype(F32)
+            for k in range(3):
+                total = total + self.in1[k, i].astype(F32)
+            self.part[i] = total.astype(self.part.dtype)
+        for d in (1, 3, 2):
+            self.wait.append(self.push(self.part.at[step4(p.y, d)], self.in2.at[d - 1], p.ydev(d)))
+
+    def p4(self):
+        p = self.place
+        self.arrive()
+        total = self.part[p.y].astype(F32)
+        for k in range(3):
+            total = total + self.in2[k].astype(F32)
+        self.out[self.piece] = total
+        here = self.out.at[self.piece]
+        self.wait = [self.push(here, here, p.xdev(d)) for d in (1, 3, 2)]
+
+    def p5(self):
+        self.arrive()
+        here = self.out.at[:, self.mine]
+        self.wait = [self.push(here, here, self.place.sibling())]
+
+    def end(self):
+        self.arrive()
+        for copy in self.sends:
+            copy.wait_send()
+
+
+SCATTER_WIDE_SENDS = 4 + 3 + 3 + 3 + 3 + 1
 
 
 def all_peers(p):
@@ -495,8 +644,7 @@
     parts = [
         Gather(w, p, rest, full_rest, region(0, None, half, 1024), True),
         Gather(w, p, rest, full_rest, region(0, None, half + 1024, 896), False),
-        Gather(w, p, down, full_down, region(pl.multiple_of(p.c * 96, 16), 48, 0, None), True),
-        Gather(w, p, down, full_down, region(pl.multiple_of(p.c * 96 + 48, 16), 48, 0, None), False),
+        GatherWide(w, p, down, full_down, 48, pl.ds(pl.multiple_of(p.c * 384, 128), 384)),
     ]
     for part_ in parts:
         part_.first()
@@ -516,6 +664,8 @@
     for k in range(4):
         unit, _ = normalise(x_all[k].astype(F32))
         normed[k] = (unit * vecs[0:1, :] + vecs[1:2, :]).astype(BF)
+    for part_ in parts:
+        part_.second()
     for copy in w_two:
         copy.wait_recv()
     for k in range(4):
@@ -523,8 +673,7 @@
         kv[p.v, k * OWN : k * OWN + OWN, :] = (projected.astype(BF).astype(F32) * scale).astype(BF)
     mine = kv.at[p.v, :, pl.ds(0, 384)]
     to_v = [w.push(mine, mine, p.vdev(d)) for d in (1, 3, 2)]
-    for part_ in parts:
-        part_.second()
+    parts[2].third()
     for copy in to_v:
         copy.wait_recv()
     head_out[192:256, :] = jnp.zeros((64, 512), F32)
@@ -532,17 +681,17 @@
         turn_keys(kv, head, turned)
         for tile in range(2):
             attend(kv, p, head, tile, bias, probs, turned, head_out, lse)
-        if head == 1:
+        if head == 0:
             for part_ in parts[:2]:
                 part_.third()
+            parts[2].fourth()
     for k in range(4):
         out_send[k] = head_out[:, k * OWN : k * OWN + OWN].T.astype(BF)
     attended[p.u] = out_send[p.u]
     out_back = [w.push(out_send.at[step4(p.u, d)], attended.at[p.u], p.udev(d)) for d in (1, 3, 2)]
-    for part_ in parts[2:]:
-        part_.third()
-    for part_ in parts:
+    for part_ in parts[:2]:
         part_.fourth()
+    parts[2].fifth((0, 1, 3, 2))
     for copy in out_back:
         copy.wait_recv()
     for part_ in parts:
@@ -571,19 +720,15 @@
     firsts = [first_part(i) for i in range(4)]
     at, to = p.c * 384, (1 - p.c) * 384
     downs = [
-        Scatter(
-            w, p, g_down, o_down, region(0, 96, at, 384), region(0, 96, to, 384),
-            region(0, 96, at, 384), True, blocks[20:25],
-        ),
-        Scatter(
-            w, p, g_down, o_down, region(96, 96, at, 384), region(96, 96, to, 384),
-            region(96, 96, at, 384), False, blocks[25:30],
-        ),
+        ScatterWide(
+            w, p, g_down, o_down, 48, pl.ds(pl.multiple_of(at, 128), 384),
+            pl.ds(pl.multiple_of(to, 128), 384), blocks[20:25],
+        )
     ]
     outs = [
         Scatter(
             w, p, g_out, o_rows, region(0, None, at, 384), region(0, None, to, 384),
-            region(0, None, at + 3 * D, 384), False, blocks[30:35],
+            region(0, None, at + 3 * D, 384), False, blocks[25:30],
         )
     ]
     for i in range(4):
@@ -642,9 +787,9 @@
         lambda: [part_.p1() for part_ in firsts[2:3]],
         lambda: [part_.p1() for part_ in firsts[3:]],
         lambda: [part_.p1() for part_ in downs],
+        lambda: [part_.p1() for part_ in outs],
         lambda: [part_.p2() for part_ in firsts[:2]],
-        lambda: [part_.p1() for part_ in outs],
-        lambda: [part_.p2() for part_ in firsts[2:]] + [part_.p3() for part_ in firsts[:2]],
+        lambda: [part_.p2() for part_ in firsts[2:]],
     ]
     to_v_back = []
     for head in range(3):
@@ -710,9 +855,9 @@
     grad_vecs[3:4, :] = bias_v[0:1, :]
     vec_in[0, p.z] = grad_vecs[...]
     vec_sends = [[w.push(grad_vecs, vec_in.at[0, p.z], p.zdev(d)) for d in (1, 3, 2)]]
-    for part_ in firsts[2:]:
+    for part_ in firsts[:2]:
         part_.p3()
-    for part_ in downs + outs:
+    for part_ in outs:
         part_.p2()
     for copy in one:
         copy.wait_recv()
@@ -727,8 +872,10 @@
         copy.wait_recv()
     vec_in[1, p.y] = ordered_sum(vec_in.at[0])
     vec_sends.append([w.push(vec_in.at[1, p.y], vec_in.at[1, p.y], p.ydev(d)) for d in (1, 3, 2)])
-    for part_ in firsts[:2]:
-        part_.p4()
+    for part_ in firsts[2:]:
+        part_.p3()
+    for part_ in downs:
+        part_.p2()
     for copy in two:
         copy.wait_recv()
     three = [w.push(in2.at[pl.ds((1 - p.c) * 2, 2)], in0, p.sibling())]
@@ -743,7 +890,7 @@
     four = [w.push(held, in3.at[p.x], p.xdev(d)) for d in (1, 3, 2)]
     for part_ in downs + outs:
         part_.p3()
-    for part_ in firsts[2:]:
+    for part_ in firsts[:2]:
         part_.p4()
     for copy in a_one:
         copy.wait_recv()
@@ -765,10 +912,12 @@
         packed_sum[p.c * 2 + k] = total
     here = packed_sum.at[pl.ds(p.c * 2, 2)]
     five = [w.push(here, here, p.sibling())]
-    for part_ in downs + outs:
+    for part_ in downs + firsts[2:] + outs:
         part_.p4()
     vec_sends[3][0].wait_recv()
     o_vec[...] = vec_in[3, 0] + vec_in[3, 1]
+    for part_ in downs:
+        part_.p5()
     five[0].wait_recv()
     groups = [natural_group(packed_sum[g]) for g in range(4)]
     for k in range(3):
@@ -820,8 +969,9 @@
         pltpu.VMEM((4, 2, 48, 640), BF),
         pltpu.VMEM((4, 48, 640), F32),
     ]
-    for rows in (48, 48, 48, 48, 96, 96, 48):
-        shapes += scatter_shapes(rows, 384, BF)
+    for _ in range(4):
+        shapes += scatter_shapes(48, 384, BF)
+    shapes += scatter_wide_shapes(48, 384, BF) + scatter_shapes(48, 384, BF)
     return pl.pallas_call(
         layer_kernel,
         out_shape=(
@@ -833,7 +983,7 @@
         ),
         in_specs=[VMEM] * 7 + [ANY, VMEM],
         out_specs=(VMEM,) * 5,
-        scratch_shapes=shapes + sems(4 * GATHER_SENDS + 7 * SCATTER_SENDS + 80, 5),
+        scratch_shapes=shapes + sems(2 * GATHER_SENDS + GATHER_WIDE_SENDS + 5 * SCATTER_SENDS + SCATTER_WIDE_SENDS + 80, 5),
         compiler_params=pltpu.CompilerParams(
             collective_id=1, has_side_effects=True, vmem_limit_bytes=62 * MIB
         ),

time: 181 us -> 165 us (0.912)
  Pallas kernels: 164 us -> 148 us
    pallas_call x1, Pallas kernels: 164 us -> 148 us  [layer(): pl.pallas_call(layer_kernel, out_shape=(jax.ShapeDtypeStruct((OWN, D), BF...]
where the time goes in v5:
time: 165 us
  Pallas kernels  148 us (90%)
  other arithmetic  10.5 us (6%)
  local copies, waits for them, and re-layouts  5.62 us (3%)
    pallas_call x1, Pallas kernels, layer(): pl.pallas_call(layer_kernel, out_shape=(jax.ShapeDtypeStruct((OWN, D), BF...  148 us
    sub x3, other arithmetic, adamw(): weight - rate * (moment_hat / (jnp.sqrt(second_hat) + EPS_ADAM) + decay *...  7.35 us

profile of v5, /device:TPU:1, one launch (start us, length us, event | category | flops | bytes accessed | tf_op | source)
XLA Modules:
  0.0 164.5 jit_solution(3401006616900922427)
XLA Ops:
  0.6 1.3 convert_element_type.21
  2.0 0.0 copy-start.12
  2.0 0.0 copy-start.13
  2.0 0.1 fusion.6
  2.1 0.1 fusion.7
  2.2 0.0 copy-start.9
  2.2 0.1 concatenate.29
  2.3 0.1 concatenate.30
  2.5 0.1 concatenate.31
  2.6 0.1 concatenate.28
  2.7 0.0 copy-start.1
  2.7 0.7 pad_maximum_fusion.w_qkv
  3.5 0.0 copy-done.12
  3.5 0.1 dynamic_slice.6
  3.5 0.0 copy-done.13
  3.5 0.2 reduce-window.8
  3.7 0.1 select_reduce_fusion
  3.8 0.6 pad.17.query_place
  4.4 1.3 broadcast_in_dim.28.key_place
  5.8 0.0 copy-done.9
  5.8 0.4 dynamic_update_slice.3.vec
  6.2 0.0 copy-start.7
  6.2 0.1 scatter.21
  6.3 0.1 scatter.24
  6.4 0.1 scatter.25
  6.5 0.1 scatter.26
  6.6 0.1 scatter.29.lanes
  6.7 0.0 copy-start.8
  6.7 0.8 slice.297.rest
  7.4 0.0 copy-done.1
  7.4 0.7 convert_element_type.23.down
  8.2 0.0 copy-done.7
  8.2 0.0 copy-done.8
  8.2 147.5 %layer.1 = (bf16[128,768]{1,0:T(8,128)(2,1)}, bf16[128,768]{1,0:T(8,128)(2,1)}, f32[48,6144]{1,0:T(8,128)}, f32[192,768]{1,0:T(8,128)}, f32[16,768]{1,0:T(8,128)}) custom-call(bf16[128,768]{1,0:T(8,128)(2,1)} %x.5, bf16[128,768]{1,0:T(8,128)(2,1)} %cot.1, bf16[4,48,640]{2,1,0:T(8,128)(2,1)} %pad_maximum_fusion.w_qkv, bf16[16,768]{1,0:T(8,128)(2,1)} %copy-done.7, ...), custom_call_target="tpu_custom_call" | custom-call | tf_op jit(solution)/shard_map/layer/pallas_call | solution.py:975
  155.7 0.0 copy-done
  155.7 0.0 copy-start.2
  155.7 0.0 copy-start.3
  155.7 0.0 copy-start.4
  155.7 4.5 %multiply_subtract_fusion = (f32[48,6144]{1,0:T(8,128)}, f32[48,6144]{1,0:T(8,128)}, f32[48,6144]{1,0:T(8,128)}) fusion(f32[48,6144]{1,0:T(8,128)S(1)} %copy-done, f32[48,6144]{1,0:T(8,128)} %get-tuple-element.90, f32[48,6144]{1,0:T(8,128)} %param.32, f32[48,6144]{1,0:T(8,128)} %param.33), kind=kLoop, calls=%fused_computation.2 | loop fusion | flops 4423680 | bytes 8257536 | tf_op jit(solution)/shard_map/sub | solution.py:999
  160.2 0.0 copy-start.10
  160.2 0.0 copy-start.11
  160.2 0.0 copy-start.6
  160.2 0.0 copy-start.5
  160.3 1.5 multiply_subtract_fusion.1
  161.7 0.0 copy-done.11
  161.7 1.4 multiply_subtract_fusion.2
  163.2 0.7 copy.35
  163.8 0.7 copy.36
  (19 shorter events, 0.1 us)
Async XLA Ops:
  2.0 1.5 copy-start.12
  2.0 1.6 copy-start.13
  2.2 3.5 %copy-start.9 = (f32[12,48]{1,0:T(8,128)S(1)}, f32[12,48]{1,0:T(8,128)}, u32[]{:S(2)}) copy-start(f32[12,48]{1,0:T(8,128)} %param.31) | copy-start | bytes 6916
  2.7 4.7 %copy-start.1 = (f32[192,768]{1,0:T(8,128)S(1)}, f32[192,768]{1,0:T(8,128)}, u32[]{:S(2)}) copy-start(f32[192,768]{1,0:T(8,128)} %param.30) | copy-start | bytes 1769476
  6.2 2.0 %copy-start.7 = (bf16[16,768]{1,0:T(8,128)(2,1)}, bf16[16,768]{1,0:T(8,128)(2,1)S(1)}, u32[]{:S(2)}) copy-start(bf16[16,768]{1,0:T(8,128)(2,1)S(1)} %dynamic_update_slice.3.vec) | copy-start | bytes 73732
  6.7 1.5 copy-start.8
  8.2 147.5 %copy-start = (f32[48,6144]{1,0:T(8,128)S(1)}, f32[48,6144]{1,0:T(8,128)}, u32[]{:S(2)}) copy-start(f32[48,6144]{1,0:T(8,128)} %param.29) | copy-start | bytes 3538948
  155.7 4.5 %copy-start.2 = (f32[192,768]{1,0:T(8,128)S(1)}, f32[192,768]{1,0:T(8,128)}, u32[]{:S(2)}) copy-start(f32[192,768]{1,0:T(8,128)} %param.34) | copy-start | bytes 1769476
  155.7 4.5 %copy-start.3 = (f32[192,768]{1,0:T(8,128)S(1)}, f32[192,768]{1,0:T(8,128)}, u32[]{:S(2)}) copy-start(f32[192,768]{1,0:T(8,128)} %param.35) | copy-start | bytes 1769476
  155.7 4.5 %copy-start.4 = (f32[192,768]{1,0:T(8,128)S(1)}, f32[192,768]{1,0:T(8,128)}, u32[]{:S(2)}) copy-start(f32[192,768]{1,0:T(8,128)} %get-tuple-element.91) | copy-start | bytes 1769476
  160.2 1.5 copy-start.10
  160.2 1.5 copy-start.11
  160.2 2.9 %copy-start.6 = (bf16[128,768]{1,0:T(8,128)(2,1)S(1)}, bf16[128,768]{1,0:T(8,128)(2,1)}, u32[]{:S(2)}) copy-start(bf16[128,768]{1,0:T(8,128)(2,1)} %get-tuple-element.143) | copy-start | bytes 589828
  160.2 3.6 %copy-start.5 = (bf16[128,768]{1,0:T(8,128)(2,1)S(1)}, bf16[128,768]{1,0:T(8,128)(2,1)}, u32[]{:S(2)}) copy-start(bf16[128,768]{1,0:T(8,128)(2,1)} %get-tuple-element.144) | copy-start | bytes 589828
